TPU v7x, 32 devices: a whole 2x2x4 slice. The times are simulated.
32 devices in a mesh: ctx: 8 (over y, x, core), fsdp: 4 (over z).
Axes of the slice: x: 2, y: 2, z: 4, core: 2. Of those that a mesh axis runs over, the one named last changes fastest.
Arguments:
- tokens: bfloat16 [4, 4096, 512], P('fsdp', 'ctx'), may hold values from -6 to 6
- cotangent: bfloat16 [4, 4096, 512], P('fsdp', 'ctx'), may hold values from -6 to 6
- block_table: int32 [16], replicated, may hold values from 0 to 15, as said below
- seg_ids: int32 [4, 4096], P('fsdp'), may hold values from 0 to 2, as said below
- group_ids: int32 [4, 4096], P('fsdp', 'ctx'), may hold values from 0 to 127, as said below
- w_qkv: bfloat16 [512, 1536], P('fsdp'), may hold values from -0.375 to 0.375
- w_out: bfloat16 [512, 512], P('fsdp'), may hold values from -1.5 to 1.5
- w_router: bfloat16 [512, 8], P('fsdp'), may hold values from -0.1875 to 0.1875
- ln_gain: bfloat16 [512], P('fsdp'), may hold values from 0.5 to 1.5
- ln_bias: bfloat16 [512], P('fsdp'), may hold values from -1 to 1
- w_up: bfloat16 [8, 512, 2048], P('fsdp'), may hold values from -2 to 2
- w_down: bfloat16 [8, 2048, 512], P('fsdp'), may hold values from -1.5 to 1.5
Outputs:
- layer_out: float32 [4, 4096, 512], P('fsdp', 'ctx')
- grad_tokens: float32 [4, 4096, 512], P('fsdp', 'ctx')
- grad_qkv: float32 [512, 1536], P('fsdp')
- grad_out: float32 [512, 512], P('fsdp')
- grad_router: float32 [512, 8], P('fsdp')
- grad_gain: float32 [512], P('fsdp')
- grad_bias: float32 [512], P('fsdp')
- grad_up: float32 [8, 512, 2048], P('fsdp')
- grad_down: float32 [8, 2048, 512], P('fsdp')
Inputs may be any that keep to these rules, and one draw needn't show every extreme that they name: `block_table`: a permutation; each index c of ctx holds stored blocks 2c and 2c + 1, which are sequence blocks j and 15 - j for some j. `seg_ids`: in sequence order each batch is the prompt (segment 0) followed by continuations 1 to 2, each a nonempty run of positions. `group_ids`: every group has exactly 32 tokens; the tokens of ctx index c have groups c * 16 to (c + 1) * 16 - 1.
All inputs are finite; a program needn't handle non-finite values.
Results may differ from a plain program's by a relative error of at most 0.019.
Values may be sent and summed in bfloat16 or wider, within the bound.
A program may use at most 256 MiB of HBM per device.

v0:
```python
import jax
import jax.numpy as jnp
from jax import lax
from jax.sharding import PartitionSpec as P

HEADS = 8
HEAD = 64
GROUP_SIZE = 32
KEY_BLOCK = 2048


highest = lax.Precision.HIGHEST
neg_large = -1e30
epsilon = 1e-05
gelu_coef = 0.7978845608028654
gelu_cubic = 0.044715


def contract_rows(left, right):
    return lax.dot_general(
        left, right, (((0,), (0,)), ((), ())), preferred_element_type=jnp.float32
    )


def contract_cols(left, right):
    return lax.dot_general(
        left, right, (((1,), (1,)), ((), ())), preferred_element_type=jnp.float32
    )


def gelu_slope(value):
    inner = gelu_coef * (value + gelu_cubic * value * value * value)
    tangent = jnp.tanh(inner)
    return 0.5 * (1.0 + tangent) + 0.5 * value * (1.0 - tangent * tangent) * gelu_coef * (
        1.0 + 3.0 * gelu_cubic * value * value
    )


def expert_forward(mixed_low, up_weight, down_weight):
    pre = jnp.einsum("ged,edh->geh", mixed_low, up_weight, preferred_element_type=jnp.float32)
    active = jax.nn.gelu(pre, approximate=True).astype(jnp.bfloat16)
    result = jnp.einsum("geh,ehd->ged", active, down_weight, preferred_element_type=jnp.float32)
    return (pre, active, result.astype(jnp.bfloat16))


def expert_backward(mixed_low, pre, active, grad_result, up_weight, down_weight):
    grad_act = jnp.einsum(
        "ged,ehd->geh", grad_result, down_weight, preferred_element_type=jnp.float32
    )
    grad_pre = (grad_act * gelu_slope(pre)).astype(jnp.bfloat16)
    grad_down_part = jnp.einsum(
        "geh,ged->ehd", active, grad_result, preferred_element_type=jnp.float32
    )
    grad_up_part = jnp.einsum(
        "ged,geh->edh", mixed_low, grad_pre, preferred_element_type=jnp.float32
    )
    grad_mixed = jnp.einsum("geh,edh->ged", grad_pre, up_weight, preferred_element_type=jnp.float32)
    return (grad_up_part, grad_down_part, grad_mixed.astype(jnp.bfloat16))


def on_device(
    tokens,
    cotangent,
    block_table,
    seg_ids,
    group_ids,
    w_qkv,
    w_out,
    w_router,
    ln_gain,
    ln_bias,
    w_up,
    w_down,
):
    tok_rows = tokens[0]
    tok_count = tok_rows.shape[0]
    width = tok_rows.shape[1]
    expert_count = w_router.shape[1]
    ctx_index = lax.axis_index("ctx")
    full_rows = seg_ids.shape[1]
    block_len = full_rows // block_table.shape[0]
    row_ids = jnp.arange(full_rows, dtype=jnp.int32)
    key_pos = jnp.take(block_table, row_ids // block_len) * block_len + row_ids % block_len
    key_seg = seg_ids[0]
    pos_rows = lax.dynamic_slice_in_dim(key_pos, ctx_index * tok_count, tok_count)
    seg_rows = lax.dynamic_slice_in_dim(key_seg, ctx_index * tok_count, tok_count)
    scale = HEAD ** (-0.5)
    qkv_full, out_full, router_full, gain_full, bias_full = (
        lax.all_gather(w_qkv, "fsdp", axis=0, tiled=True),
        lax.all_gather(w_out, "fsdp", axis=0, tiled=True),
        lax.all_gather(w_router, "fsdp", axis=0, tiled=True),
        lax.all_gather(ln_gain, "fsdp", axis=0, tiled=True),
        lax.all_gather(ln_bias, "fsdp", axis=0, tiled=True),
    )
    qkv = jnp.dot(tok_rows, qkv_full, preferred_element_type=jnp.float32).astype(jnp.bfloat16)
    query_heads = qkv[:, :width].reshape(tok_count, HEADS, HEAD)
    key_all, val_all = (
        lax.all_gather(qkv[:, width : 2 * width], "ctx", axis=0, tiled=True),
        lax.all_gather(qkv[:, 2 * width :], "ctx", axis=0, tiled=True),
    )
    key_heads = key_all.reshape(full_rows, HEADS, HEAD)
    val_heads = val_all.reshape(full_rows, HEADS, HEAD)
    block_count = full_rows // KEY_BLOCK
    block_ids = jnp.arange(block_count, dtype=jnp.int32)

    def block_scores(index):
        start = index * KEY_BLOCK
        key_block = lax.dynamic_slice_in_dim(key_heads, start, KEY_BLOCK, 0)
        val_block = lax.dynamic_slice_in_dim(val_heads, start, KEY_BLOCK, 0)
        pos_block = lax.dynamic_slice_in_dim(key_pos, start, KEY_BLOCK, 0)
        seg_block = lax.dynamic_slice_in_dim(key_seg, start, KEY_BLOCK, 0)
        scores = (
            jnp.einsum("qhd,khd->hqk", query_heads, key_block, preferred_element_type=jnp.float32)
            * scale
        )
        allowed = (pos_block[None, :] <= pos_rows[:, None]) & (
            (seg_block[None, :] == 0) | (seg_block[None, :] == seg_rows[:, None])
        )
        return (scores, allowed[None], key_block, val_block)

    def lse_step(carry, index):
        top, total = carry
        scores, allowed, key_block, val_block = block_scores(index)
        masked = jnp.where(allowed, scores, neg_large)
        new_top = jnp.maximum(top, jnp.max(masked, axis=-1))
        weights = jnp.where(allowed, jnp.exp(masked - new_top[..., None]), 0.0)
        return ((new_top, total * jnp.exp(top - new_top) + jnp.sum(weights, axis=-1)), None)

    start_top = jnp.full((HEADS, tok_count), neg_large, jnp.float32)
    (top, total), unused = lax.scan(
        lse_step, (start_top, jnp.zeros((HEADS, tok_count), jnp.float32)), block_ids
    )
    log_total = top + jnp.log(total)

    def block_probs(index):
        scores, allowed, key_block, val_block = block_scores(index)
        probs = jnp.where(allowed, jnp.exp(scores - log_total[..., None]), 0.0)
        return (probs, key_block, val_block)

    def value_step(accum, index):
        probs, key_block, val_block = block_probs(index)
        return (
            accum
            + jnp.einsum(
                "hqk,khd->qhd",
                probs.astype(jnp.bfloat16),
                val_block,
                preferred_element_type=jnp.float32,
            ),
            None,
        )

    accum, unused = lax.scan(
        value_step, jnp.zeros((tok_count, HEADS, HEAD), jnp.float32), block_ids
    )
    attended = accum.reshape(tok_count, width).astype(jnp.bfloat16)
    hidden = tok_rows.astype(jnp.float32) + jnp.dot(
        attended, out_full, preferred_element_type=jnp.float32
    )
    center = hidden - jnp.mean(hidden, axis=-1, keepdims=True)
    inv_dev = lax.rsqrt(jnp.mean(center * center, axis=-1, keepdims=True) + epsilon)
    unit = center * inv_dev
    gain_f = gain_full.astype(jnp.float32)
    normed_low = (unit * gain_f + bias_full.astype(jnp.float32)).astype(jnp.bfloat16)
    logits = jnp.dot(normed_low, router_full, preferred_element_type=jnp.float32)
    groups_dev = tok_count // GROUP_SIZE
    local_group = group_ids[0] - ctx_index * groups_dev
    member = (local_group[:, None] == jnp.arange(groups_dev, dtype=jnp.int32)[None, :]).astype(
        jnp.float32
    )
    expo = jnp.exp(logits)
    group_total = jnp.dot(member.T, expo, precision=highest)
    mix_weights = expo / jnp.dot(member, group_total, precision=highest)
    weights_low = mix_weights.astype(jnp.bfloat16)
    mixing = member.astype(jnp.bfloat16).T[:, None, :] * weights_low.T[None, :, :]
    mixing_flat = mixing.reshape(groups_dev * expert_count, tok_count)
    mixed_low = jnp.dot(mixing_flat, normed_low, preferred_element_type=jnp.float32).astype(
        jnp.bfloat16
    )
    mixed_low = mixed_low.reshape(groups_dev, expert_count, width)
    owner_mixed = lax.all_to_all(mixed_low, "fsdp", split_axis=1, concat_axis=0, tiled=True)
    pre, active, owner_out = expert_forward(owner_mixed, w_up, w_down)
    expert_out = lax.all_to_all(owner_out, "fsdp", split_axis=0, concat_axis=1, tiled=True)
    expert_flat = expert_out.reshape(groups_dev * expert_count, width)
    spread = contract_rows(mixing_flat, expert_flat)
    layer_out = hidden + spread
    cot_rows = cotangent[0]
    cot_f = cot_rows.astype(jnp.float32)
    grad_expert = jnp.dot(mixing_flat, cot_rows, preferred_element_type=jnp.float32).astype(
        jnp.bfloat16
    )
    grad_expert = grad_expert.reshape(groups_dev, expert_count, width)
    coef = contract_cols(cot_rows, expert_flat).reshape(tok_count, groups_dev, expert_count)
    grad_mix_spread = jnp.sum(coef * member[:, :, None], axis=1)
    owner_grad = lax.all_to_all(grad_expert, "fsdp", split_axis=1, concat_axis=0, tiled=True)
    grad_up_own, grad_down_own, owner_back = expert_backward(
        owner_mixed, pre, active, owner_grad, w_up, w_down
    )
    grad_mixed = lax.all_to_all(owner_back, "fsdp", split_axis=0, concat_axis=1, tiled=True)
    grad_mixed_flat = grad_mixed.reshape(groups_dev * expert_count, width)
    grad_norm_mix = contract_rows(mixing_flat, grad_mixed_flat)
    grad_mixing = contract_cols(grad_mixed_flat, normed_low).reshape(
        groups_dev, expert_count, tok_count
    )
    grad_mix_mixing = jnp.sum(grad_mixing * member.T[:, None, :], axis=0).T
    grad_mix = grad_mix_spread + grad_mix_mixing
    product = mix_weights * grad_mix
    token_dot = jnp.dot(member, jnp.dot(member.T, product, precision=highest), precision=highest)
    grad_logits = (product - mix_weights * token_dot).astype(jnp.bfloat16)
    grad_router_part = contract_rows(normed_low, grad_logits)
    grad_norm_router = contract_cols(grad_logits, router_full)
    grad_normed = grad_norm_mix + grad_norm_router
    grad_gain_part = jnp.sum(grad_normed * unit, axis=0)
    grad_bias_part = jnp.sum(grad_normed, axis=0)
    scaled = grad_normed * gain_f
    grad_hidden = cot_f + inv_dev * (
        scaled
        - jnp.mean(scaled, axis=-1, keepdims=True)
        - unit * jnp.mean(scaled * unit, axis=-1, keepdims=True)
    )
    grad_branch = grad_hidden.astype(jnp.bfloat16)
    grad_out_part = contract_rows(attended, grad_branch)
    grad_heads = (
        contract_cols(grad_branch, out_full).astype(jnp.bfloat16).reshape(tok_count, HEADS, HEAD)
    )
    delta = jnp.sum(grad_heads.astype(jnp.float32) * accum, axis=-1).T

    def grad_step(grad_query, index):
        probs, key_block, val_block = block_probs(index)
        grad_probs = jnp.einsum(
            "qhd,khd->hqk", grad_heads, val_block, preferred_element_type=jnp.float32
        )
        grad_scores = (probs * (grad_probs - delta[..., None])).astype(jnp.bfloat16)
        grad_query = (
            grad_query
            + jnp.einsum("hqk,khd->qhd", grad_scores, key_block, preferred_element_type=jnp.float32)
            * scale
        )
        grad_key = (
            jnp.einsum("hqk,qhd->khd", grad_scores, query_heads, preferred_element_type=jnp.float32)
            * scale
        )
        grad_val = jnp.einsum(
            "hqk,qhd->khd",
            probs.astype(jnp.bfloat16),
            grad_heads,
            preferred_element_type=jnp.float32,
        )
        return (grad_query, (grad_key, grad_val))

    grad_query, (grad_keys, grad_vals) = lax.scan(
        grad_step, jnp.zeros((tok_count, HEADS, HEAD), jnp.float32), block_ids
    )
    grad_key_own, grad_val_own = (
        lax.psum_scatter(
            grad_keys.reshape(full_rows, width), "ctx", scatter_dimension=0, tiled=True
        ),
        lax.psum_scatter(
            grad_vals.reshape(full_rows, width), "ctx", scatter_dimension=0, tiled=True
        ),
    )
    grad_qkv_low = jnp.concatenate(
        [grad_query.reshape(tok_count, width), grad_key_own, grad_val_own], axis=1
    ).astype(jnp.bfloat16)
    grad_qkv_part = contract_rows(tok_rows, grad_qkv_low)
    grad_tokens = grad_hidden + contract_cols(grad_qkv_low, qkv_full)
    dense = (
        lax.psum_scatter(grad_qkv_part, "fsdp", scatter_dimension=0, tiled=True),
        lax.psum_scatter(grad_out_part, "fsdp", scatter_dimension=0, tiled=True),
        lax.psum_scatter(grad_router_part, "fsdp", scatter_dimension=0, tiled=True),
        lax.psum_scatter(grad_gain_part, "fsdp", scatter_dimension=0, tiled=True),
        lax.psum_scatter(grad_bias_part, "fsdp", scatter_dimension=0, tiled=True),
    )
    totals = lax.psum(
        (dense[0], dense[1], dense[2], dense[3], dense[4], grad_up_own, grad_down_own), "ctx"
    )
    return (
        layer_out[None],
        grad_tokens[None],
        totals[0],
        totals[1],
        totals[2],
        totals[3],
        totals[4],
        totals[5],
        totals[6],
    )


def solution(mesh):
    placed = (
        P("fsdp", "ctx", None),
        P("fsdp", "ctx", None),
        P(),
        P("fsdp", None),
        P("fsdp", "ctx"),
        P("fsdp", None),
        P("fsdp", None),
        P("fsdp", None),
        P("fsdp"),
        P("fsdp"),
        P("fsdp", None, None),
        P("fsdp", None, None),
    )
    return jax.shard_map(
        on_device,
        mesh=mesh,
        in_specs=placed,
        out_specs=(
            P("fsdp", "ctx", None),
            P("fsdp", "ctx", None),
            P("fsdp", None),
            P("fsdp", None),
            P("fsdp", None),
            P("fsdp"),
            P("fsdp"),
            P("fsdp", None, None),
            P("fsdp", None, None),
        ),
        check_vma=False,
    )
```

profile of v0, /device:TPU:0, one launch (start us, length us, event | category | flops | bytes accessed | tf_op | source)
XLA Modules:
  0.0 1294.8 jit_solution(16020932533069069465)
XLA Ops:
  8.0 41.4 %all-gather.6.cloned.1.call-done = bf16[512,1536]{1,0:T(8,128)(2,1)} async-done(((bf16[128,1536]{1,0:T(8,128)(2,1)}), bf16[512,1536]{1,0:T(8,128)(2,1)}) %all-gather.6.cloned.1.call-update) | async-done | bytes 1572880 | tf_op jit(solution)/shard_map/all_gather | solution.py:89
  54.2 8.8 all-gather.1
  63.5 8.2 all-gather
  78.0 5.6 fusion.112
  83.7 12.2 all_gather.27
  96.0 16.1 %all_gather.24 = bf16[512,512]{1,0:T(8,128)(2,1)} all-gather(bf16[128,512]{1,0:T(8,128)(2,1)S(1)} %copy-done.44), channel_id=1, replica_groups=mesh['ctx'=8,'fsdp'=4] {'fsdp'}, dimensions={0}, use_global_device_ids=true | all-gather | bytes 655360 | tf_op jit(solution)/shard_map/all_gather | solution.py:90
  113.0 6.4 copy.73
  119.4 67.5 %while.39 = (s32[]{:T(128)}, f32[8,512]{1,0:T(8,128)S(1)}, f32[8,512]{1,0:T(8,128)S(1)}, s32[2]{0:T(128)S(1)}, s32[4096]{0:T(1024)S(1)}, /*index=5*/s32[512]{0:T...) while((s32[]{:T(128)}, f32[8,512]{1,0:T(8,128)S(1)}, ...), condition=%wide.region_3.4_spmd.clone, body=%wide.region_0.0_spmd.clone.sunk | while | flops 1145067520 | bytes 73146584 | solution.py:130
  122.5 15.9 %fusion.195 = (f32[8,512]{1,0:T(8,128)S(1)}, f32[8,2048,512]{2,1,0:T(8,128)}) fusion(pred[512,2048]{0,1:T(8,128)(4,1)S(1)} %or_and_fusion.6, bf16[512,8,64]{0,2,1:T(8,128)(2,1)S(1)} %get-tuple-element.788, bf16[4096,8,64]{0,2,1:T(8,128)(2,1)} %get-tuple-element.787, s32[]{:T(128)S(6)} %select_n.201), kind=kOutput, calls=%fused_computation.2.clone.1 | convolution fusion | flops 1098903552 | bytes 37240836 | tf_op jit(solution)/shard_map/while/body/eval_jaxpr/qhd,khd->hqk/dot_general | solution.py:113
  138.4 15.1 %select_reduce_fusion.2 = f32[8,512]{1,0:T(8,128)S(1)} fusion(f32[8,2048,512]{2,1,0:T(8,128)} %get-tuple-element.720, f32[8,512]{1,0:T(8,128)S(1)} %select_maximum_fusion.2, pred[512,2048]{0,1:T(8,128)(4,1)S(1)} %or_and_fusion.6), kind=kLoop, calls=%fused_computation.1.clone.1 | loop fusion | flops 41938944 | bytes 34635776 | tf_op jit(solution)/shard_map/while/body/eval_jaxpr/reduce_sum | solution.py:127
  156.6 15.4 %fusion.195 = (f32[8,512]{1,0:T(8,128)S(1)}, f32[8,2048,512]{2,1,0:T(8,128)}) fusion(pred[512,2048]{0,1:T(8,128)(4,1)S(1)} %or_and_fusion.6, bf16[512,8,64]{0,2,1:T(8,128)(2,1)S(1)} %get-tuple-element.788, bf16[4096,8,64]{0,2,1:T(8,128)(2,1)} %get-tuple-element.787, s32[]{:T(128)S(6)} %select_n.201), kind=kOutput, calls=%fused_computation.2.clone.1 | convolution fusion | flops 1098903552 | bytes 37240836 | tf_op jit(solution)/shard_map/while/body/eval_jaxpr/qhd,khd->hqk/dot_general | solution.py:113
  172.0 14.9 %select_reduce_fusion.2 = f32[8,512]{1,0:T(8,128)S(1)} fusion(f32[8,2048,512]{2,1,0:T(8,128)} %get-tuple-element.720, f32[8,512]{1,0:T(8,128)S(1)} %select_maximum_fusion.2, pred[512,2048]{0,1:T(8,128)(4,1)S(1)} %or_and_fusion.6), kind=kLoop, calls=%fused_computation.1.clone.1 | loop fusion | flops 41938944 | bytes 34635776 | tf_op jit(solution)/shard_map/while/body/eval_jaxpr/reduce_sum | solution.py:127
  186.9 6.5 copy.72
  193.4 28.5 %while.40 = (s32[]{:T(128)}, f32[512,8,64]{0,2,1:T(8,128)S(1)}, s32[2]{0:T(128)S(1)}, bf16[4096,8,64]{0,2,1:T(8,128)(2,1)}, s32[4096]{0:T(1024)S(1)}, /*index=5*...) while((s32[]{:T(128)}, f32[512,8,64]{0,2,1:T(8,128)S(1)}, ...), condition=%wide.region_5.6_spmd.clone, body=%wide.region_4.5_spmd.clone.sunk | while | flops 2185758720 | bytes 8988384 | solution.py:153
  196.5 11.1 fusion.200
  210.8 11.1 fusion.200
  232.6 5.1 all-to-all-done
  242.7 4.9 all-to-all-done.2
  284.1 480.9 %while.41 = (s32[]{:T(128)}, f32[512,8,64]{0,2,1:T(8,128)}, f32[2,2048,8,64]{1,0,3,2:T(2,128)}, f32[2,2048,8,64]{1,0,3,2:T(2,128)}, s32[2]{0:T(128)S(1)}, /*inde...) while((s32[]{:T(128)}, f32[512,8,64]{0,2,1:T(8,128)}, ...), condition=%wide.region_14.15_spmd.clone, body=%wide.region_13.14_spmd.clone.sunk | while | flops 5458626560 | bytes 299410016 | solution.py:251
  300.6 15.1 %fusion.211 = f32[8,2048,512]{2,1,0:T(8,128)} fusion(bf16[512,8,64]{0,2,1:T(8,128)(2,1)S(1)} %get-tuple-element.886, bf16[4096,8,64]{0,2,1:T(8,128)(2,1)} %get-tuple-element.881, s32[]{:T(128)S(6)} %select_n.206), kind=kOutput, calls=%fused_computation.35.clone.1 | convolution fusion | flops 1073741824 | bytes 36175876 | tf_op jit(solution)/shard_map/while/body/eval_jaxpr/qhd,khd->hqk/dot_general | solution.py:113
  317.5 20.8 %fusion.212 = bf16[8,512,2048]{1,2,0:T(8,128)(2,1)} fusion(f32[8,2048,512]{2,1,0:T(8,128)} %fusion.211, bf16[512,8,64]{0,2,1:T(8,128)(2,1)S(1)} %get-tuple-element.889, f32[8,512]{1,0:T(8,128)S(1)} %get-tuple-element.890, f32[8,512]{1,0:T(8,128)S(1)} %get-tuple-element.887, pred[512,2048]{0,1:T(8,128)(4,1)S(1)} %or_and_fusion.8, ...), kind=kOutput, calls=%fused_computation.24.clone.1 | convolution fusion | flops 1124073472 | bytes 54034436 | tf_op jit(solution)/shard_map/while/body/eval_jaxpr/qhd,khd->hqk/dot_general | solution.py:230
  338.3 10.5 fusion.213
  349.9 7.2 multiply_bitcast_fusion.2
  357.1 8.5 copy.125
  365.6 70.8 %dynamic_update_slice.11 = f32[2,2048,8,64]{1,0,3,2:T(2,128)} dynamic-update-slice(f32[2,2048,8,64]{1,0,3,2:T(2,128)} %get-tuple-element.859, f32[1,2048,8,64]{1,0,3,2:T(1,128)} %copy.125, s32[]{:T(128)S(6)} %copy.148, s32[]{:T(128)} %constant.122.clone.1..sunk.2, s32[]{:T(128)} %constant.122.clone.1..sunk.2, s32[]{:T(128)} %constant.122.clone.1..sunk.2) | dynamic-update-slice | bytes 8388612 | tf_op jit(solution)/shard_map/while/body/jit(dynamic_update_index_in_dim)/dynamic_update_slice | solution.py:251
  436.4 16.1 %fusion.214 = f32[1,2048,8,64]{1,3,2,0:T(8,128)} fusion(bf16[512,8,64]{0,2,1:T(8,128)(2,1)S(1)} %get-tuple-element.889, f32[8,2048,512]{2,1,0:T(8,128)} %fusion.211, f32[8,512]{1,0:T(8,128)S(1)} %copy-done.58, pred[512,2048]{0,1:T(8,128)(4,1)S(1)} %copy-done.5), kind=kOutput, calls=%fused_computation.31.clone.1 | convolution fusion | flops 1107296256 | bytes 39337984 | tf_op jit(solution)/shard_map/while/body/eval_jaxpr/hqk,qhd->khd/dot_general | solution.py:243
  452.5 8.5 copy.126
  461.0 70.8 %dynamic_update_slice.12 = f32[2,2048,8,64]{1,0,3,2:T(2,128)} dynamic-update-slice(f32[2,2048,8,64]{1,0,3,2:T(2,128)} %get-tuple-element.860, f32[1,2048,8,64]{1,0,3,2:T(1,128)} %copy.126, s32[]{:T(128)S(6)} %copy.148, s32[]{:T(128)} %constant.122.clone.1..sunk.2, s32[]{:T(128)} %constant.122.clone.1..sunk.2, s32[]{:T(128)} %constant.122.clone.1..sunk.2) | dynamic-update-slice | bytes 8388612 | tf_op jit(solution)/shard_map/while/body/jit(dynamic_update_index_in_dim)/dynamic_update_slice | solution.py:251
  533.1 15.1 %fusion.211 = f32[8,2048,512]{2,1,0:T(8,128)} fusion(bf16[512,8,64]{0,2,1:T(8,128)(2,1)S(1)} %get-tuple-element.886, bf16[4096,8,64]{0,2,1:T(8,128)(2,1)} %get-tuple-element.881, s32[]{:T(128)S(6)} %select_n.206), kind=kOutput, calls=%fused_computation.35.clone.1 | convolution fusion | flops 1073741824 | bytes 36175876 | tf_op jit(solution)/shard_map/while/body/eval_jaxpr/qhd,khd->hqk/dot_general | solution.py:113
  550.0 20.8 %fusion.212 = bf16[8,512,2048]{1,2,0:T(8,128)(2,1)} fusion(f32[8,2048,512]{2,1,0:T(8,128)} %fusion.211, bf16[512,8,64]{0,2,1:T(8,128)(2,1)S(1)} %get-tuple-element.889, f32[8,512]{1,0:T(8,128)S(1)} %get-tuple-element.890, f32[8,512]{1,0:T(8,128)S(1)} %get-tuple-element.887, pred[512,2048]{0,1:T(8,128)(4,1)S(1)} %or_and_fusion.8, ...), kind=kOutput, calls=%fused_computation.24.clone.1 | convolution fusion | flops 1124073472 | bytes 54034436 | tf_op jit(solution)/shard_map/while/body/eval_jaxpr/qhd,khd->hqk/dot_general | solution.py:230
  570.8 10.7 fusion.213
  582.7 7.2 multiply_bitcast_fusion.2
  589.9 8.5 copy.125
  598.4 70.8 %dynamic_update_slice.11 = f32[2,2048,8,64]{1,0,3,2:T(2,128)} dynamic-update-slice(f32[2,2048,8,64]{1,0,3,2:T(2,128)} %get-tuple-element.859, f32[1,2048,8,64]{1,0,3,2:T(1,128)} %copy.125, s32[]{:T(128)S(6)} %copy.148, s32[]{:T(128)} %constant.122.clone.1..sunk.2, s32[]{:T(128)} %constant.122.clone.1..sunk.2, s32[]{:T(128)} %constant.122.clone.1..sunk.2) | dynamic-update-slice | bytes 8388612 | tf_op jit(solution)/shard_map/while/body/jit(dynamic_update_index_in_dim)/dynamic_update_slice | solution.py:251
  669.2 16.1 %fusion.214 = f32[1,2048,8,64]{1,3,2,0:T(8,128)} fusion(bf16[512,8,64]{0,2,1:T(8,128)(2,1)S(1)} %get-tuple-element.889, f32[8,2048,512]{2,1,0:T(8,128)} %fusion.211, f32[8,512]{1,0:T(8,128)S(1)} %copy-done.58, pred[512,2048]{0,1:T(8,128)(4,1)S(1)} %copy-done.5), kind=kOutput, calls=%fused_computation.31.clone.1 | convolution fusion | flops 1107296256 | bytes 39337984 | tf_op jit(solution)/shard_map/while/body/eval_jaxpr/hqk,qhd->khd/dot_general | solution.py:243
  685.3 8.5 copy.126
  693.8 70.8 %dynamic_update_slice.12 = f32[2,2048,8,64]{1,0,3,2:T(2,128)} dynamic-update-slice(f32[2,2048,8,64]{1,0,3,2:T(2,128)} %get-tuple-element.860, f32[1,2048,8,64]{1,0,3,2:T(1,128)} %copy.126, s32[]{:T(128)S(6)} %copy.148, s32[]{:T(128)} %constant.122.clone.1..sunk.2, s32[]{:T(128)} %constant.122.clone.1..sunk.2, s32[]{:T(128)} %constant.122.clone.1..sunk.2) | dynamic-update-slice | bytes 8388612 | tf_op jit(solution)/shard_map/while/body/jit(dynamic_update_index_in_dim)/dynamic_update_slice | solution.py:251
  765.0 14.8 %copy.118 = f32[64,8,2,2048]{3,1,2,0:T(8,128)} copy(f32[64,8,2,2048]{3,2,1,0:T(2,128)} %bitcast.259) | data formatting | bytes 16777216
  780.0 15.3 %copy.117 = f32[64,8,2,2048]{3,1,2,0:T(8,128)} copy(f32[64,8,2,2048]{3,2,1,0:T(2,128)} %bitcast.258) | data formatting | bytes 16777216
  798.4 51.8 %reduce-scatter.8.cloned.1.call-done = f32[512,512]{0,1:T(8,128)} async-done(((f32[4096,512]{0,1:T(8,128)}), f32[512,512]{0,1:T(8,128)}) %reduce-scatter.8.cloned.1.call-update) | async-done | bytes 1048592 | tf_op jit(solution)/shard_map/reduce_scatter | solution.py:258
  851.5 74.3 %reduce-scatter.6.cloned.1.call-done = f32[512,512]{0,1:T(8,128)} async-done(((f32[4096,512]{0,1:T(8,128)}), f32[512,512]{0,1:T(8,128)}) %reduce-scatter.6.cloned.1.call-update) | async-done | bytes 1048592 | tf_op jit(solution)/shard_map/reduce_scatter | solution.py:255
  942.3 13.4 %reduce-scatter.12.cloned.1.call-done = f32[128,512]{1,0:T(8,128)} async-done(((f32[512,512]{1,0:T(8,128)}), f32[128,512]{1,0:T(8,128)}) %reduce-scatter.12.cloned.1.call-update) | async-done | bytes 262160 | tf_op jit(solution)/shard_map/reduce_scatter | solution.py:269
  955.7 61.3 %reduce-scatter.10.cloned.1.call-done = f32[128,1536]{0,1:T(8,128)} async-done(((f32[512,1536]{0,1:T(8,128)}), f32[128,1536]{0,1:T(8,128)}) %reduce-scatter.10.cloned.1.call-update) | async-done | bytes 786448 | tf_op jit(solution)/shard_map/reduce_scatter | solution.py:268
  1022.8 10.4 all-reduce.4
  1033.4 4.9 reduce-scatter.14.cloned.1.call-done
  1038.3 12.9 all-reduce.2
  1055.2 217.3 %all-reduce.7.cloned.1.call-done = (f32[128,1536]{0,1:T(8,128)}, f32[128,512]{1,0:T(8,128)}, f32[2,512,2048]{2,1,0:T(8,128)}, f32[2,2048,512]{2,1,0:T(8,128)}) async-done(((f32[128,1536]{0,1:T(8,128)}, f32[128,512]{1,0:T(8,128)}, f32[2,512,2048]{2,1,0:T(8,128)}, f32[2,2048,512]{2,1,0:T(8,128)}), (f32[128,1536]{0,1:T(8,128)}, f32[128,512]{1,0:T(8,128)}, f32[2,512,2048]{2,1,0:T(8,128)}, ...) | async-done | bytes 17825808 | tf_op jit(solution)/shard_map/psum | solution.py:274
  1276.6 8.0 copy.161
  (304 shorter events, 119.4 us)
Async XLA Ops:
  7.2 42.2 %all-gather.6.cloned.1.call-start = ((), (), s32[]{:S(2)}) async-start(), calls=%async_computation.9 | async-start | bytes 1966080 | tf_op jit(solution)/shard_map/all_gather | solution.py:89
  7.9 45.3 %copy-start.39 = (bf16[1,512,512]{2,1,0:T(8,128)(2,1)S(1)}, bf16[1,512,512]{2,1,0:T(8,128)(2,1)}, u32[]{:S(2)}) copy-start(bf16[1,512,512]{2,1,0:T(8,128)(2,1)} %param.18) | copy-start | bytes 1572868
  7.9 46.3 %copy-start.64 = (bf16[128]{0:T(256)(128)(2,1)S(1)}, bf16[128]{0:T(256)(128)(2,1)}, u32[]{:S(2)}) copy-start(bf16[128]{0:T(256)(128)(2,1)} %param.27) | copy-start | bytes 772
  7.9 55.6 %copy-start.65 = (bf16[128]{0:T(256)(128)(2,1)S(1)}, bf16[128]{0:T(256)(128)(2,1)}, u32[]{:S(2)}) copy-start(bf16[128]{0:T(256)(128)(2,1)} %param.26) | copy-start | bytes 772
  7.9 64.9 %copy-start.46 = (s32[16]{0:T(128)S(1)}, s32[16]{0:T(128)}, u32[]{:S(2)}) copy-start(s32[16]{0:T(128)} %param.20) | copy-start | bytes 196
  8.0 75.8 %copy-start.62 = (bf16[128,8]{0,1:T(8,128)(2,1)S(1)}, bf16[128,8]{0,1:T(8,128)(2,1)}, u32[]{:S(2)}) copy-start(bf16[128,8]{0,1:T(8,128)(2,1)} %param.25) | copy-start | bytes 6148
  8.0 88.0 %copy-start.30 = (s32[1,4096]{1,0:T(1,128)S(1)}, s32[1,4096]{1,0:T(1,128)}, u32[]{:S(2)}) copy-start(s32[1,4096]{1,0:T(1,128)} %param.21) | copy-start | bytes 49156
  8.0 88.0 %copy-start.44 = (bf16[128,512]{1,0:T(8,128)(2,1)S(1)}, bf16[128,512]{1,0:T(8,128)(2,1)}, u32[]{:S(2)}) copy-start(bf16[128,512]{1,0:T(8,128)(2,1)} %param.24) | copy-start | bytes 393220
  8.0 105.0 %all-gather.10.cloned.1.call-start = ((), (), s32[]{:S(2)}) async-start(), calls=%async_computation.11 | async-start | bytes 4718592 | tf_op jit(solution)/shard_map/all_gather | solution.py:98
  52.0 60.1 %copy-start.63 = (s32[1,512]{1,0:T(1,128)S(1)}, s32[1,512]{1,0:T(1,128)}, u32[]{:S(2)}) copy-start(s32[1,512]{1,0:T(1,128)} %param.22) | copy-start | bytes 6148
  53.1 133.8 %all-gather.8.cloned.1.call-start = ((), (), s32[]{:S(2)}) async-start(), calls=%async_computation.10 | async-start | bytes 4718592 | tf_op jit(solution)/shard_map/all_gather | solution.py:99
  193.4 30.9 %copy-start.16 = (bf16[512,512]{1,0:T(8,128)(2,1)S(1)}, bf16[512,512]{1,0:T(8,128)(2,1)}, u32[]{:S(2)}) copy-start(bf16[512,512]{1,0:T(8,128)(2,1)} %all_gather.24) | copy-start | bytes 1572868
  224.3 18.4 %copy-start.13 = (bf16[512,8,64]{0,2,1:T(8,128)(2,1)}, bf16[512,8,64]{0,2,1:T(8,128)(2,1)S(1)}, u32[]{:S(2)}) copy-start(bf16[512,8,64]{0,2,1:T(8,128)(2,1)S(1)} %convert_element_type.105) | copy-start | bytes 1572868
  226.0 55.6 %copy-start.1 = (f32[512,512]{0,1:T(8,128)}, f32[512,512]{0,1:T(8,128)S(1)}, u32[]{:S(2)}) copy-start(f32[512,512]{0,1:T(8,128)S(1)} %get-tuple-element.510) | copy-start | bytes 3145732
  226.3 25.8 %copy-start.53 = (f32[512]{0:T(512)}, f32[512]{0:T(512)S(1)}, u32[]{:S(2)}) copy-start(f32[512]{0:T(512)S(1)} %add_rsqrt_fusion) | copy-start | bytes 6148
  226.5 51.7 %copy-start.9 = (bf16[512,512]{0,1:T(8,128)(2,1)}, bf16[512,512]{0,1:T(8,128)(2,1)S(1)}, u32[]{:S(2)}) copy-start(bf16[512,512]{0,1:T(8,128)(2,1)S(1)} %add_convert_fusion) | copy-start | bytes 1572868
  227.0 48.4 %copy-start.42 = (bf16[8,512]{1,0:T(8,128)(2,1)}, bf16[8,512]{1,0:T(8,128)(2,1)S(1)}, u32[]{:S(2)}) copy-start(bf16[8,512]{1,0:T(8,128)(2,1)S(1)} %convert_bitcast_fusion) | copy-start | bytes 24580
  228.0 9.7 all-to-all-start
  237.7 9.9 all-to-all-start.2
  256.8 9.2 all-to-all-start.3
  260.2 18.1 %copy-start.45 = (f32[16,512]{1,0:T(8,128)S(1)}, f32[16,512]{1,0:T(8,128)}, u32[]{:S(2)}) copy-start(f32[16,512]{1,0:T(8,128)} %get-tuple-element.491) | copy-start | bytes 98308
  266.0 9.2 all-to-all-start.1
  269.4 580.8 %reduce-scatter.8.cloned.1.call-start = ((), (), s32[]{:S(2)}) async-start(), calls=%async_computation.13 | async-start | bytes 9437184 | tf_op jit(solution)/shard_map/reduce_scatter | solution.py:258
  299.3 18.2 %copy-start.54 = (f32[8,512]{1,0:T(8,128)}, f32[8,512]{1,0:T(8,128)S(1)}, u32[]{:S(2)}) copy-start(f32[8,512]{1,0:T(8,128)S(1)} %get-tuple-element.890) | copy-start | bytes 49156 | tf_op jit(solution)/shard_map/while
  300.6 17.0 %copy-start.21 = (bf16[4096,8,64]{0,2,1:T(8,128)(2,1)S(1)}, bf16[4096,8,64]{0,2,1:T(8,128)(2,1)}, u32[]{:S(2)}) copy-start(bf16[4096,8,64]{0,2,1:T(8,128)(2,1)} %get-tuple-element.888) | copy-start | bytes 12582916 | tf_op jit(solution)/shard_map/while
  317.5 20.8 %copy-start.4 = (pred[512,2048]{0,1:T(8,128)(4,1)}, pred[512,2048]{0,1:T(8,128)(4,1)S(1)}, u32[]{:S(2)}) copy-start(pred[512,2048]{0,1:T(8,128)(4,1)S(1)} %or_and_fusion.8) | copy-start | bytes 3145732 | tf_op jit(solution)/shard_map/while
  365.6 70.8 %copy-start.5 = (pred[512,2048]{0,1:T(8,128)(4,1)S(1)}, pred[512,2048]{0,1:T(8,128)(4,1)}, u32[]{:S(2)}) copy-start(pred[512,2048]{0,1:T(8,128)(4,1)} %copy-done.4) | copy-start | bytes 3145732 | tf_op jit(solution)/shard_map/while
  365.6 70.8 %copy-start.58 = (f32[8,512]{1,0:T(8,128)S(1)}, f32[8,512]{1,0:T(8,128)}, u32[]{:S(2)}) copy-start(f32[8,512]{1,0:T(8,128)} %get-tuple-element.988) | copy-start | bytes 49156 | tf_op jit(solution)/shard_map/while
  461.0 70.8 %copy-start.27 = (s32[4096]{0:T(1024)S(1)}, s32[4096]{0:T(1024)}, u32[]{:S(2)}) copy-start(s32[4096]{0:T(1024)} %copy-done.26) | copy-start | bytes 49156 | tf_op jit(solution)/shard_map/while
  461.0 70.8 %copy-start.32 = (s32[4096]{0:T(1024)S(1)}, s32[4096]{0:T(1024)}, u32[]{:S(2)}) copy-start(s32[4096]{0:T(1024)} %copy-done.31) | copy-start | bytes 49156 | tf_op jit(solution)/shard_map/while
  461.0 70.8 %copy-start.55 = (f32[8,512]{1,0:T(8,128)S(1)}, f32[8,512]{1,0:T(8,128)}, u32[]{:S(2)}) copy-start(f32[8,512]{1,0:T(8,128)} %copy-done.54) | copy-start | bytes 49156 | tf_op jit(solution)/shard_map/while
  531.8 16.4 %copy-start.31 = (s32[4096]{0:T(1024)}, s32[4096]{0:T(1024)S(1)}, u32[]{:S(2)}) copy-start(s32[4096]{0:T(1024)S(1)} %get-tuple-element.884) | copy-start | bytes 49156 | tf_op jit(solution)/shard_map/while
  531.8 18.2 %copy-start.54 = (f32[8,512]{1,0:T(8,128)}, f32[8,512]{1,0:T(8,128)S(1)}, u32[]{:S(2)}) copy-start(f32[8,512]{1,0:T(8,128)S(1)} %get-tuple-element.890) | copy-start | bytes 49156 | tf_op jit(solution)/shard_map/while
  533.1 17.0 %copy-start.21 = (bf16[4096,8,64]{0,2,1:T(8,128)(2,1)S(1)}, bf16[4096,8,64]{0,2,1:T(8,128)(2,1)}, u32[]{:S(2)}) copy-start(bf16[4096,8,64]{0,2,1:T(8,128)(2,1)} %get-tuple-element.888) | copy-start | bytes 12582916 | tf_op jit(solution)/shard_map/while
  550.0 20.8 %copy-start.4 = (pred[512,2048]{0,1:T(8,128)(4,1)}, pred[512,2048]{0,1:T(8,128)(4,1)S(1)}, u32[]{:S(2)}) copy-start(pred[512,2048]{0,1:T(8,128)(4,1)S(1)} %or_and_fusion.8) | copy-start | bytes 3145732 | tf_op jit(solution)/shard_map/while
  598.4 70.8 %copy-start.5 = (pred[512,2048]{0,1:T(8,128)(4,1)S(1)}, pred[512,2048]{0,1:T(8,128)(4,1)}, u32[]{:S(2)}) copy-start(pred[512,2048]{0,1:T(8,128)(4,1)} %copy-done.4) | copy-start | bytes 3145732 | tf_op jit(solution)/shard_map/while
  598.4 70.8 %copy-start.58 = (f32[8,512]{1,0:T(8,128)S(1)}, f32[8,512]{1,0:T(8,128)}, u32[]{:S(2)}) copy-start(f32[8,512]{1,0:T(8,128)} %get-tuple-element.988) | copy-start | bytes 49156 | tf_op jit(solution)/shard_map/while
  693.8 70.8 %copy-start.27 = (s32[4096]{0:T(1024)S(1)}, s32[4096]{0:T(1024)}, u32[]{:S(2)}) copy-start(s32[4096]{0:T(1024)} %copy-done.26) | copy-start | bytes 49156 | tf_op jit(solution)/shard_map/while
  693.8 70.8 %copy-start.32 = (s32[4096]{0:T(1024)S(1)}, s32[4096]{0:T(1024)}, u32[]{:S(2)}) copy-start(s32[4096]{0:T(1024)} %copy-done.31) | copy-start | bytes 49156 | tf_op jit(solution)/shard_map/while
  693.8 70.8 %copy-start.55 = (f32[8,512]{1,0:T(8,128)S(1)}, f32[8,512]{1,0:T(8,128)}, u32[]{:S(2)}) copy-start(f32[8,512]{1,0:T(8,128)} %copy-done.54) | copy-start | bytes 49156 | tf_op jit(solution)/shard_map/while
  779.8 146.0 %reduce-scatter.6.cloned.1.call-start = ((), (), s32[]{:S(2)}) async-start(), calls=%async_computation.12 | async-start | bytes 9437184 | tf_op jit(solution)/shard_map/reduce_scatter | solution.py:255
  795.4 160.3 %reduce-scatter.12.cloned.1.call-start = ((), (), s32[]{:S(2)}) async-start(), calls=%async_computation.15 | async-start | bytes 1310720 | tf_op jit(solution)/shard_map/reduce_scatter | solution.py:269
  798.3 218.8 %reduce-scatter.10.cloned.1.call-start = ((), (), s32[]{:S(2)}) async-start(), calls=%async_computation.14 | async-start | bytes 3932160 | tf_op jit(solution)/shard_map/reduce_scatter | solution.py:268
  798.4 133.2 %copy-start.35 = (bf16[512,8,64]{0,2,1:T(8,128)(2,1)}, bf16[512,8,64]{0,2,1:T(8,128)(2,1)S(1)}, u32[]{:S(2)}) copy-start(bf16[512,8,64]{0,2,1:T(8,128)(2,1)S(1)} %convert.10) | copy-start | bytes 1572868
  851.5 80.1 %copy-start.37 = (bf16[512,512]{0,1:T(8,128)(2,1)}, bf16[512,512]{0,1:T(8,128)(2,1)S(1)}, u32[]{:S(2)}) copy-start(bf16[512,512]{0,1:T(8,128)(2,1)S(1)} %convert.12) | copy-start | bytes 1572868
  931.7 106.6 %reduce-scatter.14.cloned.1.call-start = ((), (), s32[]{:S(2)}) async-start(), calls=%async_computation.16 | async-start | bytes 20480 | tf_op jit(solution)/shard_map/reduce_scatter | solution.py:270
  937.4 335.1 %all-reduce.7.cloned.1.call-start = ((), (), s32[]{:S(2)}) async-start(), calls=%async_computation.17 | async-start | bytes 35651584 | tf_op jit(solution)/shard_map/psum | solution.py:274
  1017.1 34.1 %copy-start.36 = (bf16[512,8,64]{0,2,1:T(8,128)(2,1)S(1)}, bf16[512,8,64]{0,2,1:T(8,128)(2,1)}, u32[]{:S(2)}) copy-start(bf16[512,8,64]{0,2,1:T(8,128)(2,1)} %copy-done.35) | copy-start | bytes 1572868
  (45 other events, 244.7 us)
Sparse Core Ops, SparseCore 0:
  9.6 39.7 all-gather.5
  53.2 35.5 all-gather.9
  113.1 35.5 all-gather.7
  779.9 70.2 reduce-scatter.7
  854.5 71.2 reduce-scatter.5
  928.5 27.1 reduce-scatter.11
  958.1 58.8 reduce-scatter.9
  1019.4 18.9 reduce-scatter.13
  1043.8 228.6 all-reduce.6
where the time goes:
time: 1320 us; the launch traced here: 1290 us
  waiting for transfers between devices  481 us (36%)
  local copies, waits for them, and re-layouts  401 us (30%)
  matrix products  233 us (18%)
  blocking collectives  68.7 us (5%)
  other arithmetic  59.7 us (5%)
  loops' own time  20 us (2%)
  between operations  15.6 us (1%)
  starting transfers between devices  14.9 us (1%)
    dynamic_update_slice x8, local copies, waits for them, and re-layouts, on_device(): lax.scan(grad_step, jnp.zeros((tok_count, HEADS, HEAD), jnp.float32), blo...  317 us
    psum x1, waiting for transfers between devices, on_device(): lax.psum((dense[0], dense[1], dense[2], dense[3], dense[4], grad_up_own,...  217 us
    reduce_scatter x1, waiting for transfers between devices, on_device(): lax.psum_scatter(grad_keys.reshape(full_rows, width), 'ctx', scatter_dime...  74.3 us
    dot_general x4, matrix products, block_scores(): jnp.einsum('qhd,khd->hqk', query_heads, key_block, preferred_element_type...  61.4 us
    reduce_scatter x1, waiting for transfers between devices, on_device(): lax.psum_scatter(grad_qkv_part, 'fsdp', scatter_dimension=0, tiled=True)  61.3 us
    unnamed x129, local copies, waits for them, and re-layouts  57.7 us
    reduce_scatter x1, waiting for transfers between devices, on_device(): lax.psum_scatter(grad_vals.reshape(full_rows, width), 'ctx', scatter_dime...  51.8 us
    dot_general x2, matrix products, grad_step(): jnp.einsum('qhd,khd->hqk', grad_heads, val_block, preferred_element_type=...  41.6 us
  transfers between devices with their start and end apart: 13, of which 11 were waited for; matrix products, arithmetic and copies ran while one was open for 11% of the time, Pallas kernels for 0%

commit v1 on v0

--- a/solution.py
+++ b/solution.py
@@ -1,6 +1,10 @@
+import functools
+
 import jax
 import jax.numpy as jnp
 from jax import lax
+from jax.experimental import pallas as pl
+from jax.experimental.pallas import tpu as pltpu
 from jax.sharding import PartitionSpec as P
 
 HEADS = 8
@@ -287,6 +291,674 @@
     )
 
 
+LOG2E = 1.4426950408889634
+HIDE = -1e30
+SUPER = 512
+VMEM = pl.BlockSpec(memory_space=pltpu.VMEM)
+SMEM = pl.BlockSpec(memory_space=pltpu.SMEM)
+ANY = pl.BlockSpec(memory_space=pl.ANY)
+LIMIT = 60 << 20
+
+
+def dot_nn(left, right):
+    return lax.dot_general(left, right, (((1,), (0,)), ((), ())), preferred_element_type=jnp.float32)
+
+
+def dot_nt(left, right):
+    return lax.dot_general(left, right, (((1,), (1,)), ((), ())), preferred_element_type=jnp.float32)
+
+
+def dot_tn(left, right):
+    return lax.dot_general(left, right, (((0,), (0,)), ((), ())), preferred_element_type=jnp.float32)
+
+
+def split3(value):
+    one = value.astype(jnp.bfloat16)
+    rest = value - one.astype(jnp.float32)
+    two = rest.astype(jnp.bfloat16)
+    three = (rest - two.astype(jnp.float32)).astype(jnp.bfloat16)
+    return one, two, three
+
+
+def read_order(table_ref, seg_ref, inv_ref, first_ref, last_ref, blocks, block_len, per):
+    for t in range(blocks):
+        inv_ref[table_ref[t]] = t
+    for s in range(blocks // per):
+        first_ref[s] = seg_ref[inv_ref[s * per], 0]
+        last_ref[s] = seg_ref[inv_ref[s * per + per - 1], block_len - 1]
+
+
+def count_below(ref, limit, n):
+    total = jnp.int32(0)
+    for s in range(n):
+        total = total + (ref[s] < limit).astype(jnp.int32)
+    return total
+
+
+def fwd_body(blocks, block_len, table_ref, seg_ref, tok_ref, w_ref, segrow_ref, att_ref, qf_ref, kf_ref, vf_ref, kp_ref, stat_ref,
+             inv_ref, first_ref, last_ref):
+    per = SUPER // block_len
+    runs = blocks // per
+    read_order(table_ref, seg_ref, inv_ref, first_ref, last_ref, blocks, block_len, per)
+    weight = w_ref[...].reshape(w_ref.shape[0] * w_ref.shape[1], w_ref.shape[2])
+    factor = HEAD ** (-0.5) * LOG2E
+    ids = lax.broadcasted_iota(jnp.int32, (8, 1), 0) + 1
+    eye = (lax.broadcasted_iota(jnp.int32, (8, HEAD), 0) == lax.broadcasted_iota(jnp.int32, (8, HEAD), 1)).astype(jnp.bfloat16)
+    lane = lax.broadcasted_iota(jnp.int32, (block_len, HEAD), 1)
+    ones_k = ((lane >= 8) & (lane < 11)).astype(jnp.float32)
+    ones_v = (lane < 3).astype(jnp.bfloat16)
+
+    def project(s, carry):
+        t = inv_ref[s]
+        rows = tok_ref[pl.ds(pl.multiple_of(t * block_len, block_len), block_len), :]
+        qkv = dot_nn(rows, weight).astype(jnp.bfloat16)
+        q, k, v = qkv[:, :HEAD], qkv[:, HEAD:2 * HEAD], qkv[:, 2 * HEAD:]
+        one, two, three = split3(k.astype(jnp.float32) * factor)
+        same = segrow_ref[pl.ds(t, 1), :] == ids
+        other = dot_tn(jnp.where(same, 0.0, 1.0).astype(jnp.bfloat16), eye).astype(jnp.bfloat16)
+        hidden = (dot_tn(jnp.where(same, HIDE, 0.0).astype(jnp.bfloat16), eye) + ones_k).astype(jnp.bfloat16)
+        at = pl.ds(pl.multiple_of(s * block_len, block_len), block_len)
+        qf_ref[at, :] = jnp.concatenate([q, q, q, other], axis=1)
+        kf_ref[at, :] = jnp.concatenate([one, two, three, hidden], axis=1)
+        vf_ref[at, :] = jnp.concatenate([v, ones_v], axis=1)
+        kp_ref[at, :] = jnp.concatenate([k, k], axis=1)
+        return carry
+
+    lax.fori_loop(0, blocks, project, 0)
+    start_hidden = count_below(first_ref, 1, runs)
+    row = lax.broadcasted_iota(jnp.int32, (SUPER, SUPER), 0)
+    col = lax.broadcasted_iota(jnp.int32, (SUPER, SUPER), 1)
+    causal = col <= row
+
+    def query_run(run, carry):
+        at_q = pl.ds(pl.multiple_of(run * SUPER, SUPER), SUPER)
+        query = qf_ref[at_q, :]
+        skip = jnp.maximum(count_below(last_ref, first_ref[run], runs) - start_hidden, 0)
+
+        def tile(index, diagonal, state):
+            top, acc = state
+            at_k = pl.ds(pl.multiple_of(index * SUPER, SUPER), SUPER)
+            scores = dot_nt(query, kf_ref[at_k, :])
+            if diagonal:
+                scores = jnp.where(causal, scores, HIDE)
+            new_top = jnp.maximum(top, jnp.max(scores, axis=1, keepdims=True))
+            weights = jnp.exp2(scores - new_top)
+            acc = acc * jnp.exp2(top - new_top) + dot_nn(weights.astype(jnp.bfloat16), vf_ref[at_k, :])
+            return new_top, acc
+
+        def step(n, state):
+            return tile(jnp.where(n < start_hidden, n, n + skip), False, state)
+
+        state = (jnp.full((SUPER, 1), HIDE, jnp.float32), jnp.zeros((SUPER, 2 * HEAD), jnp.float32))
+        state = lax.fori_loop(0, run - skip, step, state)
+        top, acc = tile(run, True, state)
+        total = acc[:, HEAD:HEAD + 1]
+        lse = top + jnp.log2(total)
+        out = acc[:, :HEAD] / total
+        stat_ref[at_q, :] = jnp.concatenate([out, jnp.broadcast_to(lse, (SUPER, HEAD))], axis=1)
+        return carry
+
+    lax.fori_loop(0, runs, query_run, 0)
+    for c in range(blocks // 2):
+        parts = []
+        for half in range(2):
+            s = table_ref[2 * c + half]
+            parts.append(stat_ref[pl.ds(pl.multiple_of(s * block_len, block_len), block_len), :HEAD])
+        att_ref[c] = jnp.concatenate(parts, axis=1).astype(jnp.bfloat16)
+
+
+def attn_fwd(tokens_all, weight, table, segs):
+    rows = tokens_all.shape[0]
+    blocks, block_len = segs.shape
+    runs = rows // SUPER
+    return pl.pallas_call(
+        functools.partial(fwd_body, blocks, block_len),
+        out_shape=(
+            jax.ShapeDtypeStruct((blocks // 2, block_len, 2 * HEAD), jnp.bfloat16),
+            jax.ShapeDtypeStruct((rows, 4 * HEAD), jnp.bfloat16),
+            jax.ShapeDtypeStruct((rows, 4 * HEAD), jnp.bfloat16),
+            jax.ShapeDtypeStruct((rows, 2 * HEAD), jnp.bfloat16),
+            jax.ShapeDtypeStruct((rows, 2 * HEAD), jnp.bfloat16),
+            jax.ShapeDtypeStruct((rows, 2 * HEAD), jnp.float32),
+        ),
+        in_specs=[SMEM, SMEM, VMEM, VMEM, VMEM],
+        out_specs=(VMEM,) * 6,
+        scratch_shapes=[pltpu.SMEM((blocks,), jnp.int32), pltpu.SMEM((runs,), jnp.int32), pltpu.SMEM((runs,), jnp.int32)],
+        compiler_params=pltpu.CompilerParams(vmem_limit_bytes=LIMIT),
+        name="attention",
+    )(table, segs, tokens_all, weight, segs)
+
+
+def bwd_body(blocks, block_len, table_ref, seg_ref, do_ref, qf_ref, kf_ref, vf_ref, kp_ref, stat_ref, out_ref,
+             inv_ref, first_ref, last_ref, qs_ref, dof_ref, dq_ref, dk_ref, dv_ref):
+    per = SUPER // block_len
+    runs = blocks // per
+    read_order(table_ref, seg_ref, inv_ref, first_ref, last_ref, blocks, block_len, per)
+    lane = lax.broadcasted_iota(jnp.int32, (block_len, HEAD), 1)
+    zero = jnp.zeros((), jnp.bfloat16)
+
+    def spread(value, offset):
+        one, two, three = (jnp.broadcast_to(part, (block_len, HEAD)) for part in split3(value))
+        out = jnp.where(lane == offset, one, zero)
+        out = jnp.where(lane == offset + 1, two, out)
+        return jnp.where(lane == offset + 2, three, out)
+
+    def prepare(s, carry):
+        t = inv_ref[s]
+        at = pl.ds(pl.multiple_of(s * block_len, block_len), block_len)
+        both = do_ref[t // 2]
+        grad = jnp.where(t % 2 == 0, both[:, :HEAD], both[:, HEAD:])
+        stat = stat_ref[at, :]
+        delta = jnp.sum(grad.astype(jnp.float32) * stat[:, :HEAD], axis=1, keepdims=True)
+        dof_ref[at, :] = jnp.concatenate([grad, spread(-delta, 0)], axis=1)
+        old = qf_ref[at, :]
+        tail = jnp.where(lane < 8, old[:, 3 * HEAD:], spread(-stat[:, HEAD:HEAD + 1], 8))
+        qs_ref[at, :] = jnp.concatenate([old[:, :3 * HEAD], tail], axis=1)
+        dq_ref[at, :] = jnp.zeros((block_len, 2 * HEAD), jnp.float32)
+        return carry
+
+    lax.fori_loop(0, blocks, prepare, 0)
+    causal = lax.broadcasted_iota(jnp.int32, (SUPER, SUPER), 0) <= lax.broadcasted_iota(jnp.int32, (SUPER, SUPER), 1)
+
+    def key_run(run, carry):
+        at_k = pl.ds(pl.multiple_of(run * SUPER, SUPER), SUPER)
+        end = jnp.where(first_ref[run] == 0, runs, count_below(first_ref, last_ref[run] + 1, runs))
+
+        def tile(index, diagonal):
+            at_q = pl.ds(pl.multiple_of(index * SUPER, SUPER), SUPER)
+            scores = dot_nt(kf_ref[at_k, :], qs_ref[at_q, :])
+            probs = jnp.exp2(scores)
+            if diagonal:
+                probs = jnp.where(causal, probs, 0.0)
+            slope = dot_nt(vf_ref[at_k, :], dof_ref[at_q, :])
+            grad = (probs * slope).astype(jnp.bfloat16)
+            dv = dot_nn(probs.astype(jnp.bfloat16), dof_ref[at_q, :])
+            dk = dot_nn(grad, qs_ref[at_q, :2 * HEAD])
+            if diagonal:
+                dv_ref[...] = dv
+                dk_ref[...] = dk
+            else:
+                dv_ref[...] += dv
+                dk_ref[...] += dk
+            dq_ref[at_q, :] += dot_tn(grad, kp_ref[at_k, :])
+
+        tile(run, True)
+
+        def step(index, inner):
+            tile(index, False)
+            return inner
+
+        lax.fori_loop(run + 1, end, step, 0)
+        scale = HEAD ** (-0.5)
+        stat_dk = (dk_ref[:, :HEAD] * scale).astype(jnp.bfloat16)
+        stat_dv = dv_ref[:, :HEAD].astype(jnp.bfloat16)
+        stat_dq = (dq_ref[at_k, :HEAD] * scale).astype(jnp.bfloat16)
+        for part in range(per):
+            t = inv_ref[run * per + part]
+            rows = slice(part * block_len, (part + 1) * block_len)
+            pieces = (stat_dq[rows], stat_dk[rows], stat_dv[rows])
+            for parity in range(2):
+                @pl.when(t % 2 == parity)
+                def _():
+                    for kind in range(3):
+                        low = kind * 2 * HEAD + parity * HEAD
+                        out_ref[t // 2, :, low:low + HEAD] = pieces[kind]
+        return carry
+
+    lax.fori_loop(0, runs, key_run, 0)
+
+
+def attn_bwd(grad, saved, table, segs):
+    blocks, block_len = segs.shape
+    rows = blocks * block_len
+    runs = rows // SUPER
+    return pl.pallas_call(
+        functools.partial(bwd_body, blocks, block_len),
+        out_shape=jax.ShapeDtypeStruct((blocks // 2, block_len, 6 * HEAD), jnp.bfloat16),
+        in_specs=[SMEM, SMEM] + [VMEM] * 6,
+        out_specs=VMEM,
+        scratch_shapes=[
+            pltpu.SMEM((blocks,), jnp.int32), pltpu.SMEM((runs,), jnp.int32), pltpu.SMEM((runs,), jnp.int32),
+            pltpu.VMEM((rows, 4 * HEAD), jnp.bfloat16), pltpu.VMEM((rows, 2 * HEAD), jnp.bfloat16),
+            pltpu.VMEM((rows, 2 * HEAD), jnp.float32), pltpu.VMEM((SUPER, 2 * HEAD), jnp.float32),
+            pltpu.VMEM((SUPER, 2 * HEAD), jnp.float32),
+        ],
+        compiler_params=pltpu.CompilerParams(vmem_limit_bytes=LIMIT),
+        name="attention_grad",
+    )(table, segs, grad, *saved)
+
+
+MESH = pl.DeviceIdType.MESH
+
+
+def flip(index, bit):
+    return index + bit - 2 * bit * lax.rem(index // bit, 2)
+
+
+def meet(devices):
+    barrier = pltpu.get_barrier_semaphore()
+    for device in devices:
+        pl.semaphore_signal(barrier, inc=1, device_id=device, device_id_type=MESH)
+    pl.semaphore_wait(barrier, len(devices))
+
+
+def push(src, dst, send_sem, recv_sem, device):
+    return pltpu.make_async_remote_copy(
+        src_ref=src, dst_ref=dst, send_sem=send_sem, recv_sem=recv_sem, device_id=device, device_id_type=MESH
+    )
+
+
+def exchange_body(axis, count, x_ref, out_ref, own_sem, send_sem, recv_sem):
+    spot = {"ctx": lax.axis_index("ctx"), "fsdp": lax.axis_index("fsdp")}
+    me = spot[axis]
+    others = [lax.rem(me + k, count) for k in range(1, count)]
+    meet([(other, spot["fsdp"]) if axis == "ctx" else (spot["ctx"], other) for other in others])
+    own = pltpu.make_async_copy(x_ref.at[me], out_ref.at[me], own_sem)
+    own.start()
+    copies = []
+    for k, other in enumerate(others):
+        device = (other, spot["fsdp"]) if axis == "ctx" else (spot["ctx"], other)
+        copies.append(push(x_ref.at[other], out_ref.at[me], send_sem.at[k], recv_sem.at[k], device))
+        copies[-1].start()
+    own.wait()
+    for copy in copies:
+        copy.wait()
+
+
+def exchange(x, axis, collective_id, name):
+    count = x.shape[0]
+    return pl.pallas_call(
+        functools.partial(exchange_body, axis, count),
+        out_shape=jax.ShapeDtypeStruct(x.shape, x.dtype),
+        in_specs=[ANY],
+        out_specs=ANY,
+        scratch_shapes=[pltpu.SemaphoreType.DMA, pltpu.SemaphoreType.DMA((count - 1,)), pltpu.SemaphoreType.DMA((count - 1,))],
+        compiler_params=pltpu.CompilerParams(collective_id=collective_id, has_side_effects=True),
+        name=name,
+    )(x)
+
+
+def gather_body(zs, tok_ref, *refs):
+    count = (len(refs) - 9) // 2
+    shards, toks_ref, wholes = refs[:count], refs[count], refs[count + 1:2 * count + 1]
+    own_sem, z_send, z_recv, far_send, near_send, own_recv, diag_recv, near_recv = refs[2 * count + 1:]
+    me, z = lax.axis_index("ctx"), lax.axis_index("fsdp")
+    sib, xn, yn, diag = flip(me, 1), flip(me, 2), flip(me, 4), flip(flip(me, 2), 4)
+    z_peers = [lax.rem(z + k, zs) for k in range(1, zs)]
+    meet([(sib, z), (xn, z), (yn, z)] + [(me, other) for other in z_peers])
+    half = tok_ref.shape[0] // 2
+
+    def part(device, k):
+        return toks_ref.at[device, pl.ds(k * half, half)]
+
+    started = []
+
+    def go(copy):
+        copy.start()
+        started.append(copy)
+
+    for k in (0, 1):
+        rows = tok_ref.at[pl.ds(k * half, half)]
+        go(push(rows, part(me, k), far_send.at[0, k], own_recv.at[0, k], (xn, z)))
+        rows = tok_ref.at[pl.ds((1 - k) * half, half)]
+        go(push(rows, part(me, 1 - k), far_send.at[1, 1 - k], own_recv.at[1, 1 - k], (yn, z)))
+    for i, (shard, whole) in enumerate(zip(shards, wholes)):
+        for k, other in enumerate(z_peers):
+            go(push(shard, whole.at[z], z_send.at[i, k], z_recv.at[i, k], (me, other)))
+    for k in (0, 1):
+        rows = tok_ref.at[pl.ds(k * half, half)]
+        go(push(rows, part(me, k), near_send.at[0, k], near_recv.at[0, k], (sib, z)))
+    locals_ = [pltpu.make_async_copy(tok_ref, toks_ref.at[me], own_sem.at[0])]
+    for i, (shard, whole) in enumerate(zip(shards, wholes)):
+        locals_.append(pltpu.make_async_copy(shard, whole.at[z], own_sem.at[i + 1]))
+    for copy in locals_:
+        copy.start()
+
+    def arrived(device, k, sem):
+        push(part(device, k), part(device, k), far_send.at[0, 0], sem, (sib, z)).wait_recv()
+
+    def relay(device, k, i):
+        go(push(part(device, k), part(device, k), near_send.at[i, k], near_recv.at[i, k], (sib, z)))
+
+    arrived(xn, 0, own_recv.at[0, 0])
+    go(push(part(xn, 0), part(xn, 0), far_send.at[2, 0], diag_recv.at[0], (yn, z)))
+    relay(xn, 0, 1)
+    arrived(yn, 1, own_recv.at[1, 1])
+    go(push(part(yn, 1), part(yn, 1), far_send.at[2, 1], diag_recv.at[1], (xn, z)))
+    relay(yn, 1, 2)
+    arrived(xn, 1, own_recv.at[0, 1])
+    relay(xn, 1, 1)
+    arrived(yn, 0, own_recv.at[1, 0])
+    relay(yn, 0, 2)
+    for k in (0, 1):
+        arrived(diag, k, diag_recv.at[k])
+        relay(diag, k, 3)
+    for k in (0, 1):
+        for i, device in enumerate((sib, flip(xn, 1), flip(yn, 1), flip(diag, 1))):
+            arrived(device, k, near_recv.at[i, k])
+    for i, whole in enumerate(wholes):
+        for k in range(zs - 1):
+            other = lax.rem(z + zs - 1 - k, zs)
+            push(whole.at[other], whole.at[other], z_send.at[i, k], z_recv.at[i, k], (me, other)).wait_recv()
+    for copy in locals_:
+        copy.wait()
+    for copy in started:
+        copy.wait_send()
+
+
+def gather(tokens, shards, ctx_count, z_count):
+    outs = [jax.ShapeDtypeStruct((ctx_count,) + tokens.shape, tokens.dtype)]
+    outs += [jax.ShapeDtypeStruct((z_count,) + shard.shape, shard.dtype) for shard in shards]
+    dma = pltpu.SemaphoreType.DMA
+    return pl.pallas_call(
+        functools.partial(gather_body, z_count),
+        out_shape=outs,
+        in_specs=[ANY] * (1 + len(shards)),
+        out_specs=[ANY] * (1 + len(shards)),
+        scratch_shapes=[
+            dma((1 + len(shards),)), dma((len(shards), z_count - 1)), dma((len(shards), z_count - 1)), dma((3, 2)), dma((4, 2)),
+            dma((2, 2)), dma((2,)), dma((4, 2)),
+        ],
+        compiler_params=pltpu.CompilerParams(collective_id=1, has_side_effects=True),
+        name="gather_tokens",
+    )(tokens, *shards)
+
+
+def norm_parts(hidden):
+    center = hidden - jnp.mean(hidden, axis=-1, keepdims=True)
+    inv_dev = lax.rsqrt(jnp.mean(center * center, axis=-1, keepdims=True) + epsilon)
+    return center * inv_dev, inv_dev
+
+
+def small_rows(pack_ref):
+    return jnp.concatenate([pack_ref[z] for z in range(pack_ref.shape[0])], axis=1)
+
+
+def mix_body(experts, groups, att_ref, tok_ref, cot_ref, wo_ref, pack_ref, gid_ref, hidden_ref, normed_ref, mix_ref, attended_ref, send_ref):
+    heads = att_ref.shape[0]
+    halves = [jnp.concatenate([att_ref[h, :, HEAD * p:HEAD * (p + 1)] for h in range(heads)], axis=1) for p in range(2)]
+    attended = jnp.concatenate(halves, axis=0)
+    attended_ref[...] = attended
+    width = tok_ref.shape[1]
+    hidden = tok_ref[...].astype(jnp.float32) + dot_nn(attended, wo_ref[...].reshape(width, width))
+    hidden_ref[...] = hidden
+    unit, inv_dev = norm_parts(hidden)
+    small = small_rows(pack_ref)
+    gain, bias = small[experts:experts + 1].astype(jnp.float32), small[experts + 1:experts + 2].astype(jnp.float32)
+    normed = (unit * gain + bias).astype(jnp.bfloat16)
+    normed_ref[...] = normed
+    expo = jnp.exp(dot_nt(small, normed)[:experts])
+    rows = tok_ref.shape[0]
+    expo = jnp.broadcast_to(expo[:, None, :], (experts, groups, rows)).reshape(experts * groups, rows)
+    member = lax.rem(lax.broadcasted_iota(jnp.int32, (experts * groups, 1), 0), groups) == lax.rem(gid_ref[...], groups)
+    expo = jnp.where(member, expo, 0.0)
+    mix = expo / jnp.sum(expo, axis=1, keepdims=True)
+    mix_ref[...] = mix
+    low = mix.astype(jnp.bfloat16)
+    owners = send_ref.shape[0]
+    per = experts * groups // owners
+    send_ref[:, 0] = dot_nn(low, normed).astype(jnp.bfloat16).reshape(owners, per, width)
+    send_ref[:, 1] = dot_nn(low, cot_ref[...]).astype(jnp.bfloat16).reshape(owners, per, width)
+
+
+def mix_tokens(att, tokens, cot, w_out, pack, gid_row, experts, groups, owners):
+    rows, width = tokens.shape
+    return pl.pallas_call(
+        functools.partial(mix_body, experts, groups),
+        out_shape=(
+            jax.ShapeDtypeStruct((rows, width), jnp.float32),
+            jax.ShapeDtypeStruct((rows, width), jnp.bfloat16),
+            jax.ShapeDtypeStruct((experts * groups, rows), jnp.float32),
+            jax.ShapeDtypeStruct((rows, width), jnp.bfloat16),
+            jax.ShapeDtypeStruct((owners, 2, experts * groups // owners, width), jnp.bfloat16),
+        ),
+        in_specs=[VMEM] * 6,
+        out_specs=(VMEM,) * 5,
+        compiler_params=pltpu.CompilerParams(vmem_limit_bytes=LIMIT),
+        name="mix_tokens",
+    )(att, tokens, cot, w_out, pack, gid_row)
+
+
+def expert_body(groups, got_ref, up_ref, down_ref, back_ref, out_acc, grad_acc):
+    own, part = pl.program_id(0), pl.program_id(1)
+    at = pl.ds(pl.multiple_of(own * groups, groups), groups)
+    sources, width = got_ref.shape[0], got_ref.shape[3]
+    mixed = got_ref[:, 0, at, :].reshape(sources * groups, width)
+    grad_out = got_ref[:, 1, at, :].reshape(sources * groups, width)
+    up, down = up_ref[0], down_ref[0]
+    pre = dot_nn(mixed, up)
+    active = jax.nn.gelu(pre, approximate=True).astype(jnp.bfloat16)
+    grad_pre = (dot_nt(grad_out, down) * gelu_slope(pre)).astype(jnp.bfloat16)
+    out, grad = dot_nn(active, down), dot_nt(grad_pre, up)
+
+    @pl.when(part == 0)
+    def _():
+        out_acc[...] = out
+        grad_acc[...] = grad
+
+    @pl.when(part != 0)
+    def _():
+        out_acc[...] += out
+        grad_acc[...] += grad
+
+    @pl.when(part == pl.num_programs(1) - 1)
+    def _():
+        back_ref[:, 0, at, :] = out_acc[...].astype(jnp.bfloat16).reshape(sources, groups, width)
+        back_ref[:, 1, at, :] = grad_acc[...].astype(jnp.bfloat16).reshape(sources, groups, width)
+
+
+def run_experts(got, w_up, w_down, groups):
+    own, width, ffn = w_up.shape
+    step = 1024
+    rows = got.shape[0] * groups
+    return pl.pallas_call(
+        functools.partial(expert_body, groups),
+        grid=(own, ffn // step),
+        out_shape=jax.ShapeDtypeStruct(got.shape, jnp.bfloat16),
+        in_specs=[
+            pl.BlockSpec(got.shape, lambda e, f: (0, 0, 0, 0)),
+            pl.BlockSpec((1, width, step), lambda e, f: (e, 0, f)),
+            pl.BlockSpec((1, step, width), lambda e, f: (e, f, 0)),
+        ],
+        out_specs=pl.BlockSpec(got.shape, lambda e, f: (0, 0, 0, 0)),
+        scratch_shapes=[pltpu.VMEM((rows, width), jnp.float32)] * 2,
+        compiler_params=pltpu.CompilerParams(vmem_limit_bytes=LIMIT),
+        name="experts",
+    )(got, w_up, w_down)
+
+
+def expert_grad_body(mixed_ref, grad_ref, up_ref, down_ref, gup_ref, gdown_ref):
+    width = up_ref.shape[1]
+    mixed, grad_out = mixed_ref[...].reshape(-1, width), grad_ref[...].reshape(-1, width)
+    pre = dot_nn(mixed, up_ref[0])
+    active = jax.nn.gelu(pre, approximate=True).astype(jnp.bfloat16)
+    grad_pre = (dot_nt(grad_out, down_ref[0]) * gelu_slope(pre)).astype(jnp.bfloat16)
+    gup_ref[0] = dot_tn(mixed, grad_pre)
+    gdown_ref[0] = dot_tn(active, grad_out)
+
+
+def expert_grads(gathered, w_up, w_down, groups):
+    own, width, ffn = w_up.shape
+    step = 512
+    sources = gathered.shape[0]
+    view = gathered.reshape(sources, 2, own, groups, width)
+    return pl.pallas_call(
+        expert_grad_body,
+        grid=(own, ffn // step),
+        out_shape=(jax.ShapeDtypeStruct(w_up.shape, jnp.float32), jax.ShapeDtypeStruct(w_down.shape, jnp.float32)),
+        in_specs=[
+            pl.BlockSpec((sources, 1, 1, groups, width), lambda e, f: (0, 0, e, 0, 0)),
+            pl.BlockSpec((sources, 1, 1, groups, width), lambda e, f: (0, 1, e, 0, 0)),
+            pl.BlockSpec((1, width, step), lambda e, f: (e, 0, f)),
+            pl.BlockSpec((1, step, width), lambda e, f: (e, f, 0)),
+        ],
+        out_specs=(pl.BlockSpec((1, width, step), lambda e, f: (e, 0, f)), pl.BlockSpec((1, step, width), lambda e, f: (e, f, 0))),
+        compiler_params=pltpu.CompilerParams(vmem_limit_bytes=LIMIT),
+        name="expert_grads",
+    )(view, view, w_up, w_down)
+
+
+def unmix_body(experts, groups, heads, hidden_ref, normed_ref, mix_ref, attended_ref, cot_ref, wo_ref, pack_ref, back_ref,
+               layer_ref, ghidden_ref, gout_ref, small_ref, ghead_ref):
+    rows, width = hidden_ref.shape
+    hidden, normed, mix, cot = hidden_ref[...], normed_ref[...], mix_ref[...], cot_ref[...]
+    low = mix.astype(jnp.bfloat16)
+    flat = experts * groups
+    expert_out, grad_mixed = back_ref[:, 0].reshape(flat, width), back_ref[:, 1].reshape(flat, width)
+    layer_ref[...] = hidden + dot_tn(low, expert_out)
+    product = mix * (dot_nt(expert_out, cot) + dot_nt(grad_mixed, normed))
+    grad_logits = product - mix * jnp.sum(product, axis=1, keepdims=True)
+    grad_logits = jnp.sum(grad_logits.reshape(experts, groups, rows), axis=1).astype(jnp.bfloat16)
+    small = small_rows(pack_ref)
+    pad = jnp.zeros((small.shape[0] - experts, rows), jnp.bfloat16)
+    grad_logits = jnp.concatenate([grad_logits, pad], axis=0)
+    grad_normed = dot_tn(jnp.concatenate([low, grad_logits], axis=0), jnp.concatenate([grad_mixed, small], axis=0))
+    gain = small[experts:experts + 1].astype(jnp.float32)
+    unit, inv_dev = norm_parts(hidden)
+    small_ref[...] = dot_nn(grad_logits, normed)
+    small_ref[experts:experts + 1] = jnp.sum(grad_normed * unit, axis=0, keepdims=True)
+    small_ref[experts + 1:experts + 2] = jnp.sum(grad_normed, axis=0, keepdims=True)
+    scaled = grad_normed * gain
+    mean = jnp.mean(scaled, axis=-1, keepdims=True)
+    grad_hidden = cot.astype(jnp.float32) + inv_dev * (scaled - mean - unit * jnp.mean(scaled * unit, axis=-1, keepdims=True))
+    ghidden_ref[...] = grad_hidden
+    branch = grad_hidden.astype(jnp.bfloat16)
+    gout_ref[...] = dot_tn(attended_ref[...], branch)
+    grad_heads = dot_nt(branch, wo_ref[...].reshape(width, width)).astype(jnp.bfloat16)
+    half = rows // 2
+    for h in range(heads):
+        at = slice(HEAD * h, HEAD * (h + 1))
+        ghead_ref[h] = jnp.concatenate([grad_heads[:half, at], grad_heads[half:, at]], axis=1)
+
+
+def unmix_tokens(hidden, normed, mix, attended, cot, w_out, pack, back, experts, groups, heads):
+    rows, width = hidden.shape
+    return pl.pallas_call(
+        functools.partial(unmix_body, experts, groups, heads),
+        out_shape=(
+            jax.ShapeDtypeStruct((rows, width), jnp.float32),
+            jax.ShapeDtypeStruct((rows, width), jnp.float32),
+            jax.ShapeDtypeStruct((width, width), jnp.float32),
+            jax.ShapeDtypeStruct((pack.shape[1], width), jnp.float32),
+            jax.ShapeDtypeStruct((heads, rows // 2, 2 * HEAD), jnp.bfloat16),
+        ),
+        in_specs=[VMEM] * 8,
+        out_specs=(VMEM,) * 5,
+        compiler_params=pltpu.CompilerParams(vmem_limit_bytes=LIMIT),
+        name="unmix_tokens",
+    )(hidden, normed, mix, attended, cot, w_out, pack, back)
+
+
+def head_weight_body(z_count, toks_ref, grad_ref, out_ref, acc_ref):
+    step = pl.program_id(0)
+    half = grad_ref.shape[1]
+    total = None
+    for p in range(2):
+        columns = [grad_ref[0, :, HEAD * (2 * kind + p):HEAD * (2 * kind + p + 1)] for kind in range(3)]
+        part = dot_tn(jnp.concatenate(columns, axis=1), toks_ref[0, p * half:(p + 1) * half, :])
+        total = part if total is None else total + part
+
+    @pl.when(step == 0)
+    def _():
+        acc_ref[...] = total
+
+    @pl.when(step != 0)
+    def _():
+        acc_ref[...] += total
+
+    @pl.when(step == pl.num_programs(0) - 1)
+    def _():
+        out_ref[...] = acc_ref[...].T
+
+
+def head_weight(tokens_all, grad, z_count):
+    count, rows, width = tokens_all.shape
+    return pl.pallas_call(
+        functools.partial(head_weight_body, z_count),
+        grid=(count,),
+        out_shape=jax.ShapeDtypeStruct((width, 3 * HEAD), jnp.float32),
+        in_specs=[
+            pl.BlockSpec((1, rows, width), lambda i: (i, 0, 0)),
+            pl.BlockSpec((1,) + grad.shape[1:], lambda i: (i, 0, 0)),
+        ],
+        out_specs=pl.BlockSpec((width, 3 * HEAD), lambda i: (0, 0)),
+        scratch_shapes=[pltpu.VMEM((3 * HEAD, width), jnp.float32)],
+        compiler_params=pltpu.CompilerParams(vmem_limit_bytes=LIMIT),
+        name="head_weight",
+    )(tokens_all, grad)
+
+
+def token_grad_body(grad_ref, weight_ref, ghidden_ref, out_ref):
+    heads, half = grad_ref.shape[0], grad_ref.shape[1]
+    for p in range(2):
+        columns = [grad_ref[h, :, HEAD * (2 * kind + p):HEAD * (2 * kind + p + 1)] for kind in range(3) for h in range(heads)]
+        at = slice(p * half, (p + 1) * half)
+        out_ref[at, :] = ghidden_ref[at, :] + dot_nt(jnp.concatenate(columns, axis=1), weight_ref[...])
+
+
+def token_grad(grad, weight, ghidden):
+    return pl.pallas_call(
+        token_grad_body,
+        out_shape=jax.ShapeDtypeStruct(ghidden.shape, jnp.float32),
+        in_specs=[VMEM] * 3,
+        out_specs=VMEM,
+        compiler_params=pltpu.CompilerParams(vmem_limit_bytes=LIMIT),
+        name="token_grad",
+    )(grad, weight, ghidden)
+
+
+def fast_device(
+    tokens, cotangent, block_table, seg_ids, group_ids, w_qkv, w_out, w_router, ln_gain, ln_bias, w_up, w_down
+):
+    ctx_count, z_count = lax.axis_size("ctx"), lax.axis_size("fsdp")
+    ctx_index, z_index = lax.axis_index("ctx"), lax.axis_index("fsdp")
+    tok_rows, cot_rows = tokens[0], cotangent[0]
+    rows, width = tok_rows.shape
+    experts = w_router.shape[1]
+    groups = rows // GROUP_SIZE
+    shard = w_qkv.shape[0]
+    segs = seg_ids[0].reshape(block_table.shape[0], -1)
+    head_cols = lax.dynamic_slice_in_dim(w_qkv.reshape(shard, 3, ctx_count, HEAD), ctx_index, 1, 2).reshape(shard, 3 * HEAD)
+    pack = jnp.concatenate(
+        [w_router.T, ln_gain[None], ln_bias[None], jnp.zeros((16 - experts - 2, shard), jnp.bfloat16)], axis=0
+    )
+    tokens_all, head_weights, out_full, pack_full = gather(tok_rows, [head_cols, w_out, pack], ctx_count, z_count)
+    qkv_full = lax.all_gather(w_qkv, "fsdp", axis=0, tiled=True)
+    att, *saved = attn_fwd(tokens_all.reshape(ctx_count * rows, width), head_weights, block_table, segs)
+    att = exchange(att, "ctx", 2, "exchange_attended")
+    hidden, normed, mix, attended, mixed = mix_tokens(
+        att, tok_rows, cot_rows, out_full, pack_full, group_ids, experts, groups, z_count
+    )
+    got = exchange(mixed, "fsdp", 3, "exchange_mixed")
+    back = exchange(run_experts(got, w_up, w_down, groups), "fsdp", 4, "exchange_back")
+    gathered = lax.all_gather(got, "ctx", axis=0, tiled=True)
+    layer_out, grad_hidden, gout_part, small_part, grad_heads = unmix_tokens(
+        hidden, normed, mix, attended, cot_rows, out_full, pack_full, back, experts, groups, ctx_count
+    )
+    grad_heads = exchange(grad_heads, "ctx", 5, "exchange_grad")
+    grad_out = lax.psum(lax.psum_scatter(gout_part, "fsdp", scatter_dimension=0, tiled=True), "ctx")
+    small = lax.psum(small_part, ("ctx", "fsdp"))
+    grad_qkv_all = attn_bwd(grad_heads, saved, block_table, segs)
+    grad_rows = exchange(grad_qkv_all, "ctx", 6, "exchange_qkv")
+    grad_up, grad_down = expert_grads(gathered, w_up, w_down, groups)
+    own_cols = head_weight(tokens_all, grad_qkv_all, z_count)
+    own_cols = lax.psum_scatter(own_cols, "fsdp", scatter_dimension=0, tiled=True)
+    cols = lax.all_gather(own_cols.reshape(shard, 3, 1, HEAD), "ctx", axis=2, tiled=True)
+    grad_tokens = token_grad(grad_rows, qkv_full, grad_hidden)
+    mine = lax.dynamic_slice_in_dim(small, z_index * shard, shard, 1)
+    return (
+        layer_out[None],
+        grad_tokens[None],
+        cols.reshape(shard, 3 * width),
+        grad_out,
+        mine[:experts].T,
+        mine[experts],
+        mine[experts + 1],
+        grad_up,
+        grad_down,
+    )
+
+
 def solution(mesh):
     placed = (
         P("fsdp", "ctx", None),
@@ -302,8 +974,9 @@
         P("fsdp", None, None),
         P("fsdp", None, None),
     )
+    step = fast_device if mesh.shape["ctx"] == HEADS else on_device
     return jax.shard_map(
-        on_device,
+        step,
         mesh=mesh,
         in_specs=placed,
         out_specs=(

time: 1320 us -> 363 us (0.28); the launches traced: 1290 us -> 361 us
  waiting for transfers between devices: 481 us -> 75.2 us
  local copies, waits for them, and re-layouts: 401 us -> 8.18 us
  matrix products: 233 us -> 0 us
  Pallas kernels: 0 us -> 209 us
  other arithmetic: 59.7 us -> 2.78 us
  loops' own time: 20 us -> 0 us
  blocking collectives: 68.7 us -> 52.7 us
  starting transfers between devices: 14.9 us -> 0.19 us
    dynamic_update_slice x8 -> x0, local copies, waits for them, and re-layouts: 317 us -> none  [on_device(): lax.scan(grad_step, jnp.zeros((tok_count, HEADS, HEAD), jnp.float32), blo...]
    dot_general x39 -> x0, matrix products: 233 us -> none  [the longest x4 61.4 us: block_scores(): jnp.einsum('qhd,khd->hqk', query_heads, key_block, preferred_element_type...]
    pallas_call x0 -> x14, Pallas kernels: none -> 209 us  [the longest x5 56.9 us: exchange(): pl.pallas_call(functools.partial(exchange_body, axis, count), out_shape=j...]
    reduce_scatter x5 -> x2, waiting for transfers between devices: 206 us -> 0.02 us  [the longest x1 0.02 us: fast_device(): lax.psum_scatter(gout_part, 'fsdp', scatter_dimension=0, tiled=True)]
    psum x1, waiting for transfers between devices: 217 us -> 38.7 us  [fast_device(): lax.psum(lax.psum_scatter(gout_part, 'fsdp', scatter_dimension=0, tiled=T...]
    unnamed x129 -> x6, local copies, waits for them, and re-layouts: 57.7 us -> 4.55 us
    all_gather x4 -> x1, blocking collectives: 45.3 us -> 11.4 us  [fast_device(): lax.all_gather(own_cols.reshape(shard, 3, 1, HEAD), 'ctx', axis=2, tiled=...]
    reduce_sum x3 -> x0, other arithmetic: 30.1 us -> none  [the longest x2 29.9 us: lse_step(): jnp.sum(weights, axis=-1)]
  transfers between devices with their start and end apart: 13 -> 5, of which waited for: 11 -> 3; matrix products, arithmetic and copies ran while one was open for 11% -> 1% of each run, Pallas kernels for 0% -> 12%
where the time goes in v1:
time: 363 us; the launch traced here: 361 us
  Pallas kernels  209 us (58%)
  waiting for transfers between devices  75.2 us (21%)
  blocking collectives  52.7 us (15%)
  between operations  13.9 us (4%)
  local copies, waits for them, and re-layouts  8.18 us (2%)
    pallas_call x5, Pallas kernels, exchange(): pl.pallas_call(functools.partial(exchange_body, axis, count), out_shape=j...  56.9 us
    pallas_call x1, Pallas kernels, attn_bwd(): pl.pallas_call(functools.partial(bwd_body, blocks, block_len), out_shape=...  42.5 us
    psum x1, blocking collectives, fast_device(): small = lax.psum(small_part, ('ctx', 'fsdp'))  41.3 us
    psum x1, waiting for transfers between devices, fast_device(): lax.psum(lax.psum_scatter(gout_part, 'fsdp', scatter_dimension=0, tiled=T...  38.7 us
    pallas_call x1, Pallas kernels, attn_fwd(): pl.pallas_call(functools.partial(fwd_body, blocks, block_len), out_shape=...  34.3 us
    pallas_call x1, Pallas kernels, gather(): pl.pallas_call(functools.partial(gather_body, z_count), out_shape=outs, i...  28.6 us
    all_gather x1, waiting for transfers between devices, fast_device(): gathered = lax.all_gather(got, 'ctx', axis=0, tiled=True)  24.5 us
    pallas_call x1, Pallas kernels, expert_grads(): pl.pallas_call(expert_grad_body, grid=(own, ffn // step), out_shape=(jax....  18 us
  transfers between devices with their start and end apart: 5, of which 3 were waited for; matrix products, arithmetic and copies ran while one was open for 1% of the time, Pallas kernels for 12%

profile of v1, /device:TPU:0, one launch (start us, length us, event | category | flops | bytes accessed | tf_op | source)
XLA Modules:
  0.0 361.5 jit_solution(13213696936167327066)
XLA Ops:
  7.2 0.0 reduce-scatter.3.cloned.1.call-start
  7.2 1.2 copy.27
  8.5 0.7 copy.28.refs_0_
  9.2 0.5 broadcast.5
  9.7 1.4 reduce.3
  11.1 0.6 reshape_squeeze.3.seg_ref.segrow_ref
  11.7 0.1 pad.3.clone
  11.8 1.4 maximum_maximum_fusion.refs_2_
  13.2 28.6 %gather_tokens.1 = (bf16[8,512,512]{2,1,0:T(8,128)(2,1)}, bf16[4,128,192]{2,1,0:T(8,128)(2,1)}, bf16[4,128,512]{2,1,0:T(8,128)(2,1)}, bf16[4,16,128]{2,1,0:T(8,128)(2,1)}) custom-call(bf16[512,512]{1,0:T(8,128)(2,1)} %bitcast.25, bf16[128,192]{1,0:T(8,128)(2,1)} %copy.28.refs_0_, bf16[128,512]{1,0:T(8,128)(2,1)} %refs_1_.1, ...), custom_call_target="tpu_custom_call" | custom-call | tf_op jit(solution)/shard_map/gather_tokens/pallas_call | solution.py:653
  41.8 34.3 %attention.1 = (bf16[8,256,128]{2,1,0:T(8,128)(2,1)}, bf16[4096,256]{1,0:T(8,128)(2,1)}, bf16[4096,256]{1,0:T(8,128)(2,1)}, bf16[4096,128]{1,0:T(8,128)(2,1)}, b...) custom-call(s32[16]{0:T(128)} %table_ref.3, s32[16,256]{1,0:T(8,128)} %reshape_squeeze.3.seg_ref.segrow_ref, ...), custom_call_target="tpu_custom_call" | custom-call | tf_op jit(solution)/shard_map/attention/pallas_call | solution.py:414
  76.1 9.2 %exchange_attended.1.att_ref = bf16[8,256,128]{2,1,0:T(8,128)(2,1)} custom-call(bf16[8,256,128]{2,1,0:T(8,128)(2,1)} %get-tuple-element.33.x_ref), custom_call_target="tpu_custom_call" | custom-call | tf_op jit(solution)/shard_map/exchange_attended/pallas_call | solution.py:570
  85.3 3.5 mix_tokens.1
  88.8 9.1 %exchange_mixed.1.got_ref = bf16[4,2,32,512]{3,2,1,0:T(8,128)(2,1)} custom-call(bf16[4,2,32,512]{3,2,1,0:T(8,128)(2,1)} %get-tuple-element.40.x_ref), custom_call_target="tpu_custom_call" | custom-call | tf_op jit(solution)/shard_map/exchange_mixed/pallas_call | solution.py:570
  97.9 7.5 %experts.1.x_ref = bf16[4,2,32,512]{3,2,1,0:T(8,128)(2,1)} custom-call(bf16[4,2,32,512]{3,2,1,0:T(8,128)(2,1)} %exchange_mixed.1.got_ref, bf16[2,512,2048]{2,1,0:T(8,128)(2,1)} %up_ref.3, bf16[2,2048,512]{2,1,0:T(8,128)(2,1)} %down_ref.3), custom_call_target="tpu_custom_call" | custom-call | tf_op jit(solution)/shard_map/experts/pallas_call | solution.py:754
  105.4 9.0 %exchange_back.1.back_ref = bf16[4,2,32,512]{3,2,1,0:T(8,128)(2,1)} custom-call(bf16[4,2,32,512]{3,2,1,0:T(8,128)(2,1)} %experts.1.x_ref), custom_call_target="tpu_custom_call" | custom-call | tf_op jit(solution)/shard_map/exchange_back/pallas_call | solution.py:570
  114.4 5.4 %unmix_tokens.1 = (f32[512,512]{1,0:T(8,128)}, f32[512,512]{1,0:T(8,128)}, f32[512,512]{1,0:T(8,128)}, f32[16,512]{1,0:T(8,128)}, bf16[8,256,128]{2,1,0:T(8,128)(2,1)}) custom-call(f32[512,512]{1,0:T(8,128)} %get-tuple-element.36.hidden_ref, bf16[512,512]{1,0:T(8,128)(2,1)} %get-tuple-element.37.normed_ref, f32[128,512]{1,0:T(8,128)} %get-tuple-element.38.mix_ref, ...), custom_call_target="tpu_custom_call" | custom-call | tf_op jit(solution)/shard_map/unmix_tokens/pallas_call | solution.py:836
  119.8 9.1 %exchange_grad.1.do_ref = bf16[8,256,128]{2,1,0:T(8,128)(2,1)} custom-call(bf16[8,256,128]{2,1,0:T(8,128)(2,1)} %get-tuple-element.42.x_ref), custom_call_target="tpu_custom_call" | custom-call | tf_op jit(solution)/shard_map/exchange_grad/pallas_call | solution.py:570
  128.9 42.5 %attention_grad.1.x_ref.grad_ref = bf16[8,256,384]{2,1,0:T(8,128)(2,1)} custom-call(s32[16]{0:T(128)} %table_ref.3, s32[16,256]{1,0:T(8,128)} %reshape_squeeze.3.seg_ref.segrow_ref, bf16[8,256,128]{2,1,0:T(8,128)(2,1)} %exchange_grad.1.do_ref, bf16[4096,256]{1,0:T(8,128)(2,1)} %get-tuple-element.43.qf_ref, bf16[4096,256]{1,0:T(8,128)(2,1)} %get-tuple-element.44.kf_ref, ...), custom_call_target="tpu_custom_call" | custom-call | tf_op jit(solution)/shard_map/attention_grad/pallas_call | solution.py:515
  171.5 7.6 %head_weight.1 = f32[512,192]{1,0:T(8,128)} custom-call(bf16[8,512,512]{2,1,0:T(8,128)(2,1)} %get-tuple-element.31.toks_ref, bf16[8,256,384]{2,1,0:T(8,128)(2,1)} %attention_grad.1.x_ref.grad_ref), custom_call_target="tpu_custom_call" | custom-call | tf_op jit(solution)/shard_map/head_weight/pallas_call | solution.py:876
  179.1 0.0 reduce-scatter.3.cloned.1.call-update
  179.1 0.0 reduce-scatter.5.cloned.1.call-start
  179.1 0.7 reduce-scatter.5.cloned.1.call-update
  179.8 0.0 copy-start
  179.9 0.0 all-gather.3.cloned.1.call-start
  179.9 0.7 all-gather.3.cloned.1.call-update
  180.6 0.0 all-gather.5.cloned.1.call-start
  180.6 0.5 all-gather.5.cloned.1.call-update
  181.2 0.0 all-reduce.2.cloned.1.call-start
  181.2 20.6 %exchange_qkv.1.grad_ref = bf16[8,256,384]{2,1,0:T(8,128)(2,1)} custom-call(bf16[8,256,384]{2,1,0:T(8,128)(2,1)} %attention_grad.1.x_ref.grad_ref), custom_call_target="tpu_custom_call" | custom-call | tf_op jit(solution)/shard_map/exchange_qkv/pallas_call | solution.py:570
  201.8 0.0 copy-done
  201.8 41.3 %psum.15 = f32[16,512]{1,0:T(8,128)S(1)} all-reduce(f32[16,512]{1,0:T(8,128)S(1)} %copy-done), channel_id=1, replica_groups=mesh['ctx'=8,'fsdp'=4] {'ctx','fsdp'}, use_global_device_ids=true, to_apply=%region_3.0 | all-reduce | flops 8192 | bytes 65536 | tf_op jit(solution)/shard_map/psum | solution.py:940
  243.1 0.6 dynamic-slice_bitcast_fusion.1
  243.7 0.6 dynamic-slice_bitcast_fusion
  244.3 0.0 reduce-scatter.3.cloned.1.call-done
  244.3 1.0 copy.29
  245.3 0.0 reduce-scatter.5.cloned.1.call-done
  245.3 0.0 all-reduce.2.cloned.1.call-update
  245.3 11.4 %all_gather.10 = f32[128,3,8,64]{0,3,2,1:T(8,128)S(1)} all-gather(f32[128,3,1,64]{0,3,2,1:T(8,128)S(1)} %bitcast.29), channel_id=1, replica_groups=mesh['ctx'=8,'fsdp'=4] {'ctx'}, dimensions={2}, use_global_device_ids=true | all-gather | bytes 884736 | tf_op jit(solution)/shard_map/all_gather | solution.py:946
  256.7 1.1 copy.30
  257.9 9.9 %all-gather.3.cloned.1.call-done.weight_ref = bf16[512,1536]{1,0:T(8,128)(2,1)} async-done(((bf16[128,1536]{1,0:T(8,128)(2,1)}), bf16[512,1536]{1,0:T(8,128)(2,1)}) %all-gather.3.cloned.1.call-update) | async-done | bytes 1572880 | tf_op jit(solution)/shard_map/all_gather | solution.py:926
  267.8 4.2 %token_grad.1 = f32[512,512]{1,0:T(8,128)} custom-call(bf16[8,256,384]{2,1,0:T(8,128)(2,1)} %exchange_qkv.1.grad_ref, bf16[512,1536]{1,0:T(8,128)(2,1)} %all-gather.3.cloned.1.call-done.weight_ref, f32[512,512]{1,0:T(8,128)} %get-tuple-element.48.ghidden_ref), custom_call_target="tpu_custom_call" | custom-call | tf_op jit(solution)/shard_map/token_grad/pallas_call | solution.py:900
  272.0 24.5 %all-gather.5.cloned.1.call-done = bf16[32,2,32,512]{3,2,1,0:T(8,128)(2,1)} async-done(((bf16[4,2,32,512]{3,2,1,0:T(8,128)(2,1)}), bf16[32,2,32,512]{3,2,1,0:T(8,128)(2,1)}) %all-gather.5.cloned.1.call-update) | async-done | bytes 2097168 | tf_op jit(solution)/shard_map/all_gather | solution.py:934
  296.5 18.0 %expert_grads.1 = (f32[2,512,2048]{2,1,0:T(8,128)}, f32[2,2048,512]{2,1,0:T(8,128)}) custom-call(bf16[32,2,2,16,512]{4,3,2,1,0:T(8,128)(2,1)} %bitcast.20, bf16[32,2,2,16,512]{4,3,2,1,0:T(8,128)(2,1)} %bitcast.21, bf16[2,512,2048]{2,1,0:T(8,128)(2,1)} %up_ref.3, bf16[2,2048,512]{2,1,0:T(8,128)(2,1)} %down_ref.3), custom_call_target="tpu_custom_call" | custom-call | tf_op jit(solution)/shard_map/expert_grads/pallas_call | solution.py:785
  314.5 38.7 %all-reduce.2.cloned.1.call-done = f32[128,512]{1,0:T(8,128)} async-done(((f32[128,512]{1,0:T(8,128)}), f32[128,512]{1,0:T(8,128)}) %all-reduce.2.cloned.1.call-update) | async-done | bytes 262160 | tf_op jit(solution)/shard_map/psum | solution.py:939
  353.3 1.7 copy.32
  (2 shorter events, 0.0 us)
Async XLA Ops:
  7.2 237.1 %reduce-scatter.3.cloned.1.call-start = ((), (), s32[]{:S(2)}) async-start(), calls=%async_computation.3 | async-start | bytes 655360 | tf_op jit(solution)/shard_map/reduce_scatter | solution.py:945
  179.1 66.2 %reduce-scatter.5.cloned.1.call-start = ((), (), s32[]{:S(2)}) async-start(), calls=%async_computation.4 | async-start | bytes 1310720 | tf_op jit(solution)/shard_map/reduce_scatter | solution.py:939
  179.8 21.9 %copy-start = (f32[16,512]{1,0:T(8,128)S(1)}, f32[16,512]{1,0:T(8,128)}, u32[]{:S(2)}) copy-start(f32[16,512]{1,0:T(8,128)} %get-tuple-element.50) | copy-start | bytes 98308
  179.9 88.0 %all-gather.3.cloned.1.call-start = ((), (), s32[]{:S(2)}) async-start(), calls=%async_computation.2 | async-start | bytes 1966080 | tf_op jit(solution)/shard_map/all_gather | solution.py:926
  180.6 115.9 %all-gather.5.cloned.1.call-start = ((), (), s32[]{:S(2)}) async-start(), calls=%async_computation.6 | async-start | bytes 2359296 | tf_op jit(solution)/shard_map/all_gather | solution.py:934
  181.2 172.1 %all-reduce.2.cloned.1.call-start = ((), (), s32[]{:S(2)}) async-start(), calls=%async_computation.5 | async-start | bytes 524288 | tf_op jit(solution)/shard_map/psum | solution.py:939
Sparse Core Ops, SparseCore 0:
  179.2 22.5 reduce-scatter.2
  204.1 26.1 reduce-scatter.4
  232.0 35.8 all-gather.2
  269.7 26.7 all-gather.4
  299.7 53.5 all-reduce.1

commit v2 on v1

--- a/solution.py
+++ b/solution.py
@@ -425,6 +425,7 @@
         out_specs=(VMEM,) * 6,
         scratch_shapes=[pltpu.SMEM((blocks,), jnp.int32), pltpu.SMEM((runs,), jnp.int32), pltpu.SMEM((runs,), jnp.int32)],
         compiler_params=pltpu.CompilerParams(vmem_limit_bytes=LIMIT),
+        cost_estimate=cost(35),
         name="attention",
     )(table, segs, tokens_all, weight, segs)
 
@@ -524,11 +525,16 @@
             pltpu.VMEM((SUPER, 2 * HEAD), jnp.float32),
         ],
         compiler_params=pltpu.CompilerParams(vmem_limit_bytes=LIMIT),
+        cost_estimate=cost(40),
         name="attention_grad",
     )(table, segs, grad, *saved)
 
 
 MESH = pl.DeviceIdType.MESH
+
+
+def cost(microseconds):
+    return pl.CostEstimate(flops=int(microseconds * 1.15e9), bytes_accessed=1 << 20, transcendentals=0)
 
 
 def flip(index, bit):
@@ -574,6 +580,7 @@
         out_specs=ANY,
         scratch_shapes=[pltpu.SemaphoreType.DMA, pltpu.SemaphoreType.DMA((count - 1,)), pltpu.SemaphoreType.DMA((count - 1,))],
         compiler_params=pltpu.CompilerParams(collective_id=collective_id, has_side_effects=True),
+        cost_estimate=cost(9),
         name=name,
     )(x)
 
@@ -660,6 +667,7 @@
             dma((2, 2)), dma((2,)), dma((4, 2)),
         ],
         compiler_params=pltpu.CompilerParams(collective_id=1, has_side_effects=True),
+        cost_estimate=cost(24),
         name="gather_tokens",
     )(tokens, *shards)
 
@@ -715,6 +723,7 @@
         in_specs=[VMEM] * 6,
         out_specs=(VMEM,) * 5,
         compiler_params=pltpu.CompilerParams(vmem_limit_bytes=LIMIT),
+        cost_estimate=cost(4),
         name="mix_tokens",
     )(att, tokens, cot, w_out, pack, gid_row)
 
@@ -763,43 +772,13 @@
         out_specs=pl.BlockSpec(got.shape, lambda e, f: (0, 0, 0, 0)),
         scratch_shapes=[pltpu.VMEM((rows, width), jnp.float32)] * 2,
         compiler_params=pltpu.CompilerParams(vmem_limit_bytes=LIMIT),
+        cost_estimate=cost(8),
         name="experts",
     )(got, w_up, w_down)
 
 
-def expert_grad_body(mixed_ref, grad_ref, up_ref, down_ref, gup_ref, gdown_ref):
-    width = up_ref.shape[1]
-    mixed, grad_out = mixed_ref[...].reshape(-1, width), grad_ref[...].reshape(-1, width)
-    pre = dot_nn(mixed, up_ref[0])
-    active = jax.nn.gelu(pre, approximate=True).astype(jnp.bfloat16)
-    grad_pre = (dot_nt(grad_out, down_ref[0]) * gelu_slope(pre)).astype(jnp.bfloat16)
-    gup_ref[0] = dot_tn(mixed, grad_pre)
-    gdown_ref[0] = dot_tn(active, grad_out)
-
-
-def expert_grads(gathered, w_up, w_down, groups):
-    own, width, ffn = w_up.shape
-    step = 512
-    sources = gathered.shape[0]
-    view = gathered.reshape(sources, 2, own, groups, width)
-    return pl.pallas_call(
-        expert_grad_body,
-        grid=(own, ffn // step),
-        out_shape=(jax.ShapeDtypeStruct(w_up.shape, jnp.float32), jax.ShapeDtypeStruct(w_down.shape, jnp.float32)),
-        in_specs=[
-            pl.BlockSpec((sources, 1, 1, groups, width), lambda e, f: (0, 0, e, 0, 0)),
-            pl.BlockSpec((sources, 1, 1, groups, width), lambda e, f: (0, 1, e, 0, 0)),
-            pl.BlockSpec((1, width, step), lambda e, f: (e, 0, f)),
-            pl.BlockSpec((1, step, width), lambda e, f: (e, f, 0)),
-        ],
-        out_specs=(pl.BlockSpec((1, width, step), lambda e, f: (e, 0, f)), pl.BlockSpec((1, step, width), lambda e, f: (e, f, 0))),
-        compiler_params=pltpu.CompilerParams(vmem_limit_bytes=LIMIT),
-        name="expert_grads",
-    )(view, view, w_up, w_down)
-
-
 def unmix_body(experts, groups, heads, hidden_ref, normed_ref, mix_ref, attended_ref, cot_ref, wo_ref, pack_ref, back_ref,
-               layer_ref, ghidden_ref, gout_ref, small_ref, ghead_ref):
+               layer_ref, ghidden_ref, rows_ref, ghead_ref):
     rows, width = hidden_ref.shape
     hidden, normed, mix, cot = hidden_ref[...], normed_ref[...], mix_ref[...], cot_ref[...]
     low = mix.astype(jnp.bfloat16)
@@ -815,15 +794,29 @@
     grad_normed = dot_tn(jnp.concatenate([low, grad_logits], axis=0), jnp.concatenate([grad_mixed, small], axis=0))
     gain = small[experts:experts + 1].astype(jnp.float32)
     unit, inv_dev = norm_parts(hidden)
-    small_ref[...] = dot_nn(grad_logits, normed)
-    small_ref[experts:experts + 1] = jnp.sum(grad_normed * unit, axis=0, keepdims=True)
-    small_ref[experts + 1:experts + 2] = jnp.sum(grad_normed, axis=0, keepdims=True)
+    small_grad = jnp.concatenate(
+        [
+            dot_nn(grad_logits, normed)[:experts],
+            jnp.sum(grad_normed * unit, axis=0, keepdims=True),
+            jnp.sum(grad_normed, axis=0, keepdims=True),
+            jnp.zeros((small.shape[0] - experts - 2, width), jnp.float32),
+        ],
+        axis=0,
+    )
     scaled = grad_normed * gain
     mean = jnp.mean(scaled, axis=-1, keepdims=True)
     grad_hidden = cot.astype(jnp.float32) + inv_dev * (scaled - mean - unit * jnp.mean(scaled * unit, axis=-1, keepdims=True))
     ghidden_ref[...] = grad_hidden
     branch = grad_hidden.astype(jnp.bfloat16)
-    gout_ref[...] = dot_tn(attended_ref[...], branch)
+    gout = dot_tn(attended_ref[...], branch)
+    owners, count = pack_ref.shape[0], rows_ref.shape[0]
+    own = width // (owners * count)
+    for c in range(count):
+        for z in range(owners):
+            low = (z * count + c) * own
+            rows_ref[c, z * own:(z + 1) * own, :] = gout[low:low + own]
+        rows_ref[c, owners * own:, :] = jnp.zeros((16, width), jnp.float32)
+        rows_ref[c, owners * own:owners * own + 2, :] = small_grad[2 * c:2 * c + 2]
     grad_heads = dot_nt(branch, wo_ref[...].reshape(width, width)).astype(jnp.bfloat16)
     half = rows // 2
     for h in range(heads):
@@ -838,80 +831,213 @@
         out_shape=(
             jax.ShapeDtypeStruct((rows, width), jnp.float32),
             jax.ShapeDtypeStruct((rows, width), jnp.float32),
-            jax.ShapeDtypeStruct((width, width), jnp.float32),
-            jax.ShapeDtypeStruct((pack.shape[1], width), jnp.float32),
+            jax.ShapeDtypeStruct((heads, width // heads + 16, width), jnp.float32),
             jax.ShapeDtypeStruct((heads, rows // 2, 2 * HEAD), jnp.bfloat16),
         ),
         in_specs=[VMEM] * 8,
-        out_specs=(VMEM,) * 5,
+        out_specs=(VMEM,) * 4,
         compiler_params=pltpu.CompilerParams(vmem_limit_bytes=LIMIT),
+        cost_estimate=cost(5),
         name="unmix_tokens",
     )(hidden, normed, mix, attended, cot, w_out, pack, back)
 
 
-def head_weight_body(z_count, toks_ref, grad_ref, out_ref, acc_ref):
-    step = pl.program_id(0)
-    half = grad_ref.shape[1]
+def head_columns(ref, p, index=None):
+    columns = []
+    for kind in range(3):
+        at = slice(HEAD * (2 * kind + p), HEAD * (2 * kind + p + 1))
+        columns.append(ref[index, :, at])
+    return jnp.concatenate(columns, axis=1)
+
+
+def closing_body(
+    owners, grads_ref, toks_ref, rows_ref, weight_ref, ghidden_ref, gathered_ref, up_ref, down_ref,
+    gtok_ref, gq_ref, gout_ref, small_ref, act_ref, gpre_ref,
+    held_grads, held_toks, held_rows, held_weight, held_hidden, held_mixed, held_up, held_down, act_buf, gpre_buf,
+    landing, zsend, zone, total_ref, all_ref,
+    load_sem, store_sem, a_send, a_recv, z_send, z_recv, c_send, c_recv,
+):
+    me, z = lax.axis_index("ctx"), lax.axis_index("fsdp")
+    count, half = grads_ref.shape[0], grads_ref.shape[1]
+    width = toks_ref.shape[2]
+    own_experts, ffn = up_ref.shape[0], up_ref.shape[2]
+    pairs = [
+        (grads_ref, held_grads), (toks_ref, held_toks), (rows_ref, held_rows), (gathered_ref, held_mixed), (up_ref, held_up),
+        (down_ref, held_down), (weight_ref, held_weight), (ghidden_ref, held_hidden),
+    ]
+    loads = [pltpu.make_async_copy(src, dst, load_sem.at[i]) for i, (src, dst) in enumerate(pairs)]
+    for copy in loads:
+        copy.start()
+    z_peers = [(me, lax.rem(z + k, owners)) for k in range(1, owners)]
+    c_peers = [(jnp.bitwise_xor(me, k), z) for k in range(1, count)]
+    meet(z_peers + c_peers)
+    swaps = []
+    for k, device in enumerate(c_peers):
+        swaps.append(push(grads_ref.at[device[0]], landing.at[me], a_send.at[k], a_recv.at[k], device))
+        swaps[-1].start()
+    own_swap = pltpu.make_async_copy(grads_ref.at[me], landing.at[me], store_sem.at[0])
+    own_swap.start()
+
+    loads[0].wait()
+    loads[1].wait()
     total = None
+    for device in range(count):
+        for p in range(2):
+            part = dot_tn(head_columns(held_grads, p, device), held_toks[device, p * half:(p + 1) * half, :])
+            total = part if total is None else total + part
+    loads[2].wait()
+    lanes = width // owners
+    small = held_rows.shape[0] - 16
+    own = small // owners
+    for c in range(owners):
+        at = slice(c * lanes, (c + 1) * lanes)
+        zsend[c, :3 * HEAD, :] = total[:, at].astype(jnp.bfloat16)
+        zsend[c, 3 * HEAD:3 * HEAD + 16, :] = held_rows[small:, at].astype(jnp.bfloat16)
+        for j in range(width // lanes):
+            low = 3 * HEAD + 16 + own * j
+            zsend[c, low:low + own, :] = held_rows[own * c:own * (c + 1), lanes * j:lanes * (j + 1)].astype(jnp.bfloat16)
+    z_copies = []
+    for k, device in enumerate(z_peers):
+        z_copies.append(push(zsend.at[device[1]], zone.at[z], z_send.at[k], z_recv.at[k], device))
+        z_copies[-1].start()
+    zone[z] = zsend[z]
+    for i in (3, 4, 5):
+        loads[i].wait()
+
+    step = 512
+
+    def expert_part(own_expert):
+        mixed = held_mixed[:, 0, own_expert].reshape(-1, width)
+        grad_out = held_mixed[:, 1, own_expert].reshape(-1, width)
+
+        def chunk(i, carry):
+            at = pl.ds(pl.multiple_of(i * step, step), step)
+            pre = dot_nn(mixed, held_up[own_expert, :, at])
+            act_buf[own_expert, :, at] = jax.nn.gelu(pre, approximate=True).astype(jnp.bfloat16)
+            slope = dot_nt(grad_out, held_down[own_expert, at, :])
+            gpre_buf[own_expert, :, at] = (slope * gelu_slope(pre)).astype(jnp.bfloat16)
+            return carry
+
+        lax.fori_loop(0, ffn // step, chunk, 0)
+        stores = [
+            pltpu.make_async_copy(act_buf.at[own_expert], act_ref.at[own_expert], store_sem.at[1 + 2 * own_expert]),
+            pltpu.make_async_copy(gpre_buf.at[own_expert], gpre_ref.at[own_expert], store_sem.at[2 + 2 * own_expert]),
+        ]
+        for copy in stores:
+            copy.start()
+        return stores
+
+    stores = expert_part(0)
+    for copy in z_copies:
+        copy.wait()
+    total = zone[0].astype(jnp.float32)
+    for k in range(1, owners):
+        total = total + zone[k].astype(jnp.float32)
+    total_ref[...] = total.astype(jnp.bfloat16)
+    c_copies = []
+    for k, device in enumerate(c_peers):
+        c_copies.append(push(total_ref, all_ref.at[me], c_send.at[k], c_recv.at[k], device))
+        c_copies[-1].start()
+    all_ref[me] = total_ref[...]
+    for own_expert in range(1, own_experts):
+        stores += expert_part(own_expert)
+    loads[6].wait()
+    loads[7].wait()
+    own_swap.wait()
+    for copy in swaps:
+        copy.wait()
     for p in range(2):
-        columns = [grad_ref[0, :, HEAD * (2 * kind + p):HEAD * (2 * kind + p + 1)] for kind in range(3)]
-        part = dot_tn(jnp.concatenate(columns, axis=1), toks_ref[0, p * half:(p + 1) * half, :])
-        total = part if total is None else total + part
-
-    @pl.when(step == 0)
-    def _():
-        acc_ref[...] = total
-
-    @pl.when(step != 0)
-    def _():
-        acc_ref[...] += total
-
-    @pl.when(step == pl.num_programs(0) - 1)
-    def _():
-        out_ref[...] = acc_ref[...].T
-
-
-def head_weight(tokens_all, grad, z_count):
-    count, rows, width = tokens_all.shape
+        columns = [landing[h, :, HEAD * (2 * kind + p):HEAD * (2 * kind + p + 1)] for kind in range(3) for h in range(count)]
+        at = slice(p * half, (p + 1) * half)
+        gtok_ref[at, :] = held_hidden[at, :] + dot_nt(jnp.concatenate(columns, axis=1), held_weight[...])
+    for copy in c_copies:
+        copy.wait()
+    per = lanes // count
+    smalls = []
+    turned = []
+    for c in range(count):
+        turned.append(all_ref[c, :3 * HEAD, :].astype(jnp.float32).T)
+        smalls.append(all_ref[c, 3 * HEAD:3 * HEAD + 16, :].astype(jnp.float32)[:2])
+        for j in range(width // lanes):
+            low = 3 * HEAD + 16 + per * j
+            gout_ref[per * c:per * (c + 1), lanes * j:lanes * (j + 1)] = all_ref[c, low:low + per, :].astype(jnp.float32)
+    for kind in range(3):
+        at = slice(HEAD * kind, HEAD * (kind + 1))
+        gq_ref[:, HEAD * count * kind:HEAD * count * (kind + 1)] = jnp.concatenate([part[:, at] for part in turned], axis=1)
+    small_ref[...] = jnp.concatenate(smalls, axis=0)
+    for copy in stores:
+        copy.wait()
+
+
+def closing(grads, tokens_all, rows, weight, ghidden, gathered, w_up, w_down, groups, owners):
+    count, width = tokens_all.shape[0], tokens_all.shape[2]
+    lanes = width // owners
+    own = (rows.shape[0] - 16) // owners
+    height = 3 * HEAD + 16 + own * (width // lanes)
+    own_experts, _, ffn = w_up.shape
+    sources = gathered.shape[0]
+    view = gathered.reshape(sources, 2, own_experts, groups, width)
+    wide = (own_experts, sources * groups, ffn)
+    dma = pltpu.SemaphoreType.DMA
+    held = [grads, tokens_all, rows, weight, ghidden, view, w_up, w_down]
     return pl.pallas_call(
-        functools.partial(head_weight_body, z_count),
-        grid=(count,),
-        out_shape=jax.ShapeDtypeStruct((width, 3 * HEAD), jnp.float32),
+        functools.partial(closing_body, owners),
+        out_shape=(
+            jax.ShapeDtypeStruct(ghidden.shape, jnp.float32),
+            jax.ShapeDtypeStruct((lanes, 3 * width), jnp.float32),
+            jax.ShapeDtypeStruct((lanes, width), jnp.float32),
+            jax.ShapeDtypeStruct((2 * count, lanes), jnp.float32),
+            jax.ShapeDtypeStruct(wide, jnp.bfloat16),
+            jax.ShapeDtypeStruct(wide, jnp.bfloat16),
+        ),
+        in_specs=[ANY] * 8,
+        out_specs=(VMEM,) * 4 + (ANY,) * 2,
+        scratch_shapes=[pltpu.VMEM(x.shape, x.dtype) for x in held] + [
+            pltpu.VMEM(wide, jnp.bfloat16), pltpu.VMEM(wide, jnp.bfloat16), pltpu.VMEM(grads.shape, jnp.bfloat16),
+            pltpu.VMEM((owners, height, lanes), jnp.bfloat16), pltpu.VMEM((owners, height, lanes), jnp.bfloat16),
+            pltpu.VMEM((height, lanes), jnp.bfloat16), pltpu.VMEM((count, height, lanes), jnp.bfloat16),
+            dma((8,)), dma((1 + 2 * own_experts,)), dma((count - 1,)), dma((count - 1,)), dma((owners - 1,)), dma((owners - 1,)),
+            dma((count - 1,)), dma((count - 1,)),
+        ],
+        compiler_params=pltpu.CompilerParams(collective_id=6, has_side_effects=True, vmem_limit_bytes=LIMIT),
+        cost_estimate=cost(24),
+        name="closing",
+    )(*held)
+
+
+def expert_grad_body(mixed_ref, grad_ref, act_ref, gpre_ref, gup_ref, gdown_ref):
+    width = gup_ref.shape[1]
+    gup_ref[0] = dot_tn(mixed_ref[...].reshape(-1, width), gpre_ref[0])
+    gdown_ref[0] = dot_tn(act_ref[0], grad_ref[...].reshape(-1, width))
+
+
+def expert_grads(gathered, active, grad_pre, groups):
+    own, rows, ffn = active.shape
+    step = 512
+    sources, width = gathered.shape[0], gathered.shape[3]
+    view = gathered.reshape(sources, 2, own, groups, width)
+    return pl.pallas_call(
+        expert_grad_body,
+        grid=(own, ffn // step),
+        out_shape=(jax.ShapeDtypeStruct((own, width, ffn), jnp.float32), jax.ShapeDtypeStruct((own, ffn, width), jnp.float32)),
         in_specs=[
-            pl.BlockSpec((1, rows, width), lambda i: (i, 0, 0)),
-            pl.BlockSpec((1,) + grad.shape[1:], lambda i: (i, 0, 0)),
+            pl.BlockSpec((sources, 1, 1, groups, width), lambda e, f: (0, 0, e, 0, 0)),
+            pl.BlockSpec((sources, 1, 1, groups, width), lambda e, f: (0, 1, e, 0, 0)),
+            pl.BlockSpec((1, rows, step), lambda e, f: (e, 0, f)),
+            pl.BlockSpec((1, rows, step), lambda e, f: (e, 0, f)),
         ],
-        out_specs=pl.BlockSpec((width, 3 * HEAD), lambda i: (0, 0)),
-        scratch_shapes=[pltpu.VMEM((3 * HEAD, width), jnp.float32)],
+        out_specs=(pl.BlockSpec((1, width, step), lambda e, f: (e, 0, f)), pl.BlockSpec((1, step, width), lambda e, f: (e, f, 0))),
         compiler_params=pltpu.CompilerParams(vmem_limit_bytes=LIMIT),
-        name="head_weight",
-    )(tokens_all, grad)
-
-
-def token_grad_body(grad_ref, weight_ref, ghidden_ref, out_ref):
-    heads, half = grad_ref.shape[0], grad_ref.shape[1]
-    for p in range(2):
-        columns = [grad_ref[h, :, HEAD * (2 * kind + p):HEAD * (2 * kind + p + 1)] for kind in range(3) for h in range(heads)]
-        at = slice(p * half, (p + 1) * half)
-        out_ref[at, :] = ghidden_ref[at, :] + dot_nt(jnp.concatenate(columns, axis=1), weight_ref[...])
-
-
-def token_grad(grad, weight, ghidden):
-    return pl.pallas_call(
-        token_grad_body,
-        out_shape=jax.ShapeDtypeStruct(ghidden.shape, jnp.float32),
-        in_specs=[VMEM] * 3,
-        out_specs=VMEM,
-        compiler_params=pltpu.CompilerParams(vmem_limit_bytes=LIMIT),
-        name="token_grad",
-    )(grad, weight, ghidden)
+        cost_estimate=cost(8),
+        name="expert_grads",
+    )(view, view, active, grad_pre)
 
 
 def fast_device(
     tokens, cotangent, block_table, seg_ids, group_ids, w_qkv, w_out, w_router, ln_gain, ln_bias, w_up, w_down
 ):
     ctx_count, z_count = lax.axis_size("ctx"), lax.axis_size("fsdp")
-    ctx_index, z_index = lax.axis_index("ctx"), lax.axis_index("fsdp")
+    ctx_index = lax.axis_index("ctx")
     tok_rows, cot_rows = tokens[0], cotangent[0]
     rows, width = tok_rows.shape
     experts = w_router.shape[1]
@@ -932,28 +1058,24 @@
     got = exchange(mixed, "fsdp", 3, "exchange_mixed")
     back = exchange(run_experts(got, w_up, w_down, groups), "fsdp", 4, "exchange_back")
     gathered = lax.all_gather(got, "ctx", axis=0, tiled=True)
-    layer_out, grad_hidden, gout_part, small_part, grad_heads = unmix_tokens(
+    layer_out, grad_hidden, part_rows, grad_heads = unmix_tokens(
         hidden, normed, mix, attended, cot_rows, out_full, pack_full, back, experts, groups, ctx_count
     )
     grad_heads = exchange(grad_heads, "ctx", 5, "exchange_grad")
-    grad_out = lax.psum(lax.psum_scatter(gout_part, "fsdp", scatter_dimension=0, tiled=True), "ctx")
-    small = lax.psum(small_part, ("ctx", "fsdp"))
-    grad_qkv_all = attn_bwd(grad_heads, saved, block_table, segs)
-    grad_rows = exchange(grad_qkv_all, "ctx", 6, "exchange_qkv")
-    grad_up, grad_down = expert_grads(gathered, w_up, w_down, groups)
-    own_cols = head_weight(tokens_all, grad_qkv_all, z_count)
-    own_cols = lax.psum_scatter(own_cols, "fsdp", scatter_dimension=0, tiled=True)
-    cols = lax.all_gather(own_cols.reshape(shard, 3, 1, HEAD), "ctx", axis=2, tiled=True)
-    grad_tokens = token_grad(grad_rows, qkv_full, grad_hidden)
-    mine = lax.dynamic_slice_in_dim(small, z_index * shard, shard, 1)
+    sum_rows = lax.psum_scatter(part_rows.reshape(-1, width), "ctx", scatter_dimension=0, tiled=True)
+    grads = attn_bwd(grad_heads, saved, block_table, segs)
+    grad_tokens, grad_qkv, grad_out, small, active, grad_pre = closing(
+        grads, tokens_all, sum_rows, qkv_full, grad_hidden, gathered, w_up, w_down, groups, z_count
+    )
+    grad_up, grad_down = expert_grads(gathered, active, grad_pre, groups)
     return (
         layer_out[None],
         grad_tokens[None],
-        cols.reshape(shard, 3 * width),
+        grad_qkv,
         grad_out,
-        mine[:experts].T,
-        mine[experts],
-        mine[experts + 1],
+        small[:experts].T,
+        small[experts],
+        small[experts + 1],
         grad_up,
         grad_down,
     )

time: 363 us -> 245 us (0.67)
  waiting for transfers between devices: 75.2 us -> 14.7 us
  blocking collectives: 52.7 us -> 0 us
  Pallas kernels: 209 us -> 203 us
    psum x1 -> x0, blocking collectives: 41.3 us -> none  [fast_device(): small = lax.psum(small_part, ('ctx', 'fsdp'))]
    psum x1 -> x0, waiting for transfers between devices: 38.7 us -> none  [fast_device(): lax.psum(lax.psum_scatter(gout_part, 'fsdp', scatter_dimension=0, tiled=T...]
    pallas_call x5 -> x4, Pallas kernels: 56.9 us -> 36.5 us  [exchange(): pl.pallas_call(functools.partial(exchange_body, axis, count), out_shape=j...]
    pallas_call x2 -> x1, Pallas kernels: 11.8 us -> 30.1 us  [closing(): pl.pallas_call(functools.partial(closing_body, owners), out_shape=(jax.Sh...]
    all_gather x1 -> x0, blocking collectives: 11.4 us -> none  [fast_device(): lax.all_gather(own_cols.reshape(shard, 3, 1, HEAD), 'ctx', axis=2, tiled=...]
    all_gather x1, waiting for transfers between devices: 24.5 us -> 13.8 us  [fast_device(): gathered = lax.all_gather(got, 'ctx', axis=0, tiled=True)]
    all_gather x1, waiting for transfers between devices: 9.95 us -> 0.01 us  [fast_device(): qkv_full = lax.all_gather(w_qkv, 'fsdp', axis=0, tiled=True)]
    pallas_call x1, Pallas kernels: 18 us -> 13.3 us  [expert_grads(): pl.pallas_call(expert_grad_body, grid=(own, ffn // step), out_shape=(jax....]
  transfers between devices with their start and end apart: 5 -> 3, of which waited for: 3 -> 1; matrix products, arithmetic and copies ran while one was open for 1% -> 0% of each run, Pallas kernels for 12% -> 21%
where the time goes in v2:
time: 245 us
  Pallas kernels  203 us (83%)
  between operations  15.6 us (6%)
  waiting for transfers between devices  14.7 us (6%)
  local copies, waits for them, and re-layouts  8.26 us (3%)
  other arithmetic  2.78 us (1%)
    pallas_call x1, Pallas kernels, attn_bwd(): pl.pallas_call(functools.partial(bwd_body, blocks, block_len), out_shape=...  43.7 us
    pallas_call x4, Pallas kernels, exchange(): pl.pallas_call(functools.partial(exchange_body, axis, count), out_shape=j...  36.5 us
    pallas_call x1, Pallas kernels, attn_fwd(): pl.pallas_call(functools.partial(fwd_body, blocks, block_len), out_shape=...  34.9 us
    pallas_call x1, Pallas kernels, closing(): pl.pallas_call(functools.partial(closing_body, owners), out_shape=(jax.Sh...  30.1 us
    pallas_call x1, Pallas kernels, gather(): pl.pallas_call(functools.partial(gather_body, z_count), out_shape=outs, i...  28.6 us
    all_gather x1, waiting for transfers between devices, fast_device(): gathered = lax.all_gather(got, 'ctx', axis=0, tiled=True)  13.8 us
    pallas_call x1, Pallas kernels, expert_grads(): pl.pallas_call(expert_grad_body, grid=(own, ffn // step), out_shape=(jax....  13.3 us
    pallas_call x1, Pallas kernels, run_experts(): pl.pallas_call(functools.partial(expert_body, groups), grid=(own, ffn //...  7.46 us
  transfers between devices with their start and end apart: 3, of which 1 were waited for; matrix products, arithmetic and copies ran while one was open for 0% of the time, Pallas kernels for 21%

profile of v2, /device:TPU:0, one launch (start us, length us, event | category | flops | bytes accessed | tf_op | source)
XLA Modules:
  0.0 245.0 jit_solution(4806469469927033948)
XLA Ops:
  8.0 0.0 reduce-scatter.2.cloned.1.call-start
  8.1 0.5 broadcast.5
  8.6 1.4 reduce.3
  10.0 0.6 reshape_squeeze.3.seg_ref.segrow_ref
  10.6 1.2 copy.24
  11.8 0.7 copy.25.refs_0_
  12.6 0.1 pad.3.clone
  12.6 1.4 maximum_maximum_fusion.refs_2_
  14.0 28.6 %gather_tokens.1 = (bf16[8,512,512]{2,1,0:T(8,128)(2,1)}, bf16[4,128,192]{2,1,0:T(8,128)(2,1)}, bf16[4,128,512]{2,1,0:T(8,128)(2,1)}, bf16[4,16,128]{2,1,0:T(8,128)(2,1)}) custom-call(bf16[512,512]{1,0:T(8,128)(2,1)} %bitcast.28, bf16[128,192]{1,0:T(8,128)(2,1)} %copy.25.refs_0_, bf16[128,512]{1,0:T(8,128)(2,1)} %refs_1_.1, ...), custom_call_target="tpu_custom_call" | custom-call | flops 27599998976 | bytes 1048576 | tf_op jit(solution)/shard_map/gather_tokens/pallas_call | solution.py:660
  42.6 34.9 %attention.1 = (bf16[8,256,128]{2,1,0:T(8,128)(2,1)}, bf16[4096,256]{1,0:T(8,128)(2,1)}, bf16[4096,256]{1,0:T(8,128)(2,1)}, bf16[4096,128]{1,0:T(8,128)(2,1)}, b...) custom-call(s32[16]{0:T(128)} %table_ref.3, s32[16,256]{1,0:T(8,128)} %reshape_squeeze.3.seg_ref.segrow_ref, ...), custom_call_target="tpu_custom_call" | custom-call | flops 40249999360 | bytes 1048576 | tf_op jit(solution)/shard_map/attention/pallas_call | solution.py:414
  77.5 9.2 %exchange_attended.1.att_ref = bf16[8,256,128]{2,1,0:T(8,128)(2,1)} custom-call(bf16[8,256,128]{2,1,0:T(8,128)(2,1)} %get-tuple-element.38.x_ref), custom_call_target="tpu_custom_call" | custom-call | flops 10350000128 | bytes 1048576 | tf_op jit(solution)/shard_map/exchange_attended/pallas_call | solution.py:576
  86.8 3.5 %mix_tokens.1 = (f32[512,512]{1,0:T(8,128)}, bf16[512,512]{1,0:T(8,128)(2,1)}, f32[128,512]{1,0:T(8,128)}, bf16[512,512]{1,0:T(8,128)(2,1)}, bf16[4,2,32,512]{3,2,1,0:T(8,128)(2,1)}) custom-call(bf16[8,256,128]{2,1,0:T(8,128)(2,1)} %exchange_attended.1.att_ref, bf16[512,512]{1,0:T(8,128)(2,1)} %bitcast.29, bf16[512,512]{1,0:T(8,128)(2,1)} %bitcast.30, ...), custom_call_target="tpu_custom_call" | custom-call | flops 4600000000 | bytes 1048576 | tf_op jit(solution)/shard_map/mix_tokens/pallas_call | solution.py:714
  90.3 9.1 %exchange_mixed.1.got_ref = bf16[4,2,32,512]{3,2,1,0:T(8,128)(2,1)} custom-call(bf16[4,2,32,512]{3,2,1,0:T(8,128)(2,1)} %get-tuple-element.45.x_ref), custom_call_target="tpu_custom_call" | custom-call | flops 10350000128 | bytes 1048576 | tf_op jit(solution)/shard_map/exchange_mixed/pallas_call | solution.py:576
  99.4 7.5 %experts.1.x_ref = bf16[4,2,32,512]{3,2,1,0:T(8,128)(2,1)} custom-call(bf16[4,2,32,512]{3,2,1,0:T(8,128)(2,1)} %exchange_mixed.1.got_ref, bf16[2,512,2048]{2,1,0:T(8,128)(2,1)} %up_ref.3, bf16[2,2048,512]{2,1,0:T(8,128)(2,1)} %down_ref.3), custom_call_target="tpu_custom_call" | custom-call | flops 9200000000 | bytes 1048576 | tf_op jit(solution)/shard_map/experts/pallas_call | solution.py:763
  106.9 9.3 %exchange_back.1.back_ref = bf16[4,2,32,512]{3,2,1,0:T(8,128)(2,1)} custom-call(bf16[4,2,32,512]{3,2,1,0:T(8,128)(2,1)} %experts.1.x_ref), custom_call_target="tpu_custom_call" | custom-call | flops 10350000128 | bytes 1048576 | tf_op jit(solution)/shard_map/exchange_back/pallas_call | solution.py:576
  116.2 5.3 %unmix_tokens.1 = (f32[512,512]{1,0:T(8,128)}, f32[512,512]{1,0:T(8,128)}, f32[8,80,512]{2,1,0:T(8,128)}, bf16[8,256,128]{2,1,0:T(8,128)(2,1)}) custom-call(f32[512,512]{1,0:T(8,128)} %get-tuple-element.41.hidden_ref, bf16[512,512]{1,0:T(8,128)(2,1)} %get-tuple-element.42.normed_ref, f32[128,512]{1,0:T(8,128)} %get-tuple-element.43.mix_ref, ...), custom_call_target="tpu_custom_call" | custom-call | flops 5750000128 | bytes 1048576 | tf_op jit(solution)/shard_map/unmix_tokens/pallas_call | solution.py:829
  121.4 0.0 reduce-scatter.2.cloned.1.call-update
  121.4 0.0 all-gather.3.cloned.1.call-start
  121.5 0.5 all-gather.3.cloned.1.call-update
  122.0 0.2 all-gather.5.cloned.1.call-start
  122.2 0.4 all-gather.5.cloned.1.call-update
  122.6 8.9 %exchange_grad.1.do_ref = bf16[8,256,128]{2,1,0:T(8,128)(2,1)} custom-call(bf16[8,256,128]{2,1,0:T(8,128)(2,1)} %get-tuple-element.47.x_ref), custom_call_target="tpu_custom_call" | custom-call | flops 10350000128 | bytes 1048576 | tf_op jit(solution)/shard_map/exchange_grad/pallas_call | solution.py:576
  131.6 43.7 %attention_grad.1.grads_ref = bf16[8,256,384]{2,1,0:T(8,128)(2,1)} custom-call(s32[16]{0:T(128)} %table_ref.3, s32[16,256]{1,0:T(8,128)} %reshape_squeeze.3.seg_ref.segrow_ref, bf16[8,256,128]{2,1,0:T(8,128)(2,1)} %exchange_grad.1.do_ref, bf16[4096,256]{1,0:T(8,128)(2,1)} %get-tuple-element.48.qf_ref, bf16[4096,256]{1,0:T(8,128)(2,1)} %get-tuple-element.49.kf_ref, ...), custom_call_target="tpu_custom_call" | custom-call | flops 46000001024 | bytes 1048576 | tf_op jit(solution)/shard_map/attention_grad/pallas_call | solution.py:516
  175.2 0.0 reduce-scatter.2.cloned.1.call-done.rows_ref
  175.2 0.0 all-gather.3.cloned.1.call-done.weight_ref
  175.2 13.8 %all-gather.5.cloned.1.call-done = bf16[32,2,32,512]{3,2,1,0:T(8,128)(2,1)} async-done(((bf16[4,2,32,512]{3,2,1,0:T(8,128)(2,1)}), bf16[32,2,32,512]{3,2,1,0:T(8,128)(2,1)}) %all-gather.5.cloned.1.call-update) | async-done | bytes 2097168 | tf_op jit(solution)/shard_map/all_gather | solution.py:1060
  189.0 30.1 %closing.1 = (f32[512,512]{1,0:T(8,128)}, f32[128,1536]{1,0:T(8,128)}, f32[128,512]{1,0:T(8,128)}, f32[16,128]{1,0:T(8,128)}, bf16[2,512,2048]{2,1,0:T(8,128)(2,1)}, /*index=5*/bf16[2,512,2048]{2,1,0:T(8,128)(2,1)}) custom-call(bf16[8,256,384]{2,1,0:T(8,128)(2,1)} %attention_grad.1.grads_ref, bf16[8,512,512]{2,1,0:T(8,128)(2,1)} %get-tuple-element.36.toks_ref, ...), custom_call_target="tpu_custom_call" | custom-call | flops 27599998976 | bytes 1048576 | tf_op jit(solution)/shard_map/closing/pallas_call | solution.py:983
  219.2 1.3 slice_bitcast_fusion.1
  220.5 1.3 slice_bitcast_fusion
  221.7 0.0 copy-start
  221.7 0.0 copy-start.1
  221.7 0.0 copy-start.2
  221.7 13.3 %expert_grads.1 = (f32[2,512,2048]{2,1,0:T(8,128)}, f32[2,2048,512]{2,1,0:T(8,128)}) custom-call(bf16[32,2,2,16,512]{4,3,2,1,0:T(8,128)(2,1)} %bitcast.26, bf16[32,2,2,16,512]{4,3,2,1,0:T(8,128)(2,1)} %bitcast.27, bf16[2,512,2048]{2,1,0:T(8,128)(2,1)} %get-tuple-element.59.act_ref, bf16[2,512,2048]{2,1,0:T(8,128)(2,1)} %get-tuple-element.60.gpre_ref), custom_call_target="tpu_custom_call" | custom-call | flops 9200000000 | bytes 1048576 | tf_op jit(solution)/shard_map/expert_grads/pallas_call | solution.py:1019
  235.0 0.0 copy-done
  235.0 1.0 copy.29
  236.0 0.0 copy-done.1
  236.0 0.9 copy.30
  236.9 0.0 copy-done.2
  236.9 0.7 copy.31
  (2 shorter events, 0.0 us)
Async XLA Ops:
  8.0 167.2 %reduce-scatter.2.cloned.1.call-start = ((), (), s32[]{:S(2)}) async-start(), calls=%async_computation.1 | async-start | bytes 1474560 | tf_op jit(solution)/shard_map/reduce_scatter | solution.py:1065
  121.4 53.8 %all-gather.3.cloned.1.call-start = ((), (), s32[]{:S(2)}) async-start(), calls=%async_computation.2 | async-start | bytes 1966080 | tf_op jit(solution)/shard_map/all_gather | solution.py:1052
  122.0 67.0 %all-gather.5.cloned.1.call-start = ((), (), s32[]{:S(2)}) async-start(), calls=%async_computation.3 | async-start | bytes 2359296 | tf_op jit(solution)/shard_map/all_gather | solution.py:1060
  221.7 13.3 %copy-start = (f32[512,512]{1,0:T(8,128)S(1)}, f32[512,512]{1,0:T(8,128)}, u32[]{:S(2)}) copy-start(f32[512,512]{1,0:T(8,128)} %get-tuple-element.55) | copy-start | bytes 3145732
  221.7 14.3 %copy-start.1 = (f32[128,1536]{1,0:T(8,128)S(1)}, f32[128,1536]{1,0:T(8,128)}, u32[]{:S(2)}) copy-start(f32[128,1536]{1,0:T(8,128)} %get-tuple-element.76) | copy-start | bytes 2359300
  221.7 15.2 %copy-start.2 = (f32[128,512]{1,0:T(8,128)S(1)}, f32[128,512]{1,0:T(8,128)}, u32[]{:S(2)}) copy-start(f32[128,512]{1,0:T(8,128)} %get-tuple-element.77) | copy-start | bytes 786436
Sparse Core Ops, SparseCore 0:
  121.6 37.5 reduce-scatter.1
Sparse Core Ops, SparseCore 1:
  123.5 37.1 all-gather.2
  162.4 26.6 all-gather.4

commit v3 on v2

--- a/solution.py
+++ b/solution.py
@@ -554,37 +554,6 @@
     )
 
 
-def exchange_body(axis, count, x_ref, out_ref, own_sem, send_sem, recv_sem):
-    spot = {"ctx": lax.axis_index("ctx"), "fsdp": lax.axis_index("fsdp")}
-    me = spot[axis]
-    others = [lax.rem(me + k, count) for k in range(1, count)]
-    meet([(other, spot["fsdp"]) if axis == "ctx" else (spot["ctx"], other) for other in others])
-    own = pltpu.make_async_copy(x_ref.at[me], out_ref.at[me], own_sem)
-    own.start()
-    copies = []
-    for k, other in enumerate(others):
-        device = (other, spot["fsdp"]) if axis == "ctx" else (spot["ctx"], other)
-        copies.append(push(x_ref.at[other], out_ref.at[me], send_sem.at[k], recv_sem.at[k], device))
-        copies[-1].start()
-    own.wait()
-    for copy in copies:
-        copy.wait()
-
-
-def exchange(x, axis, collective_id, name):
-    count = x.shape[0]
-    return pl.pallas_call(
-        functools.partial(exchange_body, axis, count),
-        out_shape=jax.ShapeDtypeStruct(x.shape, x.dtype),
-        in_specs=[ANY],
-        out_specs=ANY,
-        scratch_shapes=[pltpu.SemaphoreType.DMA, pltpu.SemaphoreType.DMA((count - 1,)), pltpu.SemaphoreType.DMA((count - 1,))],
-        compiler_params=pltpu.CompilerParams(collective_id=collective_id, has_side_effects=True),
-        cost_estimate=cost(9),
-        name=name,
-    )(x)
-
-
 def gather_body(zs, tok_ref, *refs):
     count = (len(refs) - 9) // 2
     shards, toks_ref, wholes = refs[:count], refs[count], refs[count + 1:2 * count + 1]
@@ -678,168 +647,165 @@
     return center * inv_dev, inv_dev
 
 
-def small_rows(pack_ref):
-    return jnp.concatenate([pack_ref[z] for z in range(pack_ref.shape[0])], axis=1)
-
-
-def mix_body(experts, groups, att_ref, tok_ref, cot_ref, wo_ref, pack_ref, gid_ref, hidden_ref, normed_ref, mix_ref, attended_ref, send_ref):
-    heads = att_ref.shape[0]
-    halves = [jnp.concatenate([att_ref[h, :, HEAD * p:HEAD * (p + 1)] for h in range(heads)], axis=1) for p in range(2)]
+def middle_body(
+    experts, groups, att_ref, tok_ref, cot_ref, wo_ref, pack_ref, gid_ref, up_ref, down_ref, later_ref,
+    layer_ref, ghidden_ref, gout_ref, small_ref, all_ref, ghead_ref,
+    tok, cot, wo, pack, up, down, att, zsend, zin, bsend, bin_, ghead,
+    load_sem, own_sem, a_send, a_recv, m_send, m_recv, b_send, b_recv, g_send, g_recv, r_send, r_recv, h_send, h_recv,
+):
+    me, z = lax.axis_index("ctx"), lax.axis_index("fsdp")
+    count, half = att_ref.shape[0], att_ref.shape[1]
+    rows, width = tok_ref.shape
+    owners, own_experts = zsend.shape[0], up_ref.shape[0]
+    flat, per = experts * groups, experts * groups // owners
+    pairs = [(tok_ref, tok), (wo_ref, wo), (pack_ref, pack), (cot_ref, cot)]
+    for e in range(own_experts):
+        pairs += [(up_ref.at[e], up.at[e]), (down_ref.at[e], down.at[e])]
+    loads = [pltpu.make_async_copy(src, dst, load_sem.at[i]) for i, (src, dst) in enumerate(pairs)]
+    for copy in loads:
+        copy.start()
+    sib, same_core = flip(me, 1), [flip(me, 2), flip(me, 4), flip(flip(me, 2), 4)]
+    z_peers = [(me, lax.rem(z + k, owners)) for k in range(1, owners)]
+    c_peers = [(jnp.bitwise_xor(me, k), z) for k in range(1, count)]
+    meet(z_peers + c_peers)
+
+    def start(copies):
+        for copy in copies:
+            copy.start()
+        return copies
+
+    def wait(copies):
+        for copy in copies:
+            copy.wait()
+
+    swap = start([push(att_ref.at[d[0]], att.at[me], a_send.at[k], a_recv.at[k], d) for k, d in enumerate(c_peers)])
+    own = start([pltpu.make_async_copy(att_ref.at[me], att.at[me], own_sem.at[0])])
+    small_in = None
+    wait(own + swap)
+    wait(loads[:4])
+    halves = [jnp.concatenate([att[h, :, HEAD * p:HEAD * (p + 1)] for h in range(count)], axis=1) for p in range(2)]
     attended = jnp.concatenate(halves, axis=0)
-    attended_ref[...] = attended
-    width = tok_ref.shape[1]
-    hidden = tok_ref[...].astype(jnp.float32) + dot_nn(attended, wo_ref[...].reshape(width, width))
-    hidden_ref[...] = hidden
+    weight = wo[...].reshape(width, width)
+    hidden = tok[...].astype(jnp.float32) + dot_nn(attended, weight)
     unit, inv_dev = norm_parts(hidden)
-    small = small_rows(pack_ref)
-    gain, bias = small[experts:experts + 1].astype(jnp.float32), small[experts + 1:experts + 2].astype(jnp.float32)
+    small_in = jnp.concatenate([pack[k] for k in range(owners)], axis=1)
+    gain, bias = small_in[experts:experts + 1].astype(jnp.float32), small_in[experts + 1:experts + 2].astype(jnp.float32)
     normed = (unit * gain + bias).astype(jnp.bfloat16)
-    normed_ref[...] = normed
-    expo = jnp.exp(dot_nt(small, normed)[:experts])
-    rows = tok_ref.shape[0]
-    expo = jnp.broadcast_to(expo[:, None, :], (experts, groups, rows)).reshape(experts * groups, rows)
-    member = lax.rem(lax.broadcasted_iota(jnp.int32, (experts * groups, 1), 0), groups) == lax.rem(gid_ref[...], groups)
+    expo = jnp.exp(dot_nt(small_in, normed)[:experts])
+    expo = jnp.broadcast_to(expo[:, None, :], (experts, groups, rows)).reshape(flat, rows)
+    member = lax.rem(lax.broadcasted_iota(jnp.int32, (flat, 1), 0), groups) == lax.rem(gid_ref[...], groups)
     expo = jnp.where(member, expo, 0.0)
     mix = expo / jnp.sum(expo, axis=1, keepdims=True)
-    mix_ref[...] = mix
     low = mix.astype(jnp.bfloat16)
-    owners = send_ref.shape[0]
-    per = experts * groups // owners
-    send_ref[:, 0] = dot_nn(low, normed).astype(jnp.bfloat16).reshape(owners, per, width)
-    send_ref[:, 1] = dot_nn(low, cot_ref[...]).astype(jnp.bfloat16).reshape(owners, per, width)
-
-
-def mix_tokens(att, tokens, cot, w_out, pack, gid_row, experts, groups, owners):
-    rows, width = tokens.shape
-    return pl.pallas_call(
-        functools.partial(mix_body, experts, groups),
-        out_shape=(
-            jax.ShapeDtypeStruct((rows, width), jnp.float32),
-            jax.ShapeDtypeStruct((rows, width), jnp.bfloat16),
-            jax.ShapeDtypeStruct((experts * groups, rows), jnp.float32),
-            jax.ShapeDtypeStruct((rows, width), jnp.bfloat16),
-            jax.ShapeDtypeStruct((owners, 2, experts * groups // owners, width), jnp.bfloat16),
-        ),
-        in_specs=[VMEM] * 6,
-        out_specs=(VMEM,) * 5,
-        compiler_params=pltpu.CompilerParams(vmem_limit_bytes=LIMIT),
-        cost_estimate=cost(4),
-        name="mix_tokens",
-    )(att, tokens, cot, w_out, pack, gid_row)
-
-
-def expert_body(groups, got_ref, up_ref, down_ref, back_ref, out_acc, grad_acc):
-    own, part = pl.program_id(0), pl.program_id(1)
-    at = pl.ds(pl.multiple_of(own * groups, groups), groups)
-    sources, width = got_ref.shape[0], got_ref.shape[3]
-    mixed = got_ref[:, 0, at, :].reshape(sources * groups, width)
-    grad_out = got_ref[:, 1, at, :].reshape(sources * groups, width)
-    up, down = up_ref[0], down_ref[0]
-    pre = dot_nn(mixed, up)
-    active = jax.nn.gelu(pre, approximate=True).astype(jnp.bfloat16)
-    grad_pre = (dot_nt(grad_out, down) * gelu_slope(pre)).astype(jnp.bfloat16)
-    out, grad = dot_nn(active, down), dot_nt(grad_pre, up)
-
-    @pl.when(part == 0)
-    def _():
-        out_acc[...] = out
-        grad_acc[...] = grad
-
-    @pl.when(part != 0)
-    def _():
-        out_acc[...] += out
-        grad_acc[...] += grad
-
-    @pl.when(part == pl.num_programs(1) - 1)
-    def _():
-        back_ref[:, 0, at, :] = out_acc[...].astype(jnp.bfloat16).reshape(sources, groups, width)
-        back_ref[:, 1, at, :] = grad_acc[...].astype(jnp.bfloat16).reshape(sources, groups, width)
-
-
-def run_experts(got, w_up, w_down, groups):
-    own, width, ffn = w_up.shape
-    step = 1024
-    rows = got.shape[0] * groups
-    return pl.pallas_call(
-        functools.partial(expert_body, groups),
-        grid=(own, ffn // step),
-        out_shape=jax.ShapeDtypeStruct(got.shape, jnp.bfloat16),
-        in_specs=[
-            pl.BlockSpec(got.shape, lambda e, f: (0, 0, 0, 0)),
-            pl.BlockSpec((1, width, step), lambda e, f: (e, 0, f)),
-            pl.BlockSpec((1, step, width), lambda e, f: (e, f, 0)),
-        ],
-        out_specs=pl.BlockSpec(got.shape, lambda e, f: (0, 0, 0, 0)),
-        scratch_shapes=[pltpu.VMEM((rows, width), jnp.float32)] * 2,
-        compiler_params=pltpu.CompilerParams(vmem_limit_bytes=LIMIT),
-        cost_estimate=cost(8),
-        name="experts",
-    )(got, w_up, w_down)
-
-
-def unmix_body(experts, groups, heads, hidden_ref, normed_ref, mix_ref, attended_ref, cot_ref, wo_ref, pack_ref, back_ref,
-               layer_ref, ghidden_ref, rows_ref, ghead_ref):
-    rows, width = hidden_ref.shape
-    hidden, normed, mix, cot = hidden_ref[...], normed_ref[...], mix_ref[...], cot_ref[...]
-    low = mix.astype(jnp.bfloat16)
-    flat = experts * groups
-    expert_out, grad_mixed = back_ref[:, 0].reshape(flat, width), back_ref[:, 1].reshape(flat, width)
+
+    def to_owners(kind, value):
+        zsend[:, kind] = value.astype(jnp.bfloat16).reshape(owners, per, width)
+        zin[z, kind] = zsend[z, kind]
+        return start([
+            push(zsend.at[d[1], kind], zin.at[z, kind], m_send.at[kind, k], m_recv.at[kind, k], d) for k, d in enumerate(z_peers)
+        ])
+
+    mixed_copies = to_owners(0, dot_nn(low, normed))
+    grad_copies = to_owners(1, dot_nn(low, cot[...]))
+    wait(loads[4:])
+    wait(mixed_copies)
+
+    def from_sources(kind, e):
+        return zin[:, kind, e * groups:(e + 1) * groups, :].reshape(owners * groups, width)
+
+    def to_sources(kind, e, value):
+        bsend[:, kind, e * groups:(e + 1) * groups, :] = value.astype(jnp.bfloat16).reshape(owners, groups, width)
+
+    def send_back(kind):
+        bin_[z, kind] = bsend[z, kind]
+        return start([
+            push(bsend.at[d[1], kind], bin_.at[z, kind], b_send.at[kind, k], b_recv.at[kind, k], d) for k, d in enumerate(z_peers)
+        ])
+
+    pres = []
+    for e in range(own_experts):
+        pre = dot_nn(from_sources(0, e), up[e])
+        pres.append(pre)
+        active = jax.nn.gelu(pre, approximate=True).astype(jnp.bfloat16)
+        to_sources(0, e, dot_nn(active, down[e]))
+    out_copies = send_back(0)
+    wait(grad_copies)
+    gather_copies = start([push(zin, all_ref.at[me], g_send.at[k], g_recv.at[k], (d, z)) for k, d in enumerate(same_core)])
+    relays = start([push(zin, all_ref.at[me], r_send.at[0], r_recv.at[0], (sib, z))])
+    own = start([pltpu.make_async_copy(zin, all_ref.at[me], own_sem.at[1])])
+    for e in range(own_experts):
+        grad_pre = (dot_nt(from_sources(1, e), down[e]) * gelu_slope(pres[e])).astype(jnp.bfloat16)
+        to_sources(1, e, dot_nt(grad_pre, up[e]))
+    back_copies = send_back(1)
+    wait(out_copies)
+    expert_out = bin_[:, 0].reshape(flat, width)
     layer_ref[...] = hidden + dot_tn(low, expert_out)
-    product = mix * (dot_nt(expert_out, cot) + dot_nt(grad_mixed, normed))
+    grad_mix = dot_nt(expert_out, cot[...])
+    wait(back_copies)
+    grad_mixed = bin_[:, 1].reshape(flat, width)
+    product = mix * (grad_mix + dot_nt(grad_mixed, normed))
     grad_logits = product - mix * jnp.sum(product, axis=1, keepdims=True)
     grad_logits = jnp.sum(grad_logits.reshape(experts, groups, rows), axis=1).astype(jnp.bfloat16)
-    small = small_rows(pack_ref)
-    pad = jnp.zeros((small.shape[0] - experts, rows), jnp.bfloat16)
+    pad = jnp.zeros((small_in.shape[0] - experts, rows), jnp.bfloat16)
     grad_logits = jnp.concatenate([grad_logits, pad], axis=0)
-    grad_normed = dot_tn(jnp.concatenate([low, grad_logits], axis=0), jnp.concatenate([grad_mixed, small], axis=0))
-    gain = small[experts:experts + 1].astype(jnp.float32)
-    unit, inv_dev = norm_parts(hidden)
-    small_grad = jnp.concatenate(
+    grad_normed = dot_tn(jnp.concatenate([low, grad_logits], axis=0), jnp.concatenate([grad_mixed, small_in], axis=0))
+    scaled = grad_normed * gain
+    mean = jnp.mean(scaled, axis=-1, keepdims=True)
+    grad_hidden = cot[...].astype(jnp.float32) + inv_dev * (scaled - mean - unit * jnp.mean(scaled * unit, axis=-1, keepdims=True))
+    branch = grad_hidden.astype(jnp.bfloat16)
+    grad_heads = dot_nt(branch, weight).astype(jnp.bfloat16)
+    for h in range(count):
+        at = slice(HEAD * h, HEAD * (h + 1))
+        ghead[h] = jnp.concatenate([grad_heads[:half, at], grad_heads[half:, at]], axis=1)
+    swap = start([push(ghead.at[d[0]], ghead_ref.at[me], h_send.at[k], h_recv.at[k], d) for k, d in enumerate(c_peers)])
+    last = start([pltpu.make_async_copy(ghead.at[me], ghead_ref.at[me], own_sem.at[2])])
+    for k, d in enumerate(same_core):
+        gather_copies[k].wait_recv()
+        relays += start([push(all_ref.at[d], all_ref.at[d], r_send.at[k + 1], r_recv.at[k + 1], (sib, z))])
+    ghidden_ref[...] = grad_hidden
+    gout_ref[...] = dot_tn(attended, branch).astype(jnp.bfloat16).reshape(gout_ref.shape)
+    small_ref[...] = jnp.concatenate(
         [
             dot_nn(grad_logits, normed)[:experts],
             jnp.sum(grad_normed * unit, axis=0, keepdims=True),
             jnp.sum(grad_normed, axis=0, keepdims=True),
-            jnp.zeros((small.shape[0] - experts - 2, width), jnp.float32),
+            jnp.zeros((small_in.shape[0] - experts - 2, width), jnp.float32),
         ],
         axis=0,
     )
-    scaled = grad_normed * gain
-    mean = jnp.mean(scaled, axis=-1, keepdims=True)
-    grad_hidden = cot.astype(jnp.float32) + inv_dev * (scaled - mean - unit * jnp.mean(scaled * unit, axis=-1, keepdims=True))
-    ghidden_ref[...] = grad_hidden
-    branch = grad_hidden.astype(jnp.bfloat16)
-    gout = dot_tn(attended_ref[...], branch)
-    owners, count = pack_ref.shape[0], rows_ref.shape[0]
-    own = width // (owners * count)
-    for c in range(count):
-        for z in range(owners):
-            low = (z * count + c) * own
-            rows_ref[c, z * own:(z + 1) * own, :] = gout[low:low + own]
-        rows_ref[c, owners * own:, :] = jnp.zeros((16, width), jnp.float32)
-        rows_ref[c, owners * own:owners * own + 2, :] = small_grad[2 * c:2 * c + 2]
-    grad_heads = dot_nt(branch, wo_ref[...].reshape(width, width)).astype(jnp.bfloat16)
-    half = rows // 2
-    for h in range(heads):
-        at = slice(HEAD * h, HEAD * (h + 1))
-        ghead_ref[h] = jnp.concatenate([grad_heads[:half, at], grad_heads[half:, at]], axis=1)
-
-
-def unmix_tokens(hidden, normed, mix, attended, cot, w_out, pack, back, experts, groups, heads):
-    rows, width = hidden.shape
+    for copy in gather_copies:
+        copy.wait_send()
+    wait(own + last + relays + swap)
+
+
+def middle(att, tokens, cot, w_out, pack, gid_row, w_up, w_down, later, experts, groups):
+    rows, width = tokens.shape
+    count, owners, own = att.shape[0], pack.shape[0], w_up.shape[0]
+    sent = (owners, 2, experts * groups // owners, width)
+    dma = pltpu.SemaphoreType.DMA
+    low, full = jnp.bfloat16, jnp.float32
     return pl.pallas_call(
-        functools.partial(unmix_body, experts, groups, heads),
+        functools.partial(middle_body, experts, groups),
         out_shape=(
-            jax.ShapeDtypeStruct((rows, width), jnp.float32),
-            jax.ShapeDtypeStruct((rows, width), jnp.float32),
-            jax.ShapeDtypeStruct((heads, width // heads + 16, width), jnp.float32),
-            jax.ShapeDtypeStruct((heads, rows // 2, 2 * HEAD), jnp.bfloat16),
+            jax.ShapeDtypeStruct((rows, width), full),
+            jax.ShapeDtypeStruct((rows, width), full),
+            jax.ShapeDtypeStruct((owners, width // owners, width), low),
+            jax.ShapeDtypeStruct((pack.shape[1], width), full),
+            jax.ShapeDtypeStruct((count,) + sent, low),
+            jax.ShapeDtypeStruct(att.shape, low),
         ),
-        in_specs=[VMEM] * 8,
-        out_specs=(VMEM,) * 4,
-        compiler_params=pltpu.CompilerParams(vmem_limit_bytes=LIMIT),
-        cost_estimate=cost(5),
-        name="unmix_tokens",
-    )(hidden, normed, mix, attended, cot, w_out, pack, back)
+        in_specs=[ANY] * 5 + [VMEM] + [ANY] * 3,
+        out_specs=(VMEM,) * 4 + (ANY,) * 2,
+        scratch_shapes=[pltpu.VMEM(x.shape, x.dtype) for x in (tokens, cot, w_out, pack, w_up, w_down, att)] + [
+            pltpu.VMEM(sent, low), pltpu.VMEM(sent, low), pltpu.VMEM(sent, low), pltpu.VMEM(sent, low), pltpu.VMEM(att.shape, low),
+            dma((4 + 2 * own,)), dma((3,)), dma((count - 1,)), dma((count - 1,)), dma((2, owners - 1)), dma((2, owners - 1)),
+            dma((2, owners - 1)), dma((2, owners - 1)), dma((3,)), dma((3,)), dma((4,)), dma((4,)), dma((count - 1,)),
+            dma((count - 1,)),
+        ],
+        compiler_params=pltpu.CompilerParams(collective_id=2, has_side_effects=True, vmem_limit_bytes=LIMIT),
+        cost_estimate=cost(35),
+        name="middle",
+    )(att, tokens, cot, w_out, pack, gid_row, w_up, w_down, later)
 
 
 def head_columns(ref, p, index=None):
@@ -851,18 +817,18 @@
 
 
 def closing_body(
-    owners, grads_ref, toks_ref, rows_ref, weight_ref, ghidden_ref, gathered_ref, up_ref, down_ref,
+    owners, grads_ref, toks_ref, small_in_ref, out_ref, weight_ref, ghidden_ref, gathered_ref, up_ref, down_ref,
     gtok_ref, gq_ref, gout_ref, small_ref, act_ref, gpre_ref,
-    held_grads, held_toks, held_rows, held_weight, held_hidden, held_mixed, held_up, held_down, act_buf, gpre_buf,
-    landing, zsend, zone, total_ref, all_ref,
-    load_sem, store_sem, a_send, a_recv, z_send, z_recv, c_send, c_recv,
+    held_grads, held_toks, held_small, held_weight, held_hidden, held_mixed, held_up, held_down, act_buf, gpre_buf,
+    landing, zsend, zone, total_ref, all_ref, out_zone, out_sum, out_part, out_own, out_all,
+    load_sem, store_sem, a_send, a_recv, z_send, z_recv, c_send, c_recv, o_send, o_recv,
 ):
     me, z = lax.axis_index("ctx"), lax.axis_index("fsdp")
     count, half = grads_ref.shape[0], grads_ref.shape[1]
     width = toks_ref.shape[2]
     own_experts, ffn = up_ref.shape[0], up_ref.shape[2]
     pairs = [
-        (grads_ref, held_grads), (toks_ref, held_toks), (rows_ref, held_rows), (gathered_ref, held_mixed), (up_ref, held_up),
+        (grads_ref, held_grads), (toks_ref, held_toks), (small_in_ref, held_small), (gathered_ref, held_mixed), (up_ref, held_up),
         (down_ref, held_down), (weight_ref, held_weight), (ghidden_ref, held_hidden),
     ]
     loads = [pltpu.make_async_copy(src, dst, load_sem.at[i]) for i, (src, dst) in enumerate(pairs)]
@@ -877,6 +843,12 @@
         swaps[-1].start()
     own_swap = pltpu.make_async_copy(grads_ref.at[me], landing.at[me], store_sem.at[0])
     own_swap.start()
+    out_copies = []
+    for k, device in enumerate(z_peers):
+        out_copies.append(push(out_ref.at[device[1]], out_zone.at[z], o_send.at[0, k], o_recv.at[0, k], device))
+        out_copies[-1].start()
+    own_out = pltpu.make_async_copy(out_ref.at[z], out_zone.at[z], store_sem.at[1])
+    own_out.start()
 
     loads[0].wait()
     loads[1].wait()
@@ -887,15 +859,10 @@
             total = part if total is None else total + part
     loads[2].wait()
     lanes = width // owners
-    small = held_rows.shape[0] - 16
-    own = small // owners
     for c in range(owners):
         at = slice(c * lanes, (c + 1) * lanes)
         zsend[c, :3 * HEAD, :] = total[:, at].astype(jnp.bfloat16)
-        zsend[c, 3 * HEAD:3 * HEAD + 16, :] = held_rows[small:, at].astype(jnp.bfloat16)
-        for j in range(width // lanes):
-            low = 3 * HEAD + 16 + own * j
-            zsend[c, low:low + own, :] = held_rows[own * c:own * (c + 1), lanes * j:lanes * (j + 1)].astype(jnp.bfloat16)
+        zsend[c, 3 * HEAD:, :] = held_small[:, at].astype(jnp.bfloat16)
     z_copies = []
     for k, device in enumerate(z_peers):
         z_copies.append(push(zsend.at[device[1]], zone.at[z], z_send.at[k], z_recv.at[k], device))
@@ -920,8 +887,8 @@
 
         lax.fori_loop(0, ffn // step, chunk, 0)
         stores = [
-            pltpu.make_async_copy(act_buf.at[own_expert], act_ref.at[own_expert], store_sem.at[1 + 2 * own_expert]),
-            pltpu.make_async_copy(gpre_buf.at[own_expert], gpre_ref.at[own_expert], store_sem.at[2 + 2 * own_expert]),
+            pltpu.make_async_copy(act_buf.at[own_expert], act_ref.at[own_expert], store_sem.at[2 + 2 * own_expert]),
+            pltpu.make_async_copy(gpre_buf.at[own_expert], gpre_ref.at[own_expert], store_sem.at[3 + 2 * own_expert]),
         ]
         for copy in stores:
             copy.start()
@@ -939,8 +906,32 @@
         c_copies.append(push(total_ref, all_ref.at[me], c_send.at[k], c_recv.at[k], device))
         c_copies[-1].start()
     all_ref[me] = total_ref[...]
+    own_out.wait()
+    for copy in out_copies:
+        copy.wait()
+    total = out_zone[0].astype(jnp.float32)
+    for k in range(1, owners):
+        total = total + out_zone[k].astype(jnp.float32)
+    per = lanes // count
+    out_sum[...] = total.astype(jnp.bfloat16).reshape(out_sum.shape)
+    part_copies = []
+    for k, device in enumerate(c_peers):
+        part_copies.append(push(out_sum.at[device[0]], out_part.at[me], o_send.at[1, k], o_recv.at[1, k], device))
+        part_copies[-1].start()
+    out_part[me] = out_sum[me]
     for own_expert in range(1, own_experts):
         stores += expert_part(own_expert)
+    for copy in part_copies:
+        copy.wait()
+    total = out_part[0].astype(jnp.float32)
+    for k in range(1, count):
+        total = total + out_part[k].astype(jnp.float32)
+    out_own[...] = total.astype(jnp.bfloat16)
+    last_copies = []
+    for k, device in enumerate(c_peers):
+        last_copies.append(push(out_own, out_all.at[me], o_send.at[2, k], o_recv.at[2, k], device))
+        last_copies[-1].start()
+    out_all[me] = out_own[...]
     loads[6].wait()
     loads[7].wait()
     own_swap.wait()
@@ -952,57 +943,59 @@
         gtok_ref[at, :] = held_hidden[at, :] + dot_nt(jnp.concatenate(columns, axis=1), held_weight[...])
     for copy in c_copies:
         copy.wait()
-    per = lanes // count
-    smalls = []
+    small = None
     turned = []
     for c in range(count):
         turned.append(all_ref[c, :3 * HEAD, :].astype(jnp.float32).T)
-        smalls.append(all_ref[c, 3 * HEAD:3 * HEAD + 16, :].astype(jnp.float32)[:2])
-        for j in range(width // lanes):
-            low = 3 * HEAD + 16 + per * j
-            gout_ref[per * c:per * (c + 1), lanes * j:lanes * (j + 1)] = all_ref[c, low:low + per, :].astype(jnp.float32)
+        part = all_ref[c, 3 * HEAD:, :].astype(jnp.float32)
+        small = part if small is None else small + part
+    small_ref[...] = small
     for kind in range(3):
         at = slice(HEAD * kind, HEAD * (kind + 1))
         gq_ref[:, HEAD * count * kind:HEAD * count * (kind + 1)] = jnp.concatenate([part[:, at] for part in turned], axis=1)
-    small_ref[...] = jnp.concatenate(smalls, axis=0)
+    for copy in last_copies:
+        copy.wait()
+    gout_ref[...] = out_all[...].astype(jnp.float32).reshape(gout_ref.shape)
     for copy in stores:
         copy.wait()
 
 
-def closing(grads, tokens_all, rows, weight, ghidden, gathered, w_up, w_down, groups, owners):
+def closing(grads, tokens_all, small, gout, weight, ghidden, gathered, w_up, w_down, groups, owners):
     count, width = tokens_all.shape[0], tokens_all.shape[2]
     lanes = width // owners
-    own = (rows.shape[0] - 16) // owners
-    height = 3 * HEAD + 16 + own * (width // lanes)
+    height = 3 * HEAD + small.shape[0]
     own_experts, _, ffn = w_up.shape
     sources = gathered.shape[0]
     view = gathered.reshape(sources, 2, own_experts, groups, width)
     wide = (own_experts, sources * groups, ffn)
     dma = pltpu.SemaphoreType.DMA
-    held = [grads, tokens_all, rows, weight, ghidden, view, w_up, w_down]
+    held = [grads, tokens_all, small, weight, ghidden, view, w_up, w_down]
+    part = (count, lanes // count, width)
     return pl.pallas_call(
         functools.partial(closing_body, owners),
         out_shape=(
             jax.ShapeDtypeStruct(ghidden.shape, jnp.float32),
             jax.ShapeDtypeStruct((lanes, 3 * width), jnp.float32),
             jax.ShapeDtypeStruct((lanes, width), jnp.float32),
-            jax.ShapeDtypeStruct((2 * count, lanes), jnp.float32),
+            jax.ShapeDtypeStruct((small.shape[0], lanes), jnp.float32),
             jax.ShapeDtypeStruct(wide, jnp.bfloat16),
             jax.ShapeDtypeStruct(wide, jnp.bfloat16),
         ),
-        in_specs=[ANY] * 8,
+        in_specs=[ANY] * 9,
         out_specs=(VMEM,) * 4 + (ANY,) * 2,
         scratch_shapes=[pltpu.VMEM(x.shape, x.dtype) for x in held] + [
             pltpu.VMEM(wide, jnp.bfloat16), pltpu.VMEM(wide, jnp.bfloat16), pltpu.VMEM(grads.shape, jnp.bfloat16),
             pltpu.VMEM((owners, height, lanes), jnp.bfloat16), pltpu.VMEM((owners, height, lanes), jnp.bfloat16),
             pltpu.VMEM((height, lanes), jnp.bfloat16), pltpu.VMEM((count, height, lanes), jnp.bfloat16),
-            dma((8,)), dma((1 + 2 * own_experts,)), dma((count - 1,)), dma((count - 1,)), dma((owners - 1,)), dma((owners - 1,)),
-            dma((count - 1,)), dma((count - 1,)),
+            pltpu.VMEM(gout.shape, jnp.bfloat16), pltpu.VMEM(part, jnp.bfloat16), pltpu.VMEM(part, jnp.bfloat16),
+            pltpu.VMEM(part[1:], jnp.bfloat16), pltpu.VMEM(part, jnp.bfloat16),
+            dma((8,)), dma((2 + 2 * own_experts,)), dma((count - 1,)), dma((count - 1,)), dma((owners - 1,)), dma((owners - 1,)),
+            dma((count - 1,)), dma((count - 1,)), dma((3, count - 1)), dma((3, count - 1)),
         ],
         compiler_params=pltpu.CompilerParams(collective_id=6, has_side_effects=True, vmem_limit_bytes=LIMIT),
-        cost_estimate=cost(24),
+        cost_estimate=cost(28),
         name="closing",
-    )(*held)
+    )(*held[:3], gout, *held[3:])
 
 
 def expert_grad_body(mixed_ref, grad_ref, act_ref, gpre_ref, gup_ref, gdown_ref):
@@ -1049,23 +1042,16 @@
         [w_router.T, ln_gain[None], ln_bias[None], jnp.zeros((16 - experts - 2, shard), jnp.bfloat16)], axis=0
     )
     tokens_all, head_weights, out_full, pack_full = gather(tok_rows, [head_cols, w_out, pack], ctx_count, z_count)
-    qkv_full = lax.all_gather(w_qkv, "fsdp", axis=0, tiled=True)
+    later, tokens_all = lax.optimization_barrier((w_qkv, tokens_all))
+    qkv_full = lax.all_gather(later, "fsdp", axis=0, tiled=True)
     att, *saved = attn_fwd(tokens_all.reshape(ctx_count * rows, width), head_weights, block_table, segs)
-    att = exchange(att, "ctx", 2, "exchange_attended")
-    hidden, normed, mix, attended, mixed = mix_tokens(
-        att, tok_rows, cot_rows, out_full, pack_full, group_ids, experts, groups, z_count
-    )
-    got = exchange(mixed, "fsdp", 3, "exchange_mixed")
-    back = exchange(run_experts(got, w_up, w_down, groups), "fsdp", 4, "exchange_back")
-    gathered = lax.all_gather(got, "ctx", axis=0, tiled=True)
-    layer_out, grad_hidden, part_rows, grad_heads = unmix_tokens(
-        hidden, normed, mix, attended, cot_rows, out_full, pack_full, back, experts, groups, ctx_count
-    )
-    grad_heads = exchange(grad_heads, "ctx", 5, "exchange_grad")
-    sum_rows = lax.psum_scatter(part_rows.reshape(-1, width), "ctx", scatter_dimension=0, tiled=True)
+    layer_out, grad_hidden, gout, small, gathered, grad_heads = middle(
+        att, tok_rows, cot_rows, out_full, pack_full, group_ids, w_up, w_down, qkv_full, experts, groups
+    )
+    gathered = gathered.reshape((ctx_count * z_count,) + gathered.shape[2:])
     grads = attn_bwd(grad_heads, saved, block_table, segs)
     grad_tokens, grad_qkv, grad_out, small, active, grad_pre = closing(
-        grads, tokens_all, sum_rows, qkv_full, grad_hidden, gathered, w_up, w_down, groups, z_count
+        grads, tokens_all, small, gout, qkv_full, grad_hidden, gathered, w_up, w_down, groups, z_count
     )
     grad_up, grad_down = expert_grads(gathered, active, grad_pre, groups)
     return (

time: 245 us -> 220 us (0.90)
  waiting for transfers between devices: 14.7 us -> 0.03 us
  Pallas kernels: 203 us -> 193 us
    all_gather x2 -> x1, waiting for transfers between devices: 13.8 us -> 0.01 us  [fast_device(): qkv_full = lax.all_gather(later, 'fsdp', axis=0, tiled=True)]
    pallas_call x7 -> x1, Pallas kernels: 52.8 us -> 39.7 us  [middle(): pl.pallas_call(functools.partial(middle_body, experts, groups), out_shape...]
    pallas_call x1, Pallas kernels: 30.1 us -> 34.1 us  [closing(): pl.pallas_call(functools.partial(closing_body, owners), out_shape=(jax.Sh...]
    unnamed x11 -> x16, local copies, waits for them, and re-layouts: 4.29 us -> 5.27 us
  transfers between devices with their start and end apart: 3 -> 1, of which waited for: 1 -> 0; matrix products, arithmetic and copies ran while one was open for 0% -> 1% of each run, Pallas kernels for 21% -> 16%
where the time goes in v3:
time: 220 us; the launch traced here: 218 us
  Pallas kernels  193 us (88%)
  between operations  14.1 us (6%)
  local copies, waits for them, and re-layouts  9.25 us (4%)
    pallas_call x1, Pallas kernels, attn_bwd(): pl.pallas_call(functools.partial(bwd_body, blocks, block_len), out_shape=...  42.5 us
    pallas_call x1, Pallas kernels, middle(): pl.pallas_call(functools.partial(middle_body, experts, groups), out_shape...  39.7 us
    pallas_call x1, Pallas kernels, attn_fwd(): pl.pallas_call(functools.partial(fwd_body, blocks, block_len), out_shape=...  34.3 us
    pallas_call x1, Pallas kernels, closing(): pl.pallas_call(functools.partial(closing_body, owners), out_shape=(jax.Sh...  34.1 us
    pallas_call x1, Pallas kernels, gather(): pl.pallas_call(functools.partial(gather_body, z_count), out_shape=outs, i...  28.6 us
    pallas_call x1, Pallas kernels, expert_grads(): pl.pallas_call(expert_grad_body, grid=(own, ffn // step), out_shape=(jax....  13.3 us
    unnamed x16, local copies, waits for them, and re-layouts  5.27 us
  transfers between devices with their start and end apart: 1, of which 0 were waited for; matrix products, arithmetic and copies ran while one was open for 1% of the time, Pallas kernels for 16%

profile of v3, /device:TPU:0, one launch (start us, length us, event | category | flops | bytes accessed | tf_op | source)
XLA Modules:
  0.0 218.0 jit_solution(8008239656533343041)
XLA Ops:
  7.2 0.0 all-gather.2.cloned.1.call-start
  7.2 1.2 copy.22
  8.5 0.7 copy.23.refs_0_
  9.2 0.1 pad.3.clone
  9.3 1.4 maximum_maximum_fusion.refs_2_
  10.7 0.0 copy-start.4
  10.7 28.6 %gather_tokens.1 = (bf16[8,512,512]{2,1,0:T(8,128)(2,1)}, bf16[4,128,192]{2,1,0:T(8,128)(2,1)}, bf16[4,128,512]{2,1,0:T(8,128)(2,1)}, bf16[4,16,128]{2,1,0:T(8,128)(2,1)}) custom-call(bf16[512,512]{1,0:T(8,128)(2,1)} %bitcast.24, bf16[128,192]{1,0:T(8,128)(2,1)} %copy.23.refs_0_, bf16[128,512]{1,0:T(8,128)(2,1)} %refs_1_.1, ...), custom_call_target="tpu_custom_call" | custom-call | flops 27599998976 | bytes 1048576 | tf_op jit(solution)/shard_map/gather_tokens/pallas_call | solution.py:629
  39.3 0.0 all-gather.2.cloned.1.call-update
  39.3 0.5 broadcast.5
  39.8 0.0 copy-done.4
  39.8 0.7 reduce.3
  40.5 0.6 reshape_squeeze.3.seg_ref.segrow_ref
  41.1 34.3 %attention.1 = (bf16[8,256,128]{2,1,0:T(8,128)(2,1)}, bf16[4096,256]{1,0:T(8,128)(2,1)}, bf16[4096,256]{1,0:T(8,128)(2,1)}, bf16[4096,128]{1,0:T(8,128)(2,1)}, b...) custom-call(s32[16]{0:T(128)} %table_ref.3, s32[16,256]{1,0:T(8,128)} %reshape_squeeze.3.seg_ref.segrow_ref, ...), custom_call_target="tpu_custom_call" | custom-call | flops 40249999360 | bytes 1048576 | tf_op jit(solution)/shard_map/attention/pallas_call | solution.py:414
  75.4 0.0 all-gather.2.cloned.1.call-done.later_ref.weight_ref
  75.4 39.7 %middle.1 = (f32[512,512]{1,0:T(8,128)}, f32[512,512]{1,0:T(8,128)}, bf16[4,128,512]{2,1,0:T(8,128)(2,1)}, f32[16,512]{1,0:T(8,128)}, bf16[8,4,2,32,512]{4,3,2,1,0:T(8,128)(2,1)}, /*index=5*/bf16[8,256,128]{2,1,0:T(8,128)(2,1)}) custom-call(bf16[8,256,128]{2,1,0:T(8,128)(2,1)} %get-tuple-element.38.att_ref, bf16[512,512]{1,0:T(8,128)(2,1)} %bitcast.25, ...), custom_call_target="tpu_custom_call" | custom-call | flops 40249999360 | bytes 1048576 | tf_op jit(solution)/shard_map/middle/pallas_call | solution.py:787
  115.1 42.5 %attention_grad.1.grads_ref = bf16[8,256,384]{2,1,0:T(8,128)(2,1)} custom-call(s32[16]{0:T(128)} %table_ref.3, s32[16,256]{1,0:T(8,128)} %reshape_squeeze.3.seg_ref.segrow_ref, bf16[8,256,128]{2,1,0:T(8,128)(2,1)} %get-tuple-element.43.do_ref, bf16[4096,256]{1,0:T(8,128)(2,1)} %get-tuple-element.44.qf_ref, bf16[4096,256]{1,0:T(8,128)(2,1)} %get-tuple-element.45.kf_ref, ...), custom_call_target="tpu_custom_call" | custom-call | flops 46000001024 | bytes 1048576 | tf_op jit(solution)/shard_map/attention_grad/pallas_call | solution.py:516
  157.7 34.1 %closing.1 = (f32[512,512]{1,0:T(8,128)}, f32[128,1536]{1,0:T(8,128)}, f32[128,512]{1,0:T(8,128)}, f32[16,128]{1,0:T(8,128)}, bf16[2,512,2048]{2,1,0:T(8,128)(2,1)}, /*index=5*/bf16[2,512,2048]{2,1,0:T(8,128)(2,1)}) custom-call(bf16[8,256,384]{2,1,0:T(8,128)(2,1)} %attention_grad.1.grads_ref, bf16[8,512,512]{2,1,0:T(8,128)(2,1)} %get-tuple-element.36.toks_ref, ...), custom_call_target="tpu_custom_call" | custom-call | flops 32199999488 | bytes 1048576 | tf_op jit(solution)/shard_map/closing/pallas_call | solution.py:974
  191.8 1.3 slice_bitcast_fusion.1
  193.0 1.3 slice_bitcast_fusion
  194.3 0.0 copy-start
  194.3 0.0 copy-start.1
  194.3 13.3 %expert_grads.1 = (f32[2,512,2048]{2,1,0:T(8,128)}, f32[2,2048,512]{2,1,0:T(8,128)}) custom-call(bf16[32,2,2,16,512]{4,3,2,1,0:T(8,128)(2,1)} %bitcast.29, bf16[32,2,2,16,512]{4,3,2,1,0:T(8,128)(2,1)} %bitcast.30, bf16[2,512,2048]{2,1,0:T(8,128)(2,1)} %get-tuple-element.57.act_ref, bf16[2,512,2048]{2,1,0:T(8,128)(2,1)} %get-tuple-element.58.gpre_ref), custom_call_target="tpu_custom_call" | custom-call | flops 9200000000 | bytes 1048576 | tf_op jit(solution)/shard_map/expert_grads/pallas_call | solution.py:1012
  207.6 0.0 copy-start.2
  207.6 0.0 copy-start.3
  207.6 0.0 copy-done
  207.6 1.0 copy.28
  208.6 0.0 copy-done.1
  208.6 1.0 copy.29
  209.6 0.0 copy-done.2
  209.6 0.9 copy.30
  210.5 0.0 copy-done.3
  210.5 0.7 copy.31
  (2 shorter events, 0.0 us)
Async XLA Ops:
  7.2 68.3 %all-gather.2.cloned.1.call-start = ((), (), s32[]{:S(2)}) async-start(), calls=%async_computation | async-start | bytes 1966080 | tf_op jit(solution)/shard_map/all_gather | solution.py:1046
  10.7 29.2 %copy-start.4 = (s32[1,4096]{1,0:T(1,128)S(1)}, s32[1,4096]{1,0:T(1,128)}, u32[]{:S(2)}) copy-start(s32[1,4096]{1,0:T(1,128)} %param.15) | copy-start | bytes 49156
  194.3 13.3 %copy-start = (f32[512,512]{1,0:T(8,128)S(1)}, f32[512,512]{1,0:T(8,128)}, u32[]{:S(2)}) copy-start(f32[512,512]{1,0:T(8,128)} %get-tuple-element.42) | copy-start | bytes 3145732
  194.3 14.3 %copy-start.1 = (f32[512,512]{1,0:T(8,128)S(1)}, f32[512,512]{1,0:T(8,128)}, u32[]{:S(2)}) copy-start(f32[512,512]{1,0:T(8,128)} %get-tuple-element.53) | copy-start | bytes 3145732
  207.6 2.0 copy-start.2
  207.6 2.8 %copy-start.3 = (f32[128,512]{1,0:T(8,128)S(1)}, f32[128,512]{1,0:T(8,128)}, u32[]{:S(2)}) copy-start(f32[128,512]{1,0:T(8,128)} %get-tuple-element.75) | copy-start | bytes 786436
Sparse Core Ops, SparseCore 0:
  39.4 35.2 all-gather.1

commit v4 on v3

--- a/solution.py
+++ b/solution.py
@@ -291,9 +291,15 @@
     )
 
 
+def cost(microseconds):
+    return pl.CostEstimate(flops=int(microseconds * 1.15e9), bytes_accessed=1 << 20, transcendentals=0)
+
+
 LOG2E = 1.4426950408889634
 HIDE = -1e30
-SUPER = 512
+SAFE = 100.0
+RUN = 1024
+HALF = 512
 VMEM = pl.BlockSpec(memory_space=pltpu.VMEM)
 SMEM = pl.BlockSpec(memory_space=pltpu.SMEM)
 ANY = pl.BlockSpec(memory_space=pl.ANY)
@@ -320,221 +326,223 @@
     return one, two, three
 
 
-def read_order(table_ref, seg_ref, inv_ref, first_ref, last_ref, blocks, block_len, per):
+def span(index, size, width=None):
+    return pl.ds(pl.multiple_of(index * size, size), size if width is None else width)
+
+
+def flipped(value):
+    return value.astype(jnp.float32).T.astype(value.dtype)
+
+
+def boundaries(seg_ref, lane):
+    segs = seg_ref[...]
+    begin = jnp.zeros(lane.shape, jnp.int32)
+    end = jnp.zeros(lane.shape, jnp.int32)
+    for c in range(1, 10):
+        below = (segs < c).astype(jnp.int32)
+        total = jnp.sum(jnp.sum(below, axis=1, keepdims=True), axis=0, keepdims=True)
+        begin = jnp.where(lane == HEAD - 1 + c, total, begin)
+        end = jnp.where(lane == HEAD - 2 + c, total, end)
+    return begin, jnp.where(lane == HEAD + 8, 0, end)
+
+
+def fwd_body(blocks, block_len, table_ref, tok_ref, w_ref, seg_ref, att_ref, qf_ref, kf_ref, vf_ref, stat_ref, vt_ref, inv_ref):
+    rows = blocks * block_len
     for t in range(blocks):
         inv_ref[table_ref[t]] = t
-    for s in range(blocks // per):
-        first_ref[s] = seg_ref[inv_ref[s * per], 0]
-        last_ref[s] = seg_ref[inv_ref[s * per + per - 1], block_len - 1]
-
-
-def count_below(ref, limit, n):
-    total = jnp.int32(0)
-    for s in range(n):
-        total = total + (ref[s] < limit).astype(jnp.int32)
-    return total
-
-
-def fwd_body(blocks, block_len, table_ref, seg_ref, tok_ref, w_ref, segrow_ref, att_ref, qf_ref, kf_ref, vf_ref, kp_ref, stat_ref,
-             inv_ref, first_ref, last_ref):
-    per = SUPER // block_len
-    runs = blocks // per
-    read_order(table_ref, seg_ref, inv_ref, first_ref, last_ref, blocks, block_len, per)
     weight = w_ref[...].reshape(w_ref.shape[0] * w_ref.shape[1], w_ref.shape[2])
-    factor = HEAD ** (-0.5) * LOG2E
-    ids = lax.broadcasted_iota(jnp.int32, (8, 1), 0) + 1
-    eye = (lax.broadcasted_iota(jnp.int32, (8, HEAD), 0) == lax.broadcasted_iota(jnp.int32, (8, HEAD), 1)).astype(jnp.bfloat16)
-    lane = lax.broadcasted_iota(jnp.int32, (block_len, HEAD), 1)
-    ones_k = ((lane >= 8) & (lane < 11)).astype(jnp.float32)
-    ones_v = (lane < 3).astype(jnp.bfloat16)
-
-    def project(s, carry):
+    weight = jnp.concatenate([weight, jnp.zeros((weight.shape[0], HEAD), weight.dtype)], axis=1)
+    lane = lax.broadcasted_iota(jnp.int32, (1, 2 * HEAD), 1)
+    begin, end = boundaries(seg_ref, lane)
+    is_flag = (lane >= HEAD) & (lane < HEAD + 8)
+    is_one = (lane >= HEAD + 8) & (lane < HEAD + 11)
+    pair = (lax.broadcasted_iota(jnp.int32, (2 * HEAD, 2 * HEAD), 0) // HEAD == lane // HEAD).astype(jnp.bfloat16)
+    ones_v = ((lane >= HEAD) & (lane < HEAD + 3)).astype(jnp.float32)
+
+    def project(s, sizes):
         t = inv_ref[s]
-        rows = tok_ref[pl.ds(pl.multiple_of(t * block_len, block_len), block_len), :]
-        qkv = dot_nn(rows, weight).astype(jnp.bfloat16)
-        q, k, v = qkv[:, :HEAD], qkv[:, HEAD:2 * HEAD], qkv[:, 2 * HEAD:]
-        one, two, three = split3(k.astype(jnp.float32) * factor)
-        same = segrow_ref[pl.ds(t, 1), :] == ids
-        other = dot_tn(jnp.where(same, 0.0, 1.0).astype(jnp.bfloat16), eye).astype(jnp.bfloat16)
-        hidden = (dot_tn(jnp.where(same, HIDE, 0.0).astype(jnp.bfloat16), eye) + ones_k).astype(jnp.bfloat16)
-        at = pl.ds(pl.multiple_of(s * block_len, block_len), block_len)
-        qf_ref[at, :] = jnp.concatenate([q, q, q, other], axis=1)
-        kf_ref[at, :] = jnp.concatenate([one, two, three, hidden], axis=1)
-        vf_ref[at, :] = jnp.concatenate([v, ones_v], axis=1)
-        kp_ref[at, :] = jnp.concatenate([k, k], axis=1)
-        return carry
-
-    lax.fori_loop(0, blocks, project, 0)
-    start_hidden = count_below(first_ref, 1, runs)
-    row = lax.broadcasted_iota(jnp.int32, (SUPER, SUPER), 0)
-    col = lax.broadcasted_iota(jnp.int32, (SUPER, SUPER), 1)
-    causal = col <= row
-
-    def query_run(run, carry):
-        at_q = pl.ds(pl.multiple_of(run * SUPER, SUPER), SUPER)
-        query = qf_ref[at_q, :]
-        skip = jnp.maximum(count_below(last_ref, first_ref[run], runs) - start_hidden, 0)
-
-        def tile(index, diagonal, state):
-            top, acc = state
-            at_k = pl.ds(pl.multiple_of(index * SUPER, SUPER), SUPER)
-            scores = dot_nt(query, kf_ref[at_k, :])
+        qkv = dot_nn(tok_ref[span(t, block_len), :], weight)
+        both = qkv[:, :2 * HEAD].astype(jnp.bfloat16).astype(jnp.float32)
+        turned = pltpu.roll(both, HEAD, 1)
+        value = qkv[:, 2 * HEAD:]
+        place = lax.broadcasted_iota(jnp.int32, (block_len, 2 * HEAD), 0) + s * block_len
+        own = (place >= begin) & (place < end)
+        at = span(s, block_len)
+        flag_q = jnp.where(is_flag & jnp.logical_not(own), 1.0, 0.0)
+        flag_k = jnp.where(own, HIDE, jnp.where(is_one, 1.0, 0.0))
+        qf_ref[at, :] = jnp.where(lane < HEAD, both, flag_q).astype(jnp.bfloat16)
+        kf_ref[at, :] = jnp.where(lane < HEAD, turned, flag_k).astype(jnp.bfloat16)
+        vf_ref[at, :] = (value + ones_v).astype(jnp.bfloat16)
+        vt_ref[:, at] = jnp.where(lane < HEAD, value, 1.0).T.astype(jnp.bfloat16)
+        return jnp.maximum(sizes, dot_nn((both * both).astype(jnp.bfloat16), pair))
+
+    sizes = lax.fori_loop(0, blocks, project, jnp.zeros((block_len, 2 * HEAD), jnp.float32), unroll=4)
+    scale = HEAD ** (-0.5) * LOG2E
+    q_size, k_size = jnp.max(sizes[:, :HEAD]), jnp.max(sizes[:, HEAD:])
+    small = q_size * k_size <= (SAFE / scale) ** 2
+    causal = lax.broadcasted_iota(jnp.int32, (HALF, HALF), 0) <= lax.broadcasted_iota(jnp.int32, (HALF, HALF), 1)
+
+    def query_run(online, run):
+        def tile(state, q_at, k_at, diagonal):
+            scores = dot_nt(kf_ref[k_at, :], qf_ref[q_at, :]) * scale
             if diagonal:
                 scores = jnp.where(causal, scores, HIDE)
-            new_top = jnp.maximum(top, jnp.max(scores, axis=1, keepdims=True))
-            weights = jnp.exp2(scores - new_top)
-            acc = acc * jnp.exp2(top - new_top) + dot_nn(weights.astype(jnp.bfloat16), vf_ref[at_k, :])
-            return new_top, acc
-
-        def step(n, state):
-            return tile(jnp.where(n < start_hidden, n, n + skip), False, state)
-
-        state = (jnp.full((SUPER, 1), HIDE, jnp.float32), jnp.zeros((SUPER, 2 * HEAD), jnp.float32))
-        state = lax.fori_loop(0, run - skip, step, state)
-        top, acc = tile(run, True, state)
-        total = acc[:, HEAD:HEAD + 1]
-        lse = top + jnp.log2(total)
-        out = acc[:, :HEAD] / total
-        stat_ref[at_q, :] = jnp.concatenate([out, jnp.broadcast_to(lse, (SUPER, HEAD))], axis=1)
-        return carry
-
-    lax.fori_loop(0, runs, query_run, 0)
+            top, acc = state
+            if online:
+                new_top = jnp.maximum(top, jnp.max(scores, axis=0, keepdims=True))
+                acc = acc * jnp.exp2(top - new_top)
+                scores, top = scores - new_top, new_top
+            return top, acc + dot_nn(vt_ref[:, k_at], jnp.exp2(scores).astype(jnp.bfloat16))
+
+        start = (jnp.full((1, RUN), HIDE if online else 0.0, jnp.float32), jnp.zeros((2 * HEAD, RUN), jnp.float32))
+        whole = lax.fori_loop(0, run, lambda n, state: tile(state, span(run, RUN), span(n, RUN), False), start)
+        early, late = span(2 * run, HALF), span(2 * run + 1, HALF)
+        first = tile([part[:, :HALF] for part in whole], early, early, True)
+        second = tile([part[:, HALF:] for part in whole], late, early, False)
+        second = tile(second, late, late, True)
+        for at, (top, acc) in ((early, first), (late, second)):
+            total = acc[HEAD:]
+            stat = jnp.concatenate([acc[:HEAD] / total, top + jnp.log2(total)], axis=0).T
+            stat_ref[at, :] = stat
+            one, two, three = split3(stat * (-1.0 / scale))
+            old = qf_ref[at, :]
+            old = jnp.where(lane == HEAD + 8, one, old)
+            old = jnp.where(lane == HEAD + 9, two, old)
+            qf_ref[at, :] = jnp.where(lane == HEAD + 10, three, old)
+
+    for online in (False, True):
+        @pl.when(small != online)
+        def _():
+            @pl.loop(0, rows // RUN)
+            def _(run):
+                query_run(online, run)
+
     for c in range(blocks // 2):
-        parts = []
-        for half in range(2):
-            s = table_ref[2 * c + half]
-            parts.append(stat_ref[pl.ds(pl.multiple_of(s * block_len, block_len), block_len), :HEAD])
+        parts = [stat_ref[span(table_ref[2 * c + half], block_len), :HEAD] for half in range(2)]
         att_ref[c] = jnp.concatenate(parts, axis=1).astype(jnp.bfloat16)
 
 
 def attn_fwd(tokens_all, weight, table, segs):
     rows = tokens_all.shape[0]
     blocks, block_len = segs.shape
-    runs = rows // SUPER
+    low = jnp.bfloat16
     return pl.pallas_call(
         functools.partial(fwd_body, blocks, block_len),
         out_shape=(
-            jax.ShapeDtypeStruct((blocks // 2, block_len, 2 * HEAD), jnp.bfloat16),
-            jax.ShapeDtypeStruct((rows, 4 * HEAD), jnp.bfloat16),
-            jax.ShapeDtypeStruct((rows, 4 * HEAD), jnp.bfloat16),
-            jax.ShapeDtypeStruct((rows, 2 * HEAD), jnp.bfloat16),
-            jax.ShapeDtypeStruct((rows, 2 * HEAD), jnp.bfloat16),
+            jax.ShapeDtypeStruct((blocks // 2, block_len, 2 * HEAD), low),
+            jax.ShapeDtypeStruct((rows, 2 * HEAD), low),
+            jax.ShapeDtypeStruct((rows, 2 * HEAD), low),
+            jax.ShapeDtypeStruct((rows, 2 * HEAD), low),
             jax.ShapeDtypeStruct((rows, 2 * HEAD), jnp.float32),
         ),
-        in_specs=[SMEM, SMEM, VMEM, VMEM, VMEM],
-        out_specs=(VMEM,) * 6,
-        scratch_shapes=[pltpu.SMEM((blocks,), jnp.int32), pltpu.SMEM((runs,), jnp.int32), pltpu.SMEM((runs,), jnp.int32)],
+        in_specs=[SMEM, VMEM, VMEM, VMEM],
+        out_specs=(VMEM,) * 5,
+        scratch_shapes=[pltpu.VMEM((2 * HEAD, rows), low), pltpu.SMEM((blocks,), jnp.int32)],
         compiler_params=pltpu.CompilerParams(vmem_limit_bytes=LIMIT),
-        cost_estimate=cost(35),
+        cost_estimate=cost(30),
         name="attention",
-    )(table, segs, tokens_all, weight, segs)
-
-
-def bwd_body(blocks, block_len, table_ref, seg_ref, do_ref, qf_ref, kf_ref, vf_ref, kp_ref, stat_ref, out_ref,
-             inv_ref, first_ref, last_ref, qs_ref, dof_ref, dq_ref, dk_ref, dv_ref):
-    per = SUPER // block_len
-    runs = blocks // per
-    read_order(table_ref, seg_ref, inv_ref, first_ref, last_ref, blocks, block_len, per)
-    lane = lax.broadcasted_iota(jnp.int32, (block_len, HEAD), 1)
-    zero = jnp.zeros((), jnp.bfloat16)
-
-    def spread(value, offset):
-        one, two, three = (jnp.broadcast_to(part, (block_len, HEAD)) for part in split3(value))
-        out = jnp.where(lane == offset, one, zero)
-        out = jnp.where(lane == offset + 1, two, out)
-        return jnp.where(lane == offset + 2, three, out)
+    )(table, tokens_all, weight, segs)
+
+
+def bwd_body(blocks, block_len, table_ref, do_ref, qf_ref, kf_ref, vf_ref, stat_ref, out_ref,
+             inv_ref, dof_ref, qt_ref, dot_ref, dq_ref, dk_ref, dv_ref):
+    rows = blocks * block_len
+    for t in range(blocks):
+        inv_ref[table_ref[t]] = t
+    lane = lax.broadcasted_iota(jnp.int32, (1, 2 * HEAD), 1)
 
     def prepare(s, carry):
         t = inv_ref[s]
-        at = pl.ds(pl.multiple_of(s * block_len, block_len), block_len)
-        both = do_ref[t // 2]
-        grad = jnp.where(t % 2 == 0, both[:, :HEAD], both[:, HEAD:])
-        stat = stat_ref[at, :]
-        delta = jnp.sum(grad.astype(jnp.float32) * stat[:, :HEAD], axis=1, keepdims=True)
-        dof_ref[at, :] = jnp.concatenate([grad, spread(-delta, 0)], axis=1)
-        old = qf_ref[at, :]
-        tail = jnp.where(lane < 8, old[:, 3 * HEAD:], spread(-stat[:, HEAD:HEAD + 1], 8))
-        qs_ref[at, :] = jnp.concatenate([old[:, :3 * HEAD], tail], axis=1)
-        dq_ref[at, :] = jnp.zeros((block_len, 2 * HEAD), jnp.float32)
+        at = span(s, block_len)
+        both = do_ref[t // 2].astype(jnp.float32)
+        both = jnp.where(t % 2 == 0, both, pltpu.roll(both, HEAD, 1))
+        grad = jnp.where(lane < HEAD, both, 0.0)
+        delta = jnp.sum(grad * stat_ref[at, :], axis=1, keepdims=True)
+        one, two, three = split3(jnp.broadcast_to(-delta, grad.shape))
+        wide = jnp.where(lane == HEAD, one, grad.astype(jnp.bfloat16))
+        wide = jnp.where(lane == HEAD + 1, two, wide)
+        dof_ref[at, :] = jnp.where(lane == HEAD + 2, three, wide)
+        turned = jnp.where(lane < HEAD, both, pltpu.roll(qf_ref[at, :].astype(jnp.float32), HEAD, 1)).T.astype(jnp.bfloat16)
+        dot_ref[:, at] = turned[:HEAD]
+        qt_ref[:, at] = turned[HEAD:]
         return carry
 
-    lax.fori_loop(0, blocks, prepare, 0)
-    causal = lax.broadcasted_iota(jnp.int32, (SUPER, SUPER), 0) <= lax.broadcasted_iota(jnp.int32, (SUPER, SUPER), 1)
-
-    def key_run(run, carry):
-        at_k = pl.ds(pl.multiple_of(run * SUPER, SUPER), SUPER)
-        end = jnp.where(first_ref[run] == 0, runs, count_below(first_ref, last_ref[run] + 1, runs))
-
-        def tile(index, diagonal):
-            at_q = pl.ds(pl.multiple_of(index * SUPER, SUPER), SUPER)
-            scores = dot_nt(kf_ref[at_k, :], qs_ref[at_q, :])
+    lax.fori_loop(0, blocks, prepare, 0, unroll=2)
+    causal = lax.broadcasted_iota(jnp.int32, (HALF, HALF), 1) <= lax.broadcasted_iota(jnp.int32, (HALF, HALF), 0)
+    scale = HEAD ** (-0.5)
+
+    @pl.loop(0, rows // RUN)
+    def _(run):
+        def tile(q_at, k_at, k_low, k_size, diagonal, first_k, first_q):
+            scores = dot_nt(qf_ref[q_at, :], kf_ref[k_at, :]) * (scale * LOG2E)
+            if diagonal:
+                scores = jnp.where(causal, scores, HIDE)
             probs = jnp.exp2(scores)
-            if diagonal:
-                probs = jnp.where(causal, probs, 0.0)
-            slope = dot_nt(vf_ref[at_k, :], dof_ref[at_q, :])
-            grad = (probs * slope).astype(jnp.bfloat16)
-            dv = dot_nn(probs.astype(jnp.bfloat16), dof_ref[at_q, :])
-            dk = dot_nn(grad, qs_ref[at_q, :2 * HEAD])
-            if diagonal:
-                dv_ref[...] = dv
-                dk_ref[...] = dk
+            grad = (probs * dot_nt(dof_ref[q_at, :], vf_ref[k_at, :])).astype(jnp.bfloat16)
+            dv = dot_nn(dot_ref[:, q_at], probs.astype(jnp.bfloat16))
+            dk = dot_nn(qt_ref[:, q_at], grad)
+            dq = dot_nn(grad, kf_ref[k_at, :])
+            at = slice(k_low, k_low + k_size)
+            if first_k:
+                dv_ref[:, at] = dv
+                dk_ref[:, at] = dk
             else:
-                dv_ref[...] += dv
-                dk_ref[...] += dk
-            dq_ref[at_q, :] += dot_tn(grad, kp_ref[at_k, :])
-
-        tile(run, True)
-
-        def step(index, inner):
-            tile(index, False)
-            return inner
-
-        lax.fori_loop(run + 1, end, step, 0)
-        scale = HEAD ** (-0.5)
-        stat_dk = (dk_ref[:, :HEAD] * scale).astype(jnp.bfloat16)
-        stat_dv = dv_ref[:, :HEAD].astype(jnp.bfloat16)
-        stat_dq = (dq_ref[at_k, :HEAD] * scale).astype(jnp.bfloat16)
-        for part in range(per):
-            t = inv_ref[run * per + part]
-            rows = slice(part * block_len, (part + 1) * block_len)
-            pieces = (stat_dq[rows], stat_dk[rows], stat_dv[rows])
+                dv_ref[:, at] += dv
+                dk_ref[:, at] += dk
+            if first_q:
+                @pl.when(run == 0)
+                def _():
+                    dq_ref[q_at, :] = dq
+
+                @pl.when(run != 0)
+                def _():
+                    dq_ref[q_at, :] += dq
+            else:
+                dq_ref[q_at, :] += dq
+
+        early, late = span(2 * run, HALF), span(2 * run + 1, HALF)
+        tile(early, early, 0, HALF, True, True, True)
+        tile(late, early, 0, HALF, False, False, True)
+        tile(late, late, HALF, HALF, True, True, False)
+
+        @pl.loop(run + 1, rows // RUN)
+        def _(index):
+            tile(span(index, RUN), span(run, RUN), 0, RUN, False, False, True)
+
+        dk, dv = (dk_ref[...] * scale).T.astype(jnp.bfloat16), dv_ref[...].T.astype(jnp.bfloat16)
+        dq = (dq_ref[span(run, RUN), :HEAD] * scale).astype(jnp.bfloat16)
+        for part in range(RUN // block_len):
+            t = inv_ref[run * (RUN // block_len) + part]
+            at = slice(part * block_len, (part + 1) * block_len)
             for parity in range(2):
                 @pl.when(t % 2 == parity)
                 def _():
-                    for kind in range(3):
+                    for kind, value in enumerate((dq, dk, dv)):
                         low = kind * 2 * HEAD + parity * HEAD
-                        out_ref[t // 2, :, low:low + HEAD] = pieces[kind]
-        return carry
-
-    lax.fori_loop(0, runs, key_run, 0)
+                        out_ref[t // 2, :, low:low + HEAD] = value[at]
 
 
 def attn_bwd(grad, saved, table, segs):
     blocks, block_len = segs.shape
     rows = blocks * block_len
-    runs = rows // SUPER
+    low, full = jnp.bfloat16, jnp.float32
     return pl.pallas_call(
         functools.partial(bwd_body, blocks, block_len),
-        out_shape=jax.ShapeDtypeStruct((blocks // 2, block_len, 6 * HEAD), jnp.bfloat16),
-        in_specs=[SMEM, SMEM] + [VMEM] * 6,
+        out_shape=jax.ShapeDtypeStruct((blocks // 2, block_len, 6 * HEAD), low),
+        in_specs=[SMEM] + [VMEM] * 5,
         out_specs=VMEM,
         scratch_shapes=[
-            pltpu.SMEM((blocks,), jnp.int32), pltpu.SMEM((runs,), jnp.int32), pltpu.SMEM((runs,), jnp.int32),
-            pltpu.VMEM((rows, 4 * HEAD), jnp.bfloat16), pltpu.VMEM((rows, 2 * HEAD), jnp.bfloat16),
-            pltpu.VMEM((rows, 2 * HEAD), jnp.float32), pltpu.VMEM((SUPER, 2 * HEAD), jnp.float32),
-            pltpu.VMEM((SUPER, 2 * HEAD), jnp.float32),
+            pltpu.SMEM((blocks,), jnp.int32), pltpu.VMEM((rows, 2 * HEAD), low),
+            pltpu.VMEM((HEAD, rows), low), pltpu.VMEM((HEAD, rows), low), pltpu.VMEM((rows, 2 * HEAD), full),
+            pltpu.VMEM((HEAD, RUN), full), pltpu.VMEM((HEAD, RUN), full),
         ],
         compiler_params=pltpu.CompilerParams(vmem_limit_bytes=LIMIT),
-        cost_estimate=cost(40),
+        cost_estimate=cost(35),
         name="attention_grad",
-    )(table, segs, grad, *saved)
+    )(table, grad, *saved)
 
 
 MESH = pl.DeviceIdType.MESH
-
-
-def cost(microseconds):
-    return pl.CostEstimate(flops=int(microseconds * 1.15e9), bytes_accessed=1 << 20, transcendentals=0)
 
 
 def flip(index, bit):
@@ -554,20 +562,21 @@
     )
 
 
-def gather_body(zs, tok_ref, *refs):
-    count = (len(refs) - 9) // 2
-    shards, toks_ref, wholes = refs[:count], refs[count], refs[count + 1:2 * count + 1]
-    own_sem, z_send, z_recv, far_send, near_send, own_recv, diag_recv, near_recv = refs[2 * count + 1:]
+def gather_body(
+    zs, tok_ref, wq_ref, wo_ref, router_ref, gain_ref, bias_ref, toks_ref, heads_ref, wos_ref, packs_ref, parts_ref,
+    head_buf, pack_buf, own_sem, z_send, z_recv, far_send, near_send, own_recv, diag_recv, near_recv,
+):
     me, z = lax.axis_index("ctx"), lax.axis_index("fsdp")
     sib, xn, yn, diag = flip(me, 1), flip(me, 2), flip(me, 4), flip(flip(me, 2), 4)
     z_peers = [lax.rem(z + k, zs) for k in range(1, zs)]
     meet([(sib, z), (xn, z), (yn, z)] + [(me, other) for other in z_peers])
     half = tok_ref.shape[0] // 2
+    count = toks_ref.shape[0]
 
     def part(device, k):
         return toks_ref.at[device, pl.ds(k * half, half)]
 
-    started = []
+    started, locals_ = [], []
 
     def go(copy):
         copy.start()
@@ -578,17 +587,34 @@
         go(push(rows, part(me, k), far_send.at[0, k], own_recv.at[0, k], (xn, z)))
         rows = tok_ref.at[pl.ds((1 - k) * half, half)]
         go(push(rows, part(me, 1 - k), far_send.at[1, 1 - k], own_recv.at[1, 1 - k], (yn, z)))
-    for i, (shard, whole) in enumerate(zip(shards, wholes)):
+
+    def share(i, shard, whole):
         for k, other in enumerate(z_peers):
             go(push(shard, whole.at[z], z_send.at[i, k], z_recv.at[i, k], (me, other)))
+        locals_.append(pltpu.make_async_copy(shard, whole.at[z], own_sem.at[i]))
+        locals_[-1].start()
+
+    depth = wq_ref.shape[0] // count
+    width = wq_ref.shape[1] // 3
+    for h in range(count):
+        @pl.when(me == h)
+        def _():
+            cols = [wq_ref[:, width * kind + HEAD * h:width * kind + HEAD * (h + 1)] for kind in range(3)]
+            head_buf[...] = jnp.concatenate(cols, axis=1)
+
+    share(0, head_buf, heads_ref)
+    share(1, wo_ref, wos_ref)
+    experts = router_ref.shape[1]
+    rows = [router_ref[...].astype(jnp.float32).T, gain_ref[...].astype(jnp.float32), bias_ref[...].astype(jnp.float32)]
+    rows.append(jnp.zeros((pack_buf.shape[0] - experts - 2, pack_buf.shape[1]), jnp.float32))
+    pack_buf[...] = jnp.concatenate(rows, axis=0).astype(jnp.bfloat16)
+    share(2, pack_buf, packs_ref)
+    share(3, wq_ref.at[pl.ds(pl.multiple_of(me * depth, depth), depth)], parts_ref)
     for k in (0, 1):
         rows = tok_ref.at[pl.ds(k * half, half)]
         go(push(rows, part(me, k), near_send.at[0, k], near_recv.at[0, k], (sib, z)))
-    locals_ = [pltpu.make_async_copy(tok_ref, toks_ref.at[me], own_sem.at[0])]
-    for i, (shard, whole) in enumerate(zip(shards, wholes)):
-        locals_.append(pltpu.make_async_copy(shard, whole.at[z], own_sem.at[i + 1]))
-    for copy in locals_:
-        copy.start()
+    locals_.append(pltpu.make_async_copy(tok_ref, toks_ref.at[me], own_sem.at[4]))
+    locals_[-1].start()
 
     def arrived(device, k, sem):
         push(part(device, k), part(device, k), far_send.at[0, 0], sem, (sib, z)).wait_recv()
@@ -612,7 +638,7 @@
     for k in (0, 1):
         for i, device in enumerate((sib, flip(xn, 1), flip(yn, 1), flip(diag, 1))):
             arrived(device, k, near_recv.at[i, k])
-    for i, whole in enumerate(wholes):
+    for i, whole in enumerate((heads_ref, wos_ref, packs_ref, parts_ref)):
         for k in range(zs - 1):
             other = lax.rem(z + zs - 1 - k, zs)
             push(whole.at[other], whole.at[other], z_send.at[i, k], z_recv.at[i, k], (me, other)).wait_recv()
@@ -622,23 +648,35 @@
         copy.wait_send()
 
 
-def gather(tokens, shards, ctx_count, z_count):
-    outs = [jax.ShapeDtypeStruct((ctx_count,) + tokens.shape, tokens.dtype)]
-    outs += [jax.ShapeDtypeStruct((z_count,) + shard.shape, shard.dtype) for shard in shards]
+def gather(tokens, w_qkv, w_out, w_router, ln_gain, ln_bias, ctx_count, z_count):
+    shard, wide = w_qkv.shape
+    low = jnp.bfloat16
+    outs = [
+        (ctx_count,) + tokens.shape, (z_count, shard, 3 * HEAD), (z_count,) + w_out.shape, (z_count, 16, shard),
+        (z_count, shard // ctx_count, wide),
+    ]
     dma = pltpu.SemaphoreType.DMA
     return pl.pallas_call(
         functools.partial(gather_body, z_count),
-        out_shape=outs,
-        in_specs=[ANY] * (1 + len(shards)),
-        out_specs=[ANY] * (1 + len(shards)),
+        out_shape=[jax.ShapeDtypeStruct(out, low) for out in outs],
+        in_specs=[VMEM] * 6,
+        out_specs=[ANY] * 5,
         scratch_shapes=[
-            dma((1 + len(shards),)), dma((len(shards), z_count - 1)), dma((len(shards), z_count - 1)), dma((3, 2)), dma((4, 2)),
-            dma((2, 2)), dma((2,)), dma((4, 2)),
+            pltpu.VMEM((shard, 3 * HEAD), low), pltpu.VMEM((16, shard), low),
+            dma((5,)), dma((4, z_count - 1)), dma((4, z_count - 1)), dma((3, 2)), dma((4, 2)), dma((2, 2)), dma((2,)), dma((4, 2)),
         ],
-        compiler_params=pltpu.CompilerParams(collective_id=1, has_side_effects=True),
+        compiler_params=pltpu.CompilerParams(collective_id=1, has_side_effects=True, vmem_limit_bytes=LIMIT),
         cost_estimate=cost(24),
         name="gather_tokens",
-    )(tokens, *shards)
+    )(tokens, w_qkv, w_out, w_router, ln_gain[None], ln_bias[None])
+
+
+def gelu_parts(value):
+    square = value * value
+    tangent = jnp.tanh(value * (square * (gelu_coef * gelu_cubic) + gelu_coef))
+    half = 0.5 * tangent + 0.5
+    rise = value * (square * (3.0 * gelu_coef * gelu_cubic) + gelu_coef)
+    return value * half, half + half * (1.0 - tangent) * rise
 
 
 def norm_parts(hidden):
@@ -648,10 +686,10 @@
 
 
 def middle_body(
-    experts, groups, att_ref, tok_ref, cot_ref, wo_ref, pack_ref, gid_ref, up_ref, down_ref, later_ref,
-    layer_ref, ghidden_ref, gout_ref, small_ref, all_ref, ghead_ref,
+    experts, groups, att_ref, tok_ref, cot_ref, wo_ref, pack_ref, gid_ref, up_ref, down_ref, wq_ref,
+    layer_ref, ghidden_ref, gout_ref, small_ref, all_ref, ghead_ref, wqs_ref,
     tok, cot, wo, pack, up, down, att, zsend, zin, bsend, bin_, ghead,
-    load_sem, own_sem, a_send, a_recv, m_send, m_recv, b_send, b_recv, g_send, g_recv, r_send, r_recv, h_send, h_recv,
+    load_sem, own_sem, a_send, a_recv, m_send, m_recv, b_send, b_recv, g_send, g_recv, r_send, r_recv, h_send, h_recv, w_send, w_recv, v_send, v_recv,
 ):
     me, z = lax.axis_index("ctx"), lax.axis_index("fsdp")
     count, half = att_ref.shape[0], att_ref.shape[1]
@@ -682,6 +720,9 @@
     own = start([pltpu.make_async_copy(att_ref.at[me], att.at[me], own_sem.at[0])])
     small_in = None
     wait(own + swap)
+    weights = start([push(wq_ref, wqs_ref.at[me], w_send.at[k], w_recv.at[k], (d, z)) for k, d in enumerate(same_core)])
+    shares = start([push(wq_ref, wqs_ref.at[me], v_send.at[3], v_recv.at[3], (sib, z))])
+    own_weight = start([pltpu.make_async_copy(wq_ref, wqs_ref.at[me], own_sem.at[3])])
     wait(loads[:4])
     halves = [jnp.concatenate([att[h, :, HEAD * p:HEAD * (p + 1)] for h in range(count)], axis=1) for p in range(2)]
     attended = jnp.concatenate(halves, axis=0)
@@ -706,9 +747,10 @@
         ])
 
     mixed_copies = to_owners(0, dot_nn(low, normed))
-    grad_copies = to_owners(1, dot_nn(low, cot[...]))
+    grad_experts = dot_nn(low, cot[...])
     wait(loads[4:])
     wait(mixed_copies)
+    grad_copies = to_owners(1, grad_experts)
 
     def from_sources(kind, e):
         return zin[:, kind, e * groups:(e + 1) * groups, :].reshape(owners * groups, width)
@@ -722,21 +764,24 @@
             push(bsend.at[d[1], kind], bin_.at[z, kind], b_send.at[kind, k], b_recv.at[kind, k], d) for k, d in enumerate(z_peers)
         ])
 
-    pres = []
+    slopes = []
     for e in range(own_experts):
         pre = dot_nn(from_sources(0, e), up[e])
-        pres.append(pre)
-        active = jax.nn.gelu(pre, approximate=True).astype(jnp.bfloat16)
-        to_sources(0, e, dot_nn(active, down[e]))
+        active, slope = gelu_parts(pre)
+        slopes.append(slope)
+        to_sources(0, e, dot_nn(active.astype(jnp.bfloat16), down[e]))
     out_copies = send_back(0)
     wait(grad_copies)
     gather_copies = start([push(zin, all_ref.at[me], g_send.at[k], g_recv.at[k], (d, z)) for k, d in enumerate(same_core)])
     relays = start([push(zin, all_ref.at[me], r_send.at[0], r_recv.at[0], (sib, z))])
     own = start([pltpu.make_async_copy(zin, all_ref.at[me], own_sem.at[1])])
     for e in range(own_experts):
-        grad_pre = (dot_nt(from_sources(1, e), down[e]) * gelu_slope(pres[e])).astype(jnp.bfloat16)
+        grad_pre = (dot_nt(from_sources(1, e), down[e]) * slopes[e]).astype(jnp.bfloat16)
         to_sources(1, e, dot_nt(grad_pre, up[e]))
     back_copies = send_back(1)
+    for k, d in enumerate(same_core):
+        weights[k].wait_recv()
+        shares += start([push(wqs_ref.at[d], wqs_ref.at[d], v_send.at[k], v_recv.at[k], (sib, z))])
     wait(out_copies)
     expert_out = bin_[:, 0].reshape(flat, width)
     layer_ref[...] = hidden + dot_tn(low, expert_out)
@@ -773,12 +818,12 @@
         ],
         axis=0,
     )
-    for copy in gather_copies:
+    for copy in gather_copies + weights:
         copy.wait_send()
-    wait(own + last + relays + swap)
-
-
-def middle(att, tokens, cot, w_out, pack, gid_row, w_up, w_down, later, experts, groups):
+    wait(own + own_weight + last + relays + shares + swap)
+
+
+def middle(att, tokens, cot, w_out, pack, gid_row, w_up, w_down, parts, experts, groups):
     rows, width = tokens.shape
     count, owners, own = att.shape[0], pack.shape[0], w_up.shape[0]
     sent = (owners, 2, experts * groups // owners, width)
@@ -793,19 +838,20 @@
             jax.ShapeDtypeStruct((pack.shape[1], width), full),
             jax.ShapeDtypeStruct((count,) + sent, low),
             jax.ShapeDtypeStruct(att.shape, low),
+            jax.ShapeDtypeStruct((count,) + parts.shape, low),
         ),
-        in_specs=[ANY] * 5 + [VMEM] + [ANY] * 3,
-        out_specs=(VMEM,) * 4 + (ANY,) * 2,
+        in_specs=[ANY] * 5 + [VMEM] + [ANY] * 2 + [VMEM],
+        out_specs=(VMEM,) * 4 + (ANY,) * 3,
         scratch_shapes=[pltpu.VMEM(x.shape, x.dtype) for x in (tokens, cot, w_out, pack, w_up, w_down, att)] + [
             pltpu.VMEM(sent, low), pltpu.VMEM(sent, low), pltpu.VMEM(sent, low), pltpu.VMEM(sent, low), pltpu.VMEM(att.shape, low),
-            dma((4 + 2 * own,)), dma((3,)), dma((count - 1,)), dma((count - 1,)), dma((2, owners - 1)), dma((2, owners - 1)),
+            dma((4 + 2 * own,)), dma((4,)), dma((count - 1,)), dma((count - 1,)), dma((2, owners - 1)), dma((2, owners - 1)),
             dma((2, owners - 1)), dma((2, owners - 1)), dma((3,)), dma((3,)), dma((4,)), dma((4,)), dma((count - 1,)),
-            dma((count - 1,)),
+            dma((count - 1,)), dma((3,)), dma((3,)), dma((4,)), dma((4,)),
         ],
         compiler_params=pltpu.CompilerParams(collective_id=2, has_side_effects=True, vmem_limit_bytes=LIMIT),
         cost_estimate=cost(35),
         name="middle",
-    )(att, tokens, cot, w_out, pack, gid_row, w_up, w_down, later)
+    )(att, tokens, cot, w_out, pack, gid_row, w_up, w_down, parts)
 
 
 def head_columns(ref, p, index=None):
@@ -829,8 +875,9 @@
     own_experts, ffn = up_ref.shape[0], up_ref.shape[2]
     pairs = [
         (grads_ref, held_grads), (toks_ref, held_toks), (small_in_ref, held_small), (gathered_ref, held_mixed), (up_ref, held_up),
-        (down_ref, held_down), (weight_ref, held_weight), (ghidden_ref, held_hidden),
+        (down_ref, held_down), (ghidden_ref, held_hidden),
     ]
+    pairs += [(weight_ref.at[c], held_weight.at[:, c]) for c in range(weight_ref.shape[0])]
     loads = [pltpu.make_async_copy(src, dst, load_sem.at[i]) for i, (src, dst) in enumerate(pairs)]
     for copy in loads:
         copy.start()
@@ -880,9 +927,9 @@
         def chunk(i, carry):
             at = pl.ds(pl.multiple_of(i * step, step), step)
             pre = dot_nn(mixed, held_up[own_expert, :, at])
-            act_buf[own_expert, :, at] = jax.nn.gelu(pre, approximate=True).astype(jnp.bfloat16)
-            slope = dot_nt(grad_out, held_down[own_expert, at, :])
-            gpre_buf[own_expert, :, at] = (slope * gelu_slope(pre)).astype(jnp.bfloat16)
+            active, slope = gelu_parts(pre)
+            act_buf[own_expert, :, at] = active.astype(jnp.bfloat16)
+            gpre_buf[own_expert, :, at] = (dot_nt(grad_out, held_down[own_expert, at, :]) * slope).astype(jnp.bfloat16)
             return carry
 
         lax.fori_loop(0, ffn // step, chunk, 0)
@@ -932,15 +979,16 @@
         last_copies.append(push(out_own, out_all.at[me], o_send.at[2, k], o_recv.at[2, k], device))
         last_copies[-1].start()
     out_all[me] = out_own[...]
-    loads[6].wait()
-    loads[7].wait()
+    for copy in loads[6:]:
+        copy.wait()
     own_swap.wait()
     for copy in swaps:
         copy.wait()
+    weight = held_weight[...].reshape(width, -1)
     for p in range(2):
         columns = [landing[h, :, HEAD * (2 * kind + p):HEAD * (2 * kind + p + 1)] for kind in range(3) for h in range(count)]
         at = slice(p * half, (p + 1) * half)
-        gtok_ref[at, :] = held_hidden[at, :] + dot_nt(jnp.concatenate(columns, axis=1), held_weight[...])
+        gtok_ref[at, :] = held_hidden[at, :] + dot_nt(jnp.concatenate(columns, axis=1), weight)
     for copy in c_copies:
         copy.wait()
     small = None
@@ -983,13 +1031,15 @@
         ),
         in_specs=[ANY] * 9,
         out_specs=(VMEM,) * 4 + (ANY,) * 2,
-        scratch_shapes=[pltpu.VMEM(x.shape, x.dtype) for x in held] + [
+        scratch_shapes=[pltpu.VMEM(x.shape, x.dtype) for x in held[:3]]
+        + [pltpu.VMEM((owners, count) + weight.shape[2:], jnp.bfloat16)]
+        + [pltpu.VMEM(x.shape, x.dtype) for x in held[4:]] + [
             pltpu.VMEM(wide, jnp.bfloat16), pltpu.VMEM(wide, jnp.bfloat16), pltpu.VMEM(grads.shape, jnp.bfloat16),
             pltpu.VMEM((owners, height, lanes), jnp.bfloat16), pltpu.VMEM((owners, height, lanes), jnp.bfloat16),
             pltpu.VMEM((height, lanes), jnp.bfloat16), pltpu.VMEM((count, height, lanes), jnp.bfloat16),
             pltpu.VMEM(gout.shape, jnp.bfloat16), pltpu.VMEM(part, jnp.bfloat16), pltpu.VMEM(part, jnp.bfloat16),
             pltpu.VMEM(part[1:], jnp.bfloat16), pltpu.VMEM(part, jnp.bfloat16),
-            dma((8,)), dma((2 + 2 * own_experts,)), dma((count - 1,)), dma((count - 1,)), dma((owners - 1,)), dma((owners - 1,)),
+            dma((7 + count,)), dma((2 + 2 * own_experts,)), dma((count - 1,)), dma((count - 1,)), dma((owners - 1,)), dma((owners - 1,)),
             dma((count - 1,)), dma((count - 1,)), dma((3, count - 1)), dma((3, count - 1)),
         ],
         compiler_params=pltpu.CompilerParams(collective_id=6, has_side_effects=True, vmem_limit_bytes=LIMIT),
@@ -998,70 +1048,85 @@
     )(*held[:3], gout, *held[3:])
 
 
-def expert_grad_body(mixed_ref, grad_ref, act_ref, gpre_ref, gup_ref, gdown_ref):
+def expert_grad_body(experts, passed, mixed_ref, grad_ref, act_ref, gpre_ref, small_ref, *refs):
+    sources, outs = refs[:passed], refs[passed + 5:]
+    gup_ref, gdown_ref, router_ref, gain_ref, bias_ref = refs[passed:passed + 5]
     width = gup_ref.shape[1]
+    for source, out in zip(sources, outs):
+        out[...] = source[...]
+    router_ref[...] = small_ref[:experts].T
+    gain_ref[...] = small_ref[experts:experts + 1]
+    bias_ref[...] = small_ref[experts + 1:experts + 2]
     gup_ref[0] = dot_tn(mixed_ref[...].reshape(-1, width), gpre_ref[0])
     gdown_ref[0] = dot_tn(act_ref[0], grad_ref[...].reshape(-1, width))
 
 
-def expert_grads(gathered, active, grad_pre, groups):
+def expert_grads(gathered, active, grad_pre, small, passed, groups, experts):
     own, rows, ffn = active.shape
     step = 512
+    steps = ffn // step
     sources, width = gathered.shape[0], gathered.shape[3]
     view = gathered.reshape(sources, 2, own, groups, width)
+    lanes = small.shape[1]
+    full = jnp.float32
+    slices = [pl.BlockSpec((x.shape[0] // (own * steps), x.shape[1]), lambda e, f: (e * steps + f, 0)) for x in passed]
     return pl.pallas_call(
-        expert_grad_body,
-        grid=(own, ffn // step),
-        out_shape=(jax.ShapeDtypeStruct((own, width, ffn), jnp.float32), jax.ShapeDtypeStruct((own, ffn, width), jnp.float32)),
+        functools.partial(expert_grad_body, experts, len(passed)),
+        grid=(own, steps),
+        out_shape=[
+            jax.ShapeDtypeStruct((own, width, ffn), full), jax.ShapeDtypeStruct((own, ffn, width), full),
+            jax.ShapeDtypeStruct((lanes, experts), full), jax.ShapeDtypeStruct((1, lanes), full), jax.ShapeDtypeStruct((1, lanes), full),
+        ] + [jax.ShapeDtypeStruct(x.shape, x.dtype) for x in passed],
         in_specs=[
             pl.BlockSpec((sources, 1, 1, groups, width), lambda e, f: (0, 0, e, 0, 0)),
             pl.BlockSpec((sources, 1, 1, groups, width), lambda e, f: (0, 1, e, 0, 0)),
             pl.BlockSpec((1, rows, step), lambda e, f: (e, 0, f)),
             pl.BlockSpec((1, rows, step), lambda e, f: (e, 0, f)),
-        ],
-        out_specs=(pl.BlockSpec((1, width, step), lambda e, f: (e, 0, f)), pl.BlockSpec((1, step, width), lambda e, f: (e, f, 0))),
+            pl.BlockSpec(small.shape, lambda e, f: (0, 0)),
+        ] + slices,
+        out_specs=[
+            pl.BlockSpec((1, width, step), lambda e, f: (e, 0, f)), pl.BlockSpec((1, step, width), lambda e, f: (e, f, 0)),
+            pl.BlockSpec((lanes, experts), lambda e, f: (0, 0)), pl.BlockSpec((1, lanes), lambda e, f: (0, 0)),
+            pl.BlockSpec((1, lanes), lambda e, f: (0, 0)),
+        ] + slices,
         compiler_params=pltpu.CompilerParams(vmem_limit_bytes=LIMIT),
-        cost_estimate=cost(8),
+        cost_estimate=cost(10),
         name="expert_grads",
-    )(view, view, active, grad_pre)
+    )(view, view, active, grad_pre, small, *passed)
 
 
 def fast_device(
     tokens, cotangent, block_table, seg_ids, group_ids, w_qkv, w_out, w_router, ln_gain, ln_bias, w_up, w_down
 ):
     ctx_count, z_count = lax.axis_size("ctx"), lax.axis_size("fsdp")
-    ctx_index = lax.axis_index("ctx")
     tok_rows, cot_rows = tokens[0], cotangent[0]
     rows, width = tok_rows.shape
     experts = w_router.shape[1]
     groups = rows // GROUP_SIZE
-    shard = w_qkv.shape[0]
     segs = seg_ids[0].reshape(block_table.shape[0], -1)
-    head_cols = lax.dynamic_slice_in_dim(w_qkv.reshape(shard, 3, ctx_count, HEAD), ctx_index, 1, 2).reshape(shard, 3 * HEAD)
-    pack = jnp.concatenate(
-        [w_router.T, ln_gain[None], ln_bias[None], jnp.zeros((16 - experts - 2, shard), jnp.bfloat16)], axis=0
-    )
-    tokens_all, head_weights, out_full, pack_full = gather(tok_rows, [head_cols, w_out, pack], ctx_count, z_count)
-    later, tokens_all = lax.optimization_barrier((w_qkv, tokens_all))
-    qkv_full = lax.all_gather(later, "fsdp", axis=0, tiled=True)
+    tokens_all, head_weights, out_full, pack_full, qkv_parts = gather(
+        tok_rows, w_qkv, w_out, w_router, ln_gain, ln_bias, ctx_count, z_count
+    )
     att, *saved = attn_fwd(tokens_all.reshape(ctx_count * rows, width), head_weights, block_table, segs)
-    layer_out, grad_hidden, gout, small, gathered, grad_heads = middle(
-        att, tok_rows, cot_rows, out_full, pack_full, group_ids, w_up, w_down, qkv_full, experts, groups
+    layer_out, grad_hidden, gout, small, gathered, grad_heads, qkv_full = middle(
+        att, tok_rows, cot_rows, out_full, pack_full, group_ids, w_up, w_down, qkv_parts, experts, groups
     )
     gathered = gathered.reshape((ctx_count * z_count,) + gathered.shape[2:])
     grads = attn_bwd(grad_heads, saved, block_table, segs)
     grad_tokens, grad_qkv, grad_out, small, active, grad_pre = closing(
         grads, tokens_all, small, gout, qkv_full, grad_hidden, gathered, w_up, w_down, groups, z_count
     )
-    grad_up, grad_down = expert_grads(gathered, active, grad_pre, groups)
+    grad_up, grad_down, grad_router, grad_gain, grad_bias, layer_out, grad_tokens, grad_qkv, grad_out = expert_grads(
+        gathered, active, grad_pre, small, [layer_out, grad_tokens, grad_qkv, grad_out], groups, experts
+    )
     return (
         layer_out[None],
         grad_tokens[None],
         grad_qkv,
         grad_out,
-        small[:experts].T,
-        small[experts],
-        small[experts + 1],
+        grad_router,
+        grad_gain[0],
+        grad_bias[0],
         grad_up,
         grad_down,
     )

time: 220 us -> 189 us (0.86)
  between operations: 14.1 us -> 0.68 us
  Pallas kernels: 193 us -> 182 us
  local copies, waits for them, and re-layouts: 9.25 us -> 4.02 us
    pallas_call x1, Pallas kernels: 34.3 us -> 25.8 us  [attn_fwd(): pl.pallas_call(functools.partial(fwd_body, blocks, block_len), out_shape=...]
    pallas_call x1, Pallas kernels: 42.5 us -> 36.9 us  [attn_bwd(): pl.pallas_call(functools.partial(bwd_body, blocks, block_len), out_shape=...]
    pallas_call x2, Pallas kernels: 41.9 us -> 44.3 us  [the longest x1 28.9 us: gather(): pl.pallas_call(functools.partial(gather_body, z_count), out_shape=[jax.Sh...]
    unnamed x16 -> x3, local copies, waits for them, and re-layouts: 5.27 us -> 3.41 us
  transfers between devices with their start and end apart: 1 -> 0, of which waited for: 0 -> 0; matrix products, arithmetic and copies ran while one was open for 1% -> 0% of each run, Pallas kernels for 16% -> 0%
where the time goes in v4:
time: 189 us
  Pallas kernels  182 us (96%)
  local copies, waits for them, and re-layouts  4.02 us (2%)
    pallas_call x1, Pallas kernels, middle(): pl.pallas_call(functools.partial(middle_body, experts, groups), out_shape...  41.5 us
    pallas_call x1, Pallas kernels, attn_bwd(): pl.pallas_call(functools.partial(bwd_body, blocks, block_len), out_shape=...  36.9 us
    pallas_call x1, Pallas kernels, closing(): pl.pallas_call(functools.partial(closing_body, owners), out_shape=(jax.Sh...  34 us
    pallas_call x1, Pallas kernels, gather(): pl.pallas_call(functools.partial(gather_body, z_count), out_shape=[jax.Sh...  28.9 us
    pallas_call x1, Pallas kernels, attn_fwd(): pl.pallas_call(functools.partial(fwd_body, blocks, block_len), out_shape=...  25.8 us
    pallas_call x1, Pallas kernels, expert_grads(): pl.pallas_call(functools.partial(expert_grad_body, experts, len(passed)),...  15.4 us

profile of v4, /device:TPU:0, one launch (start us, length us, event | category | flops | bytes accessed | tf_op | source)
XLA Modules:
  0.0 188.6 jit_solution(12483650150995933863)
XLA Ops:
  0.6 0.5 broadcast.3
  1.2 1.4 reduce.3
  2.6 0.6 reshape_squeeze.3.seg_ref
  3.2 1.4 copy.21.router_ref
  4.6 28.9 %gather_tokens.1 = (bf16[8,512,512]{2,1,0:T(8,128)(2,1)}, bf16[4,128,192]{2,1,0:T(8,128)(2,1)}, bf16[4,128,512]{2,1,0:T(8,128)(2,1)}, bf16[4,16,128]{2,1,0:T(8,128)(2,1)}, bf16[4,16,1536]{2,1,0:T(8,128)(2,1)}) custom-call(bf16[512,512]{1,0:T(8,128)(2,1)} %bitcast.10, bf16[128,1536]{1,0:T(8,128)(2,1)} %wq_ref.1, bf16[128,512]{1,0:T(8,128)(2,1)} %wo_ref.1, ...), custom_call_target="tpu_custom_call" | custom-call | flops 27599998976 | bytes 1048576 | tf_op jit(solution)/shard_map/gather_tokens/pallas_call | solution.py:659
  33.5 25.8 %attention.1 = (bf16[8,256,128]{2,1,0:T(8,128)(2,1)}, bf16[4096,128]{1,0:T(8,128)(2,1)}, bf16[4096,128]{1,0:T(8,128)(2,1)}, bf16[4096,128]{1,0:T(8,128)(2,1)}, f32[4096,128]{1,0:T(8,128)}) custom-call(s32[16]{0:T(128)} %table_ref.3, bf16[4096,512]{1,0:T(8,128)(2,1)} %bitcast.15, bf16[4,128,192]{2,1,0:T(8,128)(2,1)} %get-tuple-element.42.w_ref, ...), custom_call_target="tpu_custom_call" | custom-call | flops 34500001792 | bytes 1048576 | tf_op jit(solution)/shard_map/attention/pallas_call | solution.py:429
  59.2 41.5 %middle.1 = (f32[512,512]{1,0:T(8,128)}, f32[512,512]{1,0:T(8,128)}, bf16[4,128,512]{2,1,0:T(8,128)(2,1)}, f32[16,512]{1,0:T(8,128)}, bf16[8,4,2,32,512]{4,3,2,1...) custom-call(bf16[8,256,128]{2,1,0:T(8,128)(2,1)} %get-tuple-element.43.att_ref, ...), custom_call_target="tpu_custom_call" | custom-call | flops 40249999360 | bytes 1048576 | tf_op jit(solution)/shard_map/middle/pallas_call | solution.py:832
  100.8 36.9 %attention_grad.1.grads_ref = bf16[8,256,384]{2,1,0:T(8,128)(2,1)} custom-call(s32[16]{0:T(128)} %table_ref.3, bf16[8,256,128]{2,1,0:T(8,128)(2,1)} %get-tuple-element.48.do_ref, bf16[4096,128]{1,0:T(8,128)(2,1)} %get-tuple-element.49.qf_ref, bf16[4096,128]{1,0:T(8,128)(2,1)} %get-tuple-element.50.kf_ref, bf16[4096,128]{1,0:T(8,128)(2,1)} %get-tuple-element.51.vf_ref, ...), custom_call_target="tpu_custom_call" | custom-call | flops 40249999360 | bytes 1048576 | tf_op jit(solution)/shard_map/attention_grad/pallas_call | solution.py:529
  137.7 34.0 %closing.1 = (f32[512,512]{1,0:T(8,128)}, f32[128,1536]{1,0:T(8,128)}, f32[128,512]{1,0:T(8,128)}, f32[16,128]{1,0:T(8,128)}, bf16[2,512,2048]{2,1,0:T(8,128)(2,1)}, /*index=5*/bf16[2,512,2048]{2,1,0:T(8,128)(2,1)}) custom-call(bf16[8,256,384]{2,1,0:T(8,128)(2,1)} %attention_grad.1.grads_ref, bf16[8,512,512]{2,1,0:T(8,128)(2,1)} %get-tuple-element.41.toks_ref, ...), custom_call_target="tpu_custom_call" | custom-call | flops 32199999488 | bytes 1048576 | tf_op jit(solution)/shard_map/closing/pallas_call | solution.py:1022
  171.7 15.4 %expert_grads.1 = (f32[2,512,2048]{2,1,0:T(8,128)}, f32[2,2048,512]{2,1,0:T(8,128)}, f32[128,8]{1,0:T(8,128)}, f32[1,128]{1,0:T(1,128)}, f32[1,128]{1,0:T(1,128)...) custom-call(bf16[32,2,2,16,512]{4,3,2,1,0:T(8,128)(2,1)} %bitcast.17, ...), custom_call_target="tpu_custom_call" | custom-call | flops 11500000256 | bytes 1048576 | tf_op jit(solution)/shard_map/expert_grads/pallas_call | solution.py:1073
  187.1 1.5 copy.22

commit v5 on v4

--- a/solution.py
+++ b/solution.py
@@ -423,8 +423,8 @@
 
 
 def attn_fwd(tokens_all, weight, table, segs):
-    rows = tokens_all.shape[0]
-    blocks, block_len = segs.shape
+    rows, blocks = tokens_all.shape[0], table.shape[0]
+    block_len = rows // blocks
     low = jnp.bfloat16
     return pl.pallas_call(
         functools.partial(fwd_body, blocks, block_len),
@@ -444,104 +444,6 @@
     )(table, tokens_all, weight, segs)
 
 
-def bwd_body(blocks, block_len, table_ref, do_ref, qf_ref, kf_ref, vf_ref, stat_ref, out_ref,
-             inv_ref, dof_ref, qt_ref, dot_ref, dq_ref, dk_ref, dv_ref):
-    rows = blocks * block_len
-    for t in range(blocks):
-        inv_ref[table_ref[t]] = t
-    lane = lax.broadcasted_iota(jnp.int32, (1, 2 * HEAD), 1)
-
-    def prepare(s, carry):
-        t = inv_ref[s]
-        at = span(s, block_len)
-        both = do_ref[t // 2].astype(jnp.float32)
-        both = jnp.where(t % 2 == 0, both, pltpu.roll(both, HEAD, 1))
-        grad = jnp.where(lane < HEAD, both, 0.0)
-        delta = jnp.sum(grad * stat_ref[at, :], axis=1, keepdims=True)
-        one, two, three = split3(jnp.broadcast_to(-delta, grad.shape))
-        wide = jnp.where(lane == HEAD, one, grad.astype(jnp.bfloat16))
-        wide = jnp.where(lane == HEAD + 1, two, wide)
-        dof_ref[at, :] = jnp.where(lane == HEAD + 2, three, wide)
-        turned = jnp.where(lane < HEAD, both, pltpu.roll(qf_ref[at, :].astype(jnp.float32), HEAD, 1)).T.astype(jnp.bfloat16)
-        dot_ref[:, at] = turned[:HEAD]
-        qt_ref[:, at] = turned[HEAD:]
-        return carry
-
-    lax.fori_loop(0, blocks, prepare, 0, unroll=2)
-    causal = lax.broadcasted_iota(jnp.int32, (HALF, HALF), 1) <= lax.broadcasted_iota(jnp.int32, (HALF, HALF), 0)
-    scale = HEAD ** (-0.5)
-
-    @pl.loop(0, rows // RUN)
-    def _(run):
-        def tile(q_at, k_at, k_low, k_size, diagonal, first_k, first_q):
-            scores = dot_nt(qf_ref[q_at, :], kf_ref[k_at, :]) * (scale * LOG2E)
-            if diagonal:
-                scores = jnp.where(causal, scores, HIDE)
-            probs = jnp.exp2(scores)
-            grad = (probs * dot_nt(dof_ref[q_at, :], vf_ref[k_at, :])).astype(jnp.bfloat16)
-            dv = dot_nn(dot_ref[:, q_at], probs.astype(jnp.bfloat16))
-            dk = dot_nn(qt_ref[:, q_at], grad)
-            dq = dot_nn(grad, kf_ref[k_at, :])
-            at = slice(k_low, k_low + k_size)
-            if first_k:
-                dv_ref[:, at] = dv
-                dk_ref[:, at] = dk
-            else:
-                dv_ref[:, at] += dv
-                dk_ref[:, at] += dk
-            if first_q:
-                @pl.when(run == 0)
-                def _():
-                    dq_ref[q_at, :] = dq
-
-                @pl.when(run != 0)
-                def _():
-                    dq_ref[q_at, :] += dq
-            else:
-                dq_ref[q_at, :] += dq
-
-        early, late = span(2 * run, HALF), span(2 * run + 1, HALF)
-        tile(early, early, 0, HALF, True, True, True)
-        tile(late, early, 0, HALF, False, False, True)
-        tile(late, late, HALF, HALF, True, True, False)
-
-        @pl.loop(run + 1, rows // RUN)
-        def _(index):
-            tile(span(index, RUN), span(run, RUN), 0, RUN, False, False, True)
-
-        dk, dv = (dk_ref[...] * scale).T.astype(jnp.bfloat16), dv_ref[...].T.astype(jnp.bfloat16)
-        dq = (dq_ref[span(run, RUN), :HEAD] * scale).astype(jnp.bfloat16)
-        for part in range(RUN // block_len):
-            t = inv_ref[run * (RUN // block_len) + part]
-            at = slice(part * block_len, (part + 1) * block_len)
-            for parity in range(2):
-                @pl.when(t % 2 == parity)
-                def _():
-                    for kind, value in enumerate((dq, dk, dv)):
-                        low = kind * 2 * HEAD + parity * HEAD
-                        out_ref[t // 2, :, low:low + HEAD] = value[at]
-
-
-def attn_bwd(grad, saved, table, segs):
-    blocks, block_len = segs.shape
-    rows = blocks * block_len
-    low, full = jnp.bfloat16, jnp.float32
-    return pl.pallas_call(
-        functools.partial(bwd_body, blocks, block_len),
-        out_shape=jax.ShapeDtypeStruct((blocks // 2, block_len, 6 * HEAD), low),
-        in_specs=[SMEM] + [VMEM] * 5,
-        out_specs=VMEM,
-        scratch_shapes=[
-            pltpu.SMEM((blocks,), jnp.int32), pltpu.VMEM((rows, 2 * HEAD), low),
-            pltpu.VMEM((HEAD, rows), low), pltpu.VMEM((HEAD, rows), low), pltpu.VMEM((rows, 2 * HEAD), full),
-            pltpu.VMEM((HEAD, RUN), full), pltpu.VMEM((HEAD, RUN), full),
-        ],
-        compiler_params=pltpu.CompilerParams(vmem_limit_bytes=LIMIT),
-        cost_estimate=cost(35),
-        name="attention_grad",
-    )(table, grad, *saved)
-
-
 MESH = pl.DeviceIdType.MESH
 
 
@@ -604,8 +506,8 @@
 
     share(0, head_buf, heads_ref)
     share(1, wo_ref, wos_ref)
-    experts = router_ref.shape[1]
-    rows = [router_ref[...].astype(jnp.float32).T, gain_ref[...].astype(jnp.float32), bias_ref[...].astype(jnp.float32)]
+    experts = router_ref.shape[0]
+    rows = [router_ref[...].astype(jnp.float32), gain_ref[...].astype(jnp.float32), bias_ref[...].astype(jnp.float32)]
     rows.append(jnp.zeros((pack_buf.shape[0] - experts - 2, pack_buf.shape[1]), jnp.float32))
     pack_buf[...] = jnp.concatenate(rows, axis=0).astype(jnp.bfloat16)
     share(2, pack_buf, packs_ref)
@@ -668,7 +570,7 @@
         compiler_params=pltpu.CompilerParams(collective_id=1, has_side_effects=True, vmem_limit_bytes=LIMIT),
         cost_estimate=cost(24),
         name="gather_tokens",
-    )(tokens, w_qkv, w_out, w_router, ln_gain[None], ln_bias[None])
+    )(tokens, w_qkv, w_out, w_router.T, ln_gain[None], ln_bias[None])
 
 
 def gelu_parts(value):
@@ -686,10 +588,10 @@
 
 
 def middle_body(
-    experts, groups, att_ref, tok_ref, cot_ref, wo_ref, pack_ref, gid_ref, up_ref, down_ref, wq_ref,
-    layer_ref, ghidden_ref, gout_ref, small_ref, all_ref, ghead_ref, wqs_ref,
+    experts, groups, att_ref, tok_ref, cot_ref, wo_ref, pack_ref, gid_ref, up_ref, down_ref,
+    layer_ref, ghidden_ref, gout_ref, small_ref, got_ref, ghead_ref,
     tok, cot, wo, pack, up, down, att, zsend, zin, bsend, bin_, ghead,
-    load_sem, own_sem, a_send, a_recv, m_send, m_recv, b_send, b_recv, g_send, g_recv, r_send, r_recv, h_send, h_recv, w_send, w_recv, v_send, v_recv,
+    load_sem, own_sem, a_send, a_recv, m_send, m_recv, b_send, b_recv, h_send, h_recv,
 ):
     me, z = lax.axis_index("ctx"), lax.axis_index("fsdp")
     count, half = att_ref.shape[0], att_ref.shape[1]
@@ -702,7 +604,6 @@
     loads = [pltpu.make_async_copy(src, dst, load_sem.at[i]) for i, (src, dst) in enumerate(pairs)]
     for copy in loads:
         copy.start()
-    sib, same_core = flip(me, 1), [flip(me, 2), flip(me, 4), flip(flip(me, 2), 4)]
     z_peers = [(me, lax.rem(z + k, owners)) for k in range(1, owners)]
     c_peers = [(jnp.bitwise_xor(me, k), z) for k in range(1, count)]
     meet(z_peers + c_peers)
@@ -720,9 +621,6 @@
     own = start([pltpu.make_async_copy(att_ref.at[me], att.at[me], own_sem.at[0])])
     small_in = None
     wait(own + swap)
-    weights = start([push(wq_ref, wqs_ref.at[me], w_send.at[k], w_recv.at[k], (d, z)) for k, d in enumerate(same_core)])
-    shares = start([push(wq_ref, wqs_ref.at[me], v_send.at[3], v_recv.at[3], (sib, z))])
-    own_weight = start([pltpu.make_async_copy(wq_ref, wqs_ref.at[me], own_sem.at[3])])
     wait(loads[:4])
     halves = [jnp.concatenate([att[h, :, HEAD * p:HEAD * (p + 1)] for h in range(count)], axis=1) for p in range(2)]
     attended = jnp.concatenate(halves, axis=0)
@@ -772,16 +670,11 @@
         to_sources(0, e, dot_nn(active.astype(jnp.bfloat16), down[e]))
     out_copies = send_back(0)
     wait(grad_copies)
-    gather_copies = start([push(zin, all_ref.at[me], g_send.at[k], g_recv.at[k], (d, z)) for k, d in enumerate(same_core)])
-    relays = start([push(zin, all_ref.at[me], r_send.at[0], r_recv.at[0], (sib, z))])
-    own = start([pltpu.make_async_copy(zin, all_ref.at[me], own_sem.at[1])])
+    got_ref[...] = zin[...]
     for e in range(own_experts):
         grad_pre = (dot_nt(from_sources(1, e), down[e]) * slopes[e]).astype(jnp.bfloat16)
         to_sources(1, e, dot_nt(grad_pre, up[e]))
     back_copies = send_back(1)
-    for k, d in enumerate(same_core):
-        weights[k].wait_recv()
-        shares += start([push(wqs_ref.at[d], wqs_ref.at[d], v_send.at[k], v_recv.at[k], (sib, z))])
     wait(out_copies)
     expert_out = bin_[:, 0].reshape(flat, width)
     layer_ref[...] = hidden + dot_tn(low, expert_out)
@@ -804,9 +697,6 @@
         ghead[h] = jnp.concatenate([grad_heads[:half, at], grad_heads[half:, at]], axis=1)
     swap = start([push(ghead.at[d[0]], ghead_ref.at[me], h_send.at[k], h_recv.at[k], d) for k, d in enumerate(c_peers)])
     last = start([pltpu.make_async_copy(ghead.at[me], ghead_ref.at[me], own_sem.at[2])])
-    for k, d in enumerate(same_core):
-        gather_copies[k].wait_recv()
-        relays += start([push(all_ref.at[d], all_ref.at[d], r_send.at[k + 1], r_recv.at[k + 1], (sib, z))])
     ghidden_ref[...] = grad_hidden
     gout_ref[...] = dot_tn(attended, branch).astype(jnp.bfloat16).reshape(gout_ref.shape)
     small_ref[...] = jnp.concatenate(
@@ -818,12 +708,10 @@
         ],
         axis=0,
     )
-    for copy in gather_copies + weights:
-        copy.wait_send()
-    wait(own + own_weight + last + relays + shares + swap)
-
-
-def middle(att, tokens, cot, w_out, pack, gid_row, w_up, w_down, parts, experts, groups):
+    wait(last + swap)
+
+
+def middle(att, tokens, cot, w_out, pack, gid_row, w_up, w_down, experts, groups):
     rows, width = tokens.shape
     count, owners, own = att.shape[0], pack.shape[0], w_up.shape[0]
     sent = (owners, 2, experts * groups // owners, width)
@@ -836,216 +724,328 @@
             jax.ShapeDtypeStruct((rows, width), full),
             jax.ShapeDtypeStruct((owners, width // owners, width), low),
             jax.ShapeDtypeStruct((pack.shape[1], width), full),
-            jax.ShapeDtypeStruct((count,) + sent, low),
+            jax.ShapeDtypeStruct(sent, low),
             jax.ShapeDtypeStruct(att.shape, low),
-            jax.ShapeDtypeStruct((count,) + parts.shape, low),
         ),
-        in_specs=[ANY] * 5 + [VMEM] + [ANY] * 2 + [VMEM],
-        out_specs=(VMEM,) * 4 + (ANY,) * 3,
+        in_specs=[ANY] * 5 + [VMEM] + [ANY] * 2,
+        out_specs=(VMEM,) * 5 + (ANY,),
         scratch_shapes=[pltpu.VMEM(x.shape, x.dtype) for x in (tokens, cot, w_out, pack, w_up, w_down, att)] + [
             pltpu.VMEM(sent, low), pltpu.VMEM(sent, low), pltpu.VMEM(sent, low), pltpu.VMEM(sent, low), pltpu.VMEM(att.shape, low),
-            dma((4 + 2 * own,)), dma((4,)), dma((count - 1,)), dma((count - 1,)), dma((2, owners - 1)), dma((2, owners - 1)),
-            dma((2, owners - 1)), dma((2, owners - 1)), dma((3,)), dma((3,)), dma((4,)), dma((4,)), dma((count - 1,)),
-            dma((count - 1,)), dma((3,)), dma((3,)), dma((4,)), dma((4,)),
+            dma((4 + 2 * own,)), dma((3,)), dma((count - 1,)), dma((count - 1,)), dma((2, owners - 1)), dma((2, owners - 1)),
+            dma((2, owners - 1)), dma((2, owners - 1)), dma((count - 1,)), dma((count - 1,)),
         ],
         compiler_params=pltpu.CompilerParams(collective_id=2, has_side_effects=True, vmem_limit_bytes=LIMIT),
         cost_estimate=cost(35),
         name="middle",
-    )(att, tokens, cot, w_out, pack, gid_row, w_up, w_down, parts)
-
-
-def head_columns(ref, p, index=None):
-    columns = []
-    for kind in range(3):
-        at = slice(HEAD * (2 * kind + p), HEAD * (2 * kind + p + 1))
-        columns.append(ref[index, :, at])
-    return jnp.concatenate(columns, axis=1)
-
-
-def closing_body(
-    owners, grads_ref, toks_ref, small_in_ref, out_ref, weight_ref, ghidden_ref, gathered_ref, up_ref, down_ref,
-    gtok_ref, gq_ref, gout_ref, small_ref, act_ref, gpre_ref,
-    held_grads, held_toks, held_small, held_weight, held_hidden, held_mixed, held_up, held_down, act_buf, gpre_buf,
-    landing, zsend, zone, total_ref, all_ref, out_zone, out_sum, out_part, out_own, out_all,
-    load_sem, store_sem, a_send, a_recv, z_send, z_recv, c_send, c_recv, o_send, o_recv,
+    )(att, tokens, cot, w_out, pack, gid_row, w_up, w_down)
+
+
+def backward_body(
+    table_ref, ghead_ref, qf_ref, kf_ref, vf_ref, stat_ref, toks_ref, up_ref, down_ref, ghidden_ref, small_ref, gout_ref, part_ref, got_ref,
+    gtok_ref, gq_ref, out_ref, sums_ref, act_ref, gpre_ref, all_ref,
+    ghead, qf, kf, vf, stat, toks, up, down, ghidden, dof, qt, dot, dq_acc, dk_acc, dv_acc, qk, dv_rows, sorted_dv, head_acc, send, landing,
+    weight, mixed_all, act_buf, gpre_buf, zsend, zone, total, totals, out_zone, out_sum, out_part, out_own, out_all,
+    load_sem, own_sem, a_send, a_recv, z_send, z_recv, c_send, c_recv, o_send, o_recv, g_send, g_recv, r_send, r_recv,
+    w_send, w_recv, v_send, v_recv,
 ):
     me, z = lax.axis_index("ctx"), lax.axis_index("fsdp")
-    count, half = grads_ref.shape[0], grads_ref.shape[1]
-    width = toks_ref.shape[2]
+    count, block_len = ghead_ref.shape[0], ghead_ref.shape[1]
+    blocks, owners = 2 * count, gout_ref.shape[0]
+    rows, width = blocks * block_len, toks_ref.shape[1]
     own_experts, ffn = up_ref.shape[0], up_ref.shape[2]
+    low = jnp.bfloat16
+
+    def start(copies):
+        for copy in copies:
+            copy.start()
+        return copies
+
+    def wait(copies):
+        for copy in copies:
+            copy.wait()
+
     pairs = [
-        (grads_ref, held_grads), (toks_ref, held_toks), (small_in_ref, held_small), (gathered_ref, held_mixed), (up_ref, held_up),
-        (down_ref, held_down), (ghidden_ref, held_hidden),
+        (ghead_ref, ghead), (qf_ref, qf), (stat_ref, stat), (kf_ref, kf), (vf_ref, vf), (toks_ref, toks), (up_ref, up), (down_ref, down),
+        (ghidden_ref, ghidden),
     ]
-    pairs += [(weight_ref.at[c], held_weight.at[:, c]) for c in range(weight_ref.shape[0])]
-    loads = [pltpu.make_async_copy(src, dst, load_sem.at[i]) for i, (src, dst) in enumerate(pairs)]
-    for copy in loads:
-        copy.start()
+    loads = start([pltpu.make_async_copy(src, dst, load_sem.at[i]) for i, (src, dst) in enumerate(pairs)])
+    sib, same_core = flip(me, 1), [flip(me, 2), flip(me, 4), flip(flip(me, 2), 4)]
     z_peers = [(me, lax.rem(z + k, owners)) for k in range(1, owners)]
     c_peers = [(jnp.bitwise_xor(me, k), z) for k in range(1, count)]
     meet(z_peers + c_peers)
-    swaps = []
-    for k, device in enumerate(c_peers):
-        swaps.append(push(grads_ref.at[device[0]], landing.at[me], a_send.at[k], a_recv.at[k], device))
-        swaps[-1].start()
-    own_swap = pltpu.make_async_copy(grads_ref.at[me], landing.at[me], store_sem.at[0])
-    own_swap.start()
-    out_copies = []
-    for k, device in enumerate(z_peers):
-        out_copies.append(push(out_ref.at[device[1]], out_zone.at[z], o_send.at[0, k], o_recv.at[0, k], device))
-        out_copies[-1].start()
-    own_out = pltpu.make_async_copy(out_ref.at[z], out_zone.at[z], store_sem.at[1])
-    own_out.start()
-
-    loads[0].wait()
-    loads[1].wait()
-    total = None
-    for device in range(count):
-        for p in range(2):
-            part = dot_tn(head_columns(held_grads, p, device), held_toks[device, p * half:(p + 1) * half, :])
-            total = part if total is None else total + part
-    loads[2].wait()
+
+    out_copies = start([push(gout_ref.at[d[1]], out_zone.at[z], o_send.at[0, k], o_recv.at[0, k], d) for k, d in enumerate(z_peers)])
+    out_zone[z] = gout_ref[z]
+    gathers = start([push(got_ref, all_ref.at[me], g_send.at[k], g_recv.at[k], (d, z)) for k, d in enumerate(same_core)])
+    relays = start([push(got_ref, all_ref.at[me], r_send.at[3], r_recv.at[3], (sib, z))])
+    own_got = start([pltpu.make_async_copy(got_ref, all_ref.at[me], own_sem.at[0])])
+    weights = start([push(part_ref, weight.at[:, me], w_send.at[k], w_recv.at[k], (d, z)) for k, d in enumerate(same_core)])
+    shares = start([push(part_ref, weight.at[:, me], v_send.at[3], v_recv.at[3], (sib, z))])
+    weight[:, me] = part_ref[...]
+
+    def mask(condition):
+        return jnp.broadcast_to(jnp.where(condition, 1.0, 0.0), (1, 2 * HEAD))
+
+    firsts = [mask(table_ref[2 * c] < table_ref[2 * c + 1]).astype(low) for c in range(count)]
+    lows = [jnp.minimum(table_ref[2 * c], table_ref[2 * c + 1]) for c in range(count)]
+    holds = [[mask(lows[c] == j).astype(low) for j in range(count)] for c in range(count)]
+
+    def blend(masks, values):
+        out = None
+        for weigh, value in zip(masks, values):
+            out = weigh * value if out is None else out + weigh * value
+        return out
+
+    lane = lax.broadcasted_iota(jnp.int32, (1, 2 * HEAD), 1)
+
+    def prepare(s, both):
+        at = slice(s * block_len, (s + 1) * block_len)
+        grad = jnp.where(lane < HEAD, both, 0.0)
+        delta = jnp.sum(grad * stat[at, :], axis=1, keepdims=True)
+        one, two, three = split3(jnp.broadcast_to(-delta, grad.shape))
+        wide = jnp.where(lane == HEAD, one, grad.astype(low))
+        wide = jnp.where(lane == HEAD + 1, two, wide)
+        dof[at, :] = jnp.where(lane == HEAD + 2, three, wide)
+        turned = jnp.where(lane < HEAD, both, pltpu.roll(qf[at, :].astype(jnp.float32), HEAD, 1)).T.astype(low)
+        dot[:, at] = turned[:HEAD]
+        qt[:, at] = turned[HEAD:]
+
+    wait(loads[:3])
+    for c in range(count):
+        block = ghead[c]
+        turned = pltpu.roll(block.astype(jnp.float32), HEAD, 1).astype(low)
+        ghead[c] = firsts[c] * block + (1 - firsts[c]) * turned
+    for j in range(count):
+        both = blend([holds[c][j] for c in range(count)], [ghead[c] for c in range(count)]).astype(jnp.float32)
+        prepare(j, both)
+        prepare(blocks - 1 - j, pltpu.roll(both, HEAD, 1))
+    wait(loads[3:5])
+    causal = lax.broadcasted_iota(jnp.int32, (HALF, HALF), 1) <= lax.broadcasted_iota(jnp.int32, (HALF, HALF), 0)
+    scale = HEAD ** (-0.5)
+
+    def key_run(run):
+        def tile(q_at, k_at, k_low, k_size, diagonal, first_k, first_q):
+            scores = dot_nt(qf[q_at, :], kf[k_at, :]) * (scale * LOG2E)
+            if diagonal:
+                scores = jnp.where(causal, scores, HIDE)
+            probs = jnp.exp2(scores)
+            grad = (probs * dot_nt(dof[q_at, :], vf[k_at, :])).astype(low)
+            dv = dot_nn(dot[:, q_at], probs.astype(low))
+            dk = dot_nn(qt[:, q_at], grad)
+            dq = dot_nn(grad, kf[k_at, :])
+            at = slice(k_low, k_low + k_size)
+            if first_k:
+                dv_acc[:, at] = dv
+                dk_acc[:, at] = dk
+            else:
+                dv_acc[:, at] += dv
+                dk_acc[:, at] += dk
+            if first_q:
+                @pl.when(run == 0)
+                def _():
+                    dq_acc[q_at, :] = dq
+
+                @pl.when(run != 0)
+                def _():
+                    dq_acc[q_at, :] += dq
+            else:
+                dq_acc[q_at, :] += dq
+
+        early, late = span(2 * run, HALF), span(2 * run + 1, HALF)
+        tile(early, early, 0, HALF, True, True, True)
+        tile(late, early, 0, HALF, False, False, True)
+        tile(late, late, HALF, HALF, True, True, False)
+
+        @pl.loop(run + 1, rows // RUN)
+        def _(index):
+            tile(span(index, RUN), span(run, RUN), 0, RUN, False, False, True)
+
+        at = span(run, RUN)
+        both = jnp.concatenate([dk_acc[...] * scale, dv_acc[...]], axis=0).T
+        query = dq_acc[at, :] * scale
+        qk[at, :] = jnp.where(lane < HEAD, query, pltpu.roll(both, HEAD, 1)).astype(low)
+        dv_rows[at, :] = both.astype(low)
+
+    def send_half(half):
+        copies = []
+        mid = block_len // 2
+        for c in range(count):
+            ats = [slice(s * block_len, (s + 1) * block_len) for s in (range(count) if half == 0 else range(blocks - 1, count - 1, -1))]
+            send[half, c, :block_len, :] = blend(holds[c], [qk[at, :] for at in ats])
+            values = blend(holds[c], [dv_rows[at, :] for at in ats])
+            sorted_dv[c] = values
+            values = values[:, HEAD:]
+            send[half, c, block_len:, :] = jnp.concatenate([values[:mid], values[mid:]], axis=1)
+        landing[half, me] = send[half, me]
+        for k, d in enumerate(c_peers):
+            copies.append(push(send.at[half, d[0]], landing.at[half, me], a_send.at[half, k], a_recv.at[half, k], d))
+        return start(copies)
+
+    def head_weights(half):
+        first, second = None, None
+        for c in range(count):
+            order = firsts[c][:, :1] if half == 0 else 1 - firsts[c][:, :1]
+            here = order * toks[2 * c * block_len:(2 * c + 1) * block_len, :]
+            here = here + (1 - order) * toks[(2 * c + 1) * block_len:(2 * c + 2) * block_len, :]
+            one, two = dot_tn(send[half, c, :block_len, :], here), dot_tn(sorted_dv[c], here)
+            first, second = (one, two) if first is None else (first + one, second + two)
+        both = jnp.concatenate([first, second[HEAD:]], axis=0)
+        if half == 0:
+            head_acc[...] = both
+        else:
+            head_acc[...] += both
+
+    @pl.loop(0, 2)
+    def _(run):
+        key_run(run)
+
+    swaps = send_half(0)
+
+    for k, d in enumerate(same_core):
+        gathers[k].wait_recv()
+        relays += start([push(all_ref.at[d], all_ref.at[d], r_send.at[k], r_recv.at[k], (sib, z))])
+        weights[k].wait_recv()
+        shares += start([push(weight.at[:, d], weight.at[:, d], v_send.at[k], v_recv.at[k], (sib, z))])
+    wait(out_copies)
+    summed = out_zone[0].astype(jnp.float32)
+    for k in range(1, owners):
+        summed = summed + out_zone[k].astype(jnp.float32)
+    out_sum[...] = summed.astype(low).reshape(out_sum.shape)
+    part_copies = start([push(out_sum.at[d[0]], out_part.at[me], o_send.at[1, k], o_recv.at[1, k], d) for k, d in enumerate(c_peers)])
+    out_part[me] = out_sum[me]
+    wait(loads[5:])
+    head_weights(0)
+
+    @pl.loop(2, rows // RUN)
+    def _(run):
+        key_run(run)
+
+    swaps += send_half(1)
+    wait(part_copies)
+    summed = out_part[0].astype(jnp.float32)
+    for k in range(1, count):
+        summed = summed + out_part[k].astype(jnp.float32)
+    out_own[...] = summed.astype(low)
+    last_copies = start([push(out_own, out_all.at[me], o_send.at[2, k], o_recv.at[2, k], d) for k, d in enumerate(c_peers)])
+    out_all[me] = out_own[...]
+    wait(own_got + relays)
+    mixed_load = start([pltpu.make_async_copy(all_ref, mixed_all, own_sem.at[1])])
+    head_weights(1)
     lanes = width // owners
     for c in range(owners):
         at = slice(c * lanes, (c + 1) * lanes)
-        zsend[c, :3 * HEAD, :] = total[:, at].astype(jnp.bfloat16)
-        zsend[c, 3 * HEAD:, :] = held_small[:, at].astype(jnp.bfloat16)
-    z_copies = []
-    for k, device in enumerate(z_peers):
-        z_copies.append(push(zsend.at[device[1]], zone.at[z], z_send.at[k], z_recv.at[k], device))
-        z_copies[-1].start()
+        zsend[c, :3 * HEAD, :] = head_acc[:, at].astype(low)
+        zsend[c, 3 * HEAD:, :] = small_ref[:, at].astype(low)
+    z_copies = start([push(zsend.at[d[1]], zone.at[z], z_send.at[k], z_recv.at[k], d) for k, d in enumerate(z_peers)])
     zone[z] = zsend[z]
-    for i in (3, 4, 5):
-        loads[i].wait()
-
+    wait(mixed_load)
     step = 512
-
-    def expert_part(own_expert):
-        mixed = held_mixed[:, 0, own_expert].reshape(-1, width)
-        grad_out = held_mixed[:, 1, own_expert].reshape(-1, width)
+    groups = got_ref.shape[2] // own_experts
+
+    def expert_part(e):
+        mixed = mixed_all[:, :, 0, e * groups:(e + 1) * groups, :].reshape(-1, width)
+        grad_out = mixed_all[:, :, 1, e * groups:(e + 1) * groups, :].reshape(-1, width)
 
         def chunk(i, carry):
-            at = pl.ds(pl.multiple_of(i * step, step), step)
-            pre = dot_nn(mixed, held_up[own_expert, :, at])
-            active, slope = gelu_parts(pre)
-            act_buf[own_expert, :, at] = active.astype(jnp.bfloat16)
-            gpre_buf[own_expert, :, at] = (dot_nt(grad_out, held_down[own_expert, at, :]) * slope).astype(jnp.bfloat16)
+            at = span(i, step)
+            active, slope = gelu_parts(dot_nn(mixed, up[e, :, at]))
+            act_buf[e, :, at] = active.astype(low)
+            gpre_buf[e, :, at] = (dot_nt(grad_out, down[e, at, :]) * slope).astype(low)
             return carry
 
         lax.fori_loop(0, ffn // step, chunk, 0)
-        stores = [
-            pltpu.make_async_copy(act_buf.at[own_expert], act_ref.at[own_expert], store_sem.at[2 + 2 * own_expert]),
-            pltpu.make_async_copy(gpre_buf.at[own_expert], gpre_ref.at[own_expert], store_sem.at[3 + 2 * own_expert]),
-        ]
-        for copy in stores:
-            copy.start()
-        return stores
+        return start([
+            pltpu.make_async_copy(act_buf.at[e], act_ref.at[e], own_sem.at[2 + 2 * e]),
+            pltpu.make_async_copy(gpre_buf.at[e], gpre_ref.at[e], own_sem.at[3 + 2 * e]),
+        ])
 
     stores = expert_part(0)
-    for copy in z_copies:
-        copy.wait()
-    total = zone[0].astype(jnp.float32)
+    wait(z_copies)
+    summed = zone[0].astype(jnp.float32)
     for k in range(1, owners):
-        total = total + zone[k].astype(jnp.float32)
-    total_ref[...] = total.astype(jnp.bfloat16)
-    c_copies = []
-    for k, device in enumerate(c_peers):
-        c_copies.append(push(total_ref, all_ref.at[me], c_send.at[k], c_recv.at[k], device))
-        c_copies[-1].start()
-    all_ref[me] = total_ref[...]
-    own_out.wait()
-    for copy in out_copies:
-        copy.wait()
-    total = out_zone[0].astype(jnp.float32)
-    for k in range(1, owners):
-        total = total + out_zone[k].astype(jnp.float32)
-    per = lanes // count
-    out_sum[...] = total.astype(jnp.bfloat16).reshape(out_sum.shape)
-    part_copies = []
-    for k, device in enumerate(c_peers):
-        part_copies.append(push(out_sum.at[device[0]], out_part.at[me], o_send.at[1, k], o_recv.at[1, k], device))
-        part_copies[-1].start()
-    out_part[me] = out_sum[me]
-    for own_expert in range(1, own_experts):
-        stores += expert_part(own_expert)
-    for copy in part_copies:
-        copy.wait()
-    total = out_part[0].astype(jnp.float32)
-    for k in range(1, count):
-        total = total + out_part[k].astype(jnp.float32)
-    out_own[...] = total.astype(jnp.bfloat16)
-    last_copies = []
-    for k, device in enumerate(c_peers):
-        last_copies.append(push(out_own, out_all.at[me], o_send.at[2, k], o_recv.at[2, k], device))
-        last_copies[-1].start()
-    out_all[me] = out_own[...]
-    for copy in loads[6:]:
-        copy.wait()
-    own_swap.wait()
-    for copy in swaps:
-        copy.wait()
-    weight = held_weight[...].reshape(width, -1)
-    for p in range(2):
-        columns = [landing[h, :, HEAD * (2 * kind + p):HEAD * (2 * kind + p + 1)] for kind in range(3) for h in range(count)]
-        at = slice(p * half, (p + 1) * half)
-        gtok_ref[at, :] = held_hidden[at, :] + dot_nt(jnp.concatenate(columns, axis=1), weight)
-    for copy in c_copies:
-        copy.wait()
+        summed = summed + zone[k].astype(jnp.float32)
+    total[...] = summed.astype(low)
+    c_copies = start([push(total, totals.at[me], c_send.at[k], c_recv.at[k], d) for k, d in enumerate(c_peers)])
+    totals[me] = total[...]
+    for e in range(1, own_experts):
+        stores += expert_part(e)
+    wait(swaps + shares)
+    flat = weight[...].reshape(width, -1)
+    parts = []
+    for half in range(2):
+        queries, keys, values = [], [], []
+        for h in range(count):
+            front, back = landing[half, h, :block_len, :], landing[half, h, block_len:, :]
+            queries.append(front[:, :HEAD])
+            keys.append(front[:, HEAD:])
+            values.append(jnp.concatenate([back[:, :HEAD], back[:, HEAD:]], axis=0))
+        parts.append(dot_nt(jnp.concatenate(queries + keys + values, axis=1), flat))
+    in_order = mask(table_ref[2 * me] < table_ref[2 * me + 1])[:, :1]
+    gtok_ref[:block_len, :] = ghidden[:block_len, :] + (in_order * parts[0] + (1.0 - in_order) * parts[1])
+    gtok_ref[block_len:, :] = ghidden[block_len:, :] + (in_order * parts[1] + (1.0 - in_order) * parts[0])
+    wait(last_copies)
+    out_ref[...] = out_all[...].astype(jnp.float32).reshape(out_ref.shape)
+    wait(c_copies)
     small = None
     turned = []
     for c in range(count):
-        turned.append(all_ref[c, :3 * HEAD, :].astype(jnp.float32).T)
-        part = all_ref[c, 3 * HEAD:, :].astype(jnp.float32)
+        turned.append(totals[c, :3 * HEAD, :].astype(jnp.float32).T)
+        part = totals[c, 3 * HEAD:, :].astype(jnp.float32)
         small = part if small is None else small + part
-    small_ref[...] = small
+    sums_ref[...] = small
     for kind in range(3):
         at = slice(HEAD * kind, HEAD * (kind + 1))
         gq_ref[:, HEAD * count * kind:HEAD * count * (kind + 1)] = jnp.concatenate([part[:, at] for part in turned], axis=1)
-    for copy in last_copies:
-        copy.wait()
-    gout_ref[...] = out_all[...].astype(jnp.float32).reshape(gout_ref.shape)
-    for copy in stores:
-        copy.wait()
-
-
-def closing(grads, tokens_all, small, gout, weight, ghidden, gathered, w_up, w_down, groups, owners):
-    count, width = tokens_all.shape[0], tokens_all.shape[2]
-    lanes = width // owners
+    wait(stores)
+    for copy in gathers + weights:
+        copy.wait_send()
+
+
+def backward(table, grad_heads, saved, tokens_all, small, gout, parts, ghidden, got, w_up, w_down, groups):
+    count, block_len = grad_heads.shape[:2]
+    qf, kf, vf, stat = saved
+    rows, width = qf.shape[0], tokens_all.shape[2]
+    owners, lanes = gout.shape[:2]
+    own_experts, _, ffn = w_up.shape
     height = 3 * HEAD + small.shape[0]
-    own_experts, _, ffn = w_up.shape
-    sources = gathered.shape[0]
-    view = gathered.reshape(sources, 2, own_experts, groups, width)
-    wide = (own_experts, sources * groups, ffn)
+    wide = (own_experts, count * owners * groups, ffn)
+    part = (count, lanes // count, width)
+    swap = (2, count, block_len + block_len // 2, 2 * HEAD)
+    toks = tokens_all.reshape(rows, width)
+    held = [grad_heads, qf, kf, vf, stat, toks, w_up, w_down, ghidden]
     dma = pltpu.SemaphoreType.DMA
-    held = [grads, tokens_all, small, weight, ghidden, view, w_up, w_down]
-    part = (count, lanes // count, width)
+    low, full = jnp.bfloat16, jnp.float32
+    scratch = [
+        ((rows, 2 * HEAD), low), ((HEAD, rows), low), ((HEAD, rows), low), ((rows, 2 * HEAD), full), ((HEAD, RUN), full), ((HEAD, RUN), full),
+        ((rows, 2 * HEAD), low), ((rows, 2 * HEAD), low), ((count, block_len, 2 * HEAD), low), ((3 * HEAD, width), full), (swap, low), (swap, low),
+        ((owners, count) + parts.shape[1:], low), ((count,) + got.shape, low), (wide, low), (wide, low),
+        ((owners, height, lanes), low), ((owners, height, lanes), low), ((height, lanes), low), ((count, height, lanes), low),
+        (gout.shape, low), (part, low), (part, low), (part[1:], low), (part, low),
+    ]
+    sems = [
+        (9,), (2 + 2 * own_experts,), (2, count - 1), (2, count - 1), (owners - 1,), (owners - 1,), (count - 1,), (count - 1,),
+        (3, count - 1), (3, count - 1), (3,), (3,), (4,), (4,), (3,), (3,), (4,), (4,),
+    ]
     return pl.pallas_call(
-        functools.partial(closing_body, owners),
+        backward_body,
         out_shape=(
-            jax.ShapeDtypeStruct(ghidden.shape, jnp.float32),
-            jax.ShapeDtypeStruct((lanes, 3 * width), jnp.float32),
-            jax.ShapeDtypeStruct((lanes, width), jnp.float32),
-            jax.ShapeDtypeStruct((small.shape[0], lanes), jnp.float32),
-            jax.ShapeDtypeStruct(wide, jnp.bfloat16),
-            jax.ShapeDtypeStruct(wide, jnp.bfloat16),
+            jax.ShapeDtypeStruct(ghidden.shape, full),
+            jax.ShapeDtypeStruct((lanes, 3 * width), full),
+            jax.ShapeDtypeStruct((lanes, width), full),
+            jax.ShapeDtypeStruct((small.shape[0], lanes), full),
+            jax.ShapeDtypeStruct(wide, low),
+            jax.ShapeDtypeStruct(wide, low),
+            jax.ShapeDtypeStruct((count,) + got.shape, low),
         ),
-        in_specs=[ANY] * 9,
-        out_specs=(VMEM,) * 4 + (ANY,) * 2,
-        scratch_shapes=[pltpu.VMEM(x.shape, x.dtype) for x in held[:3]]
-        + [pltpu.VMEM((owners, count) + weight.shape[2:], jnp.bfloat16)]
-        + [pltpu.VMEM(x.shape, x.dtype) for x in held[4:]] + [
-            pltpu.VMEM(wide, jnp.bfloat16), pltpu.VMEM(wide, jnp.bfloat16), pltpu.VMEM(grads.shape, jnp.bfloat16),
-            pltpu.VMEM((owners, height, lanes), jnp.bfloat16), pltpu.VMEM((owners, height, lanes), jnp.bfloat16),
-            pltpu.VMEM((height, lanes), jnp.bfloat16), pltpu.VMEM((count, height, lanes), jnp.bfloat16),
-            pltpu.VMEM(gout.shape, jnp.bfloat16), pltpu.VMEM(part, jnp.bfloat16), pltpu.VMEM(part, jnp.bfloat16),
-            pltpu.VMEM(part[1:], jnp.bfloat16), pltpu.VMEM(part, jnp.bfloat16),
-            dma((7 + count,)), dma((2 + 2 * own_experts,)), dma((count - 1,)), dma((count - 1,)), dma((owners - 1,)), dma((owners - 1,)),
-            dma((count - 1,)), dma((count - 1,)), dma((3, count - 1)), dma((3, count - 1)),
-        ],
+        in_specs=[SMEM] + [ANY] * 9 + [VMEM] * 4,
+        out_specs=(VMEM,) * 4 + (ANY,) * 3,
+        scratch_shapes=[pltpu.VMEM(x.shape, x.dtype) for x in held]
+        + [pltpu.VMEM(shape, dtype) for shape, dtype in scratch]
+        + [dma(shape) for shape in sems],
         compiler_params=pltpu.CompilerParams(collective_id=6, has_side_effects=True, vmem_limit_bytes=LIMIT),
-        cost_estimate=cost(28),
-        name="closing",
-    )(*held[:3], gout, *held[3:])
+        cost_estimate=cost(60),
+        name="backward",
+    )(table, grad_heads, qf, kf, vf, stat, toks, w_up, w_down, ghidden, small, gout, parts, got)
 
 
 def expert_grad_body(experts, passed, mixed_ref, grad_ref, act_ref, gpre_ref, small_ref, *refs):
@@ -1054,7 +1054,7 @@
     width = gup_ref.shape[1]
     for source, out in zip(sources, outs):
         out[...] = source[...]
-    router_ref[...] = small_ref[:experts].T
+    router_ref[...] = small_ref[:experts]
     gain_ref[...] = small_ref[experts:experts + 1]
     bias_ref[...] = small_ref[experts + 1:experts + 2]
     gup_ref[0] = dot_tn(mixed_ref[...].reshape(-1, width), gpre_ref[0])
@@ -1075,7 +1075,7 @@
         grid=(own, steps),
         out_shape=[
             jax.ShapeDtypeStruct((own, width, ffn), full), jax.ShapeDtypeStruct((own, ffn, width), full),
-            jax.ShapeDtypeStruct((lanes, experts), full), jax.ShapeDtypeStruct((1, lanes), full), jax.ShapeDtypeStruct((1, lanes), full),
+            jax.ShapeDtypeStruct((experts, lanes), full), jax.ShapeDtypeStruct((1, lanes), full), jax.ShapeDtypeStruct((1, lanes), full),
         ] + [jax.ShapeDtypeStruct(x.shape, x.dtype) for x in passed],
         in_specs=[
             pl.BlockSpec((sources, 1, 1, groups, width), lambda e, f: (0, 0, e, 0, 0)),
@@ -1086,7 +1086,7 @@
         ] + slices,
         out_specs=[
             pl.BlockSpec((1, width, step), lambda e, f: (e, 0, f)), pl.BlockSpec((1, step, width), lambda e, f: (e, f, 0)),
-            pl.BlockSpec((lanes, experts), lambda e, f: (0, 0)), pl.BlockSpec((1, lanes), lambda e, f: (0, 0)),
+            pl.BlockSpec((experts, lanes), lambda e, f: (0, 0)), pl.BlockSpec((1, lanes), lambda e, f: (0, 0)),
             pl.BlockSpec((1, lanes), lambda e, f: (0, 0)),
         ] + slices,
         compiler_params=pltpu.CompilerParams(vmem_limit_bytes=LIMIT),
@@ -1103,19 +1103,17 @@
     rows, width = tok_rows.shape
     experts = w_router.shape[1]
     groups = rows // GROUP_SIZE
-    segs = seg_ids[0].reshape(block_table.shape[0], -1)
     tokens_all, head_weights, out_full, pack_full, qkv_parts = gather(
         tok_rows, w_qkv, w_out, w_router, ln_gain, ln_bias, ctx_count, z_count
     )
-    att, *saved = attn_fwd(tokens_all.reshape(ctx_count * rows, width), head_weights, block_table, segs)
-    layer_out, grad_hidden, gout, small, gathered, grad_heads, qkv_full = middle(
-        att, tok_rows, cot_rows, out_full, pack_full, group_ids, w_up, w_down, qkv_parts, experts, groups
+    att, *saved = attn_fwd(tokens_all.reshape(ctx_count * rows, width), head_weights, block_table, seg_ids)
+    layer_out, grad_hidden, gout, small, got, grad_heads = middle(
+        att, tok_rows, cot_rows, out_full, pack_full, group_ids, w_up, w_down, experts, groups
+    )
+    grad_tokens, grad_qkv, grad_out, small, active, grad_pre, gathered = backward(
+        block_table, grad_heads, saved, tokens_all, small, gout, qkv_parts, grad_hidden, got, w_up, w_down, groups
     )
     gathered = gathered.reshape((ctx_count * z_count,) + gathered.shape[2:])
-    grads = attn_bwd(grad_heads, saved, block_table, segs)
-    grad_tokens, grad_qkv, grad_out, small, active, grad_pre = closing(
-        grads, tokens_all, small, gout, qkv_full, grad_hidden, gathered, w_up, w_down, groups, z_count
-    )
     grad_up, grad_down, grad_router, grad_gain, grad_bias, layer_out, grad_tokens, grad_qkv, grad_out = expert_grads(
         gathered, active, grad_pre, small, [layer_out, grad_tokens, grad_qkv, grad_out], groups, experts
     )
@@ -1124,7 +1122,7 @@
         grad_tokens[None],
         grad_qkv,
         grad_out,
-        grad_router,
+        grad_router.T,
         grad_gain[0],
         grad_bias[0],
         grad_up,

time: 189 us -> 167 us (0.88)
  Pallas kernels: 182 us -> 167 us
  local copies, waits for them, and re-layouts: 4.02 us -> 0 us
    pallas_call x2 -> x1, Pallas kernels: 70.9 us -> 57.8 us  [backward(): pl.pallas_call(backward_body, out_shape=(jax.ShapeDtypeStruct(ghidden.sha...]
    unnamed x3 -> x0, local copies, waits for them, and re-layouts: 3.41 us -> none
    pallas_call x1, Pallas kernels: 41.5 us -> 38.6 us  [middle(): pl.pallas_call(functools.partial(middle_body, experts, groups), out_shape...]
where the time goes in v5:
time: 167 us; the launch traced here: 168 us
  Pallas kernels  167 us (100%)
    pallas_call x1, Pallas kernels, backward(): pl.pallas_call(backward_body, out_shape=(jax.ShapeDtypeStruct(ghidden.sha...  57.8 us
    pallas_call x1, Pallas kernels, middle(): pl.pallas_call(functools.partial(middle_body, experts, groups), out_shape...  38.6 us
    pallas_call x1, Pallas kernels, gather(): pl.pallas_call(functools.partial(gather_body, z_count), out_shape=[jax.Sh...  28.9 us
    pallas_call x1, Pallas kernels, attn_fwd(): pl.pallas_call(functools.partial(fwd_body, blocks, block_len), out_shape=...  25.9 us
    pallas_call x1, Pallas kernels, expert_grads(): pl.pallas_call(functools.partial(expert_grad_body, experts, len(passed)),...  15.4 us

profile of v5, /device:TPU:0, one launch (start us, length us, event | category | flops | bytes accessed | tf_op | source)
XLA Modules:
  0.0 167.5 jit_solution(12454255022684790986)
XLA Ops:
  0.6 28.9 %gather_tokens.1 = (bf16[8,512,512]{2,1,0:T(8,128)(2,1)}, bf16[4,128,192]{2,1,0:T(8,128)(2,1)}, bf16[4,128,512]{2,1,0:T(8,128)(2,1)}, bf16[4,16,128]{2,1,0:T(8,128)(2,1)}, bf16[4,16,1536]{2,1,0:T(8,128)(2,1)}) custom-call(bf16[512,512]{1,0:T(8,128)(2,1)} %bitcast.12, bf16[128,1536]{1,0:T(8,128)(2,1)} %wq_ref.1, bf16[128,512]{1,0:T(8,128)(2,1)} %wo_ref.1, ...), custom_call_target="tpu_custom_call" | custom-call | flops 27599998976 | bytes 1048576 | tf_op jit(solution)/shard_map/gather_tokens/pallas_call | solution.py:561
  29.6 25.9 %attention.1 = (bf16[8,256,128]{2,1,0:T(8,128)(2,1)}, bf16[4096,128]{1,0:T(8,128)(2,1)}, bf16[4096,128]{1,0:T(8,128)(2,1)}, bf16[4096,128]{1,0:T(8,128)(2,1)}, f32[4096,128]{1,0:T(8,128)}) custom-call(s32[16]{0:T(128)} %table_ref.3, bf16[4096,512]{1,0:T(8,128)(2,1)} %bitcast.18, bf16[4,128,192]{2,1,0:T(8,128)(2,1)} %get-tuple-element.42.w_ref, s32[1,4096]{1,0:T(1,128)} %seg_ref.1), custom_call_target="tpu_custom_call" | custom-call | flops 34500001792 | bytes 1048576 | tf_op jit(solution)/shard_map/attention/pallas_call | solution.py:429
  55.5 38.6 %middle.1 = (f32[512,512]{1,0:T(8,128)}, f32[512,512]{1,0:T(8,128)}, bf16[4,128,512]{2,1,0:T(8,128)(2,1)}, f32[16,512]{1,0:T(8,128)}, bf16[4,2,32,512]{3,2,1,0:T(8,128)(2,1)}, /*index=5*/bf16[8,256,128]{2,1,0:T(8,128)(2,1)}) custom-call(bf16[8,256,128]{2,1,0:T(8,128)(2,1)} %get-tuple-element.43.att_ref, bf16[512,512]{1,0:T(8,128)(2,1)} %bitcast.13, ...), custom_call_target="tpu_custom_call" | custom-call | flops 40249999360 | bytes 1048576 | tf_op jit(solution)/shard_map/middle/pallas_call | solution.py:720
  94.1 57.8 %backward.1 = (f32[512,512]{1,0:T(8,128)}, f32[128,1536]{1,0:T(8,128)}, f32[128,512]{1,0:T(8,128)}, f32[16,128]{1,0:T(8,128)}, bf16[2,512,2048]{2,1,0:T(8,128)(2...) custom-call(s32[16]{0:T(128)} %table_ref.3, bf16[8,256,128]{2,1,0:T(8,128)(2,1)} %get-tuple-element.46.ghead_ref, ...), custom_call_target="tpu_custom_call" | custom-call | flops 69000003584 | bytes 1048576 | tf_op jit(solution)/shard_map/backward/pallas_call | solution.py:1029
  151.9 15.4 %expert_grads.1 = (f32[2,512,2048]{2,1,0:T(8,128)}, f32[2,2048,512]{2,1,0:T(8,128)}, f32[8,128]{1,0:T(8,128)}, f32[1,128]{1,0:T(1,128)}, f32[1,128]{1,0:T(1,128)...) custom-call(bf16[32,2,2,16,512]{4,3,2,1,0:T(8,128)(2,1)} %bitcast.20, ...), custom_call_target="tpu_custom_call" | custom-call | flops 11500000256 | bytes 1048576 | tf_op jit(solution)/shard_map/expert_grads/pallas_call | solution.py:1073
